TPU v7x, 512 devices: a whole 4x4x16 slice. The times are simulated.
512 devices in a mesh: tok: 2 (over core), row: 16 (over x, y), col: 16 (over z).
Axes of the slice: x: 4, y: 4, z: 16, core: 2. Of those that a mesh axis runs over, the one named last changes fastest.
Arguments:
- tokens: bfloat16 [512, 16384], P(('tok', 'col'), 'row'), may hold values from -6 to 6
- w1_blocks: bfloat16 [16, 16, 18, 128, 128], P('row', 'col'), may hold values from -0.1875 to 0.1875
- w1_coords: int32 [16, 16, 18, 2], P('row', 'col'), may hold values from 0 to 31, as said below
- w1_count: int32 [16, 16], P('row', 'col'), may hold values from 2 to 18, as said below
- w2_blocks: bfloat16 [16, 16, 18, 128, 128], P('row', 'col'), may hold values from -0.09375 to 0.09375
- w2_coords: int32 [16, 16, 18, 2], P('row', 'col'), may hold values from 0 to 31, as said below
- w2_count: int32 [16, 16], P('row', 'col'), may hold values from 2 to 18, as said below
- cotangent: bfloat16 [512, 16384], P(('tok', 'col'), 'row'), may hold values from -6 to 6
Outputs:
- output: bfloat16 [512, 16384], P(('tok', 'col'), 'row')
- input_grad: bfloat16 [512, 16384], P(('tok', 'col'), 'row')
- w1_grad: bfloat16 [16, 16, 18, 128, 128], P('row', 'col')
- w2_grad: bfloat16 [16, 16, 18, 128, 128], P('row', 'col')
Inputs may be any that keep to these rules, and one draw needn't show every extreme that they name: `w1_coords`: within one tile all 18 slots name distinct blocks; the first entry lies below 8 and the second below 32. `w2_coords`: within one tile all 18 slots name distinct blocks; the first entry lies below 32 and the second below 8. `w1_count`: some tile lists 18 blocks. `w2_count`: some tile lists 18 blocks.
All inputs are finite; a program needn't handle non-finite values.
Results may differ from a plain program's by a relative error of at most 0.022.
Values may be sent and summed in bfloat16 or wider, within the bound.
No kernel may reach another device: no remote copies, remote signals or barrier semaphores. Data moves between devices by JAX's collectives and lax.ppermute only.
A program may use at most 64 MiB of HBM per device.

v0:
```python
import jax
import jax.numpy as jnp
from jax import lax
from jax.sharding import PartitionSpec as P

F = 65536
BS = 128


def apply_blocks(source, blocks, source_index, target_index, listed, targets, transpose):
    row_count = source.shape[0]
    pieces = source.reshape(row_count, -1, BS)
    chosen = jnp.take(pieces, source_index, axis=1)
    if transpose:
        products = jnp.einsum("mnc,nbc->mnb", chosen, blocks, preferred_element_type=jnp.float32)
    else:
        products = jnp.einsum("mnb,nbc->mnc", chosen, blocks, preferred_element_type=jnp.float32)
    valid_slots = (jnp.arange(blocks.shape[0], dtype=jnp.int32) < listed).astype(jnp.float32)
    products = products * valid_slots[None, :, None]
    placed = jnp.zeros((row_count, targets, products.shape[2]), jnp.float32)
    placed = placed.at[:, target_index].add(products)
    return placed.reshape(row_count, targets * BS)


def block_grads(left, right, left_index, right_index, listed):
    row_count = left.shape[0]
    first = jnp.take(left.reshape(row_count, -1, BS), left_index, axis=1)
    second = jnp.take(right.reshape(row_count, -1, BS), right_index, axis=1)
    grads = jnp.einsum("mnb,mnc->nbc", first, second, preferred_element_type=jnp.float32)
    valid_slots = (jnp.arange(left_index.shape[0], dtype=jnp.int32) < listed).astype(jnp.float32)
    return grads * valid_slots[:, None, None]


def reduce_rows(partial_value):
    return lax.psum_scatter(
        partial_value.astype(jnp.bfloat16), "row", scatter_dimension=0, tiled=True
    ).astype(jnp.float32)


def gather_rows(shares):
    return lax.all_gather(shares, "row", axis=0, tiled=True)


def on_device(tokens, w1_blocks, w1_coords, w1_count, w2_blocks, w2_coords, w2_count, cotangent):
    token_rows, cotan_rows = (
        lax.all_gather(tokens, "col", axis=0, tiled=True),
        lax.all_gather(cotangent, "col", axis=0, tiled=True),
    )
    feature_blocks = token_rows.shape[1] // BS
    hidden_blocks = F // lax.axis_size("col") // BS
    first_blocks = w1_blocks[0, 0]
    first_coords = w1_coords[0, 0]
    first_listed = w1_count[0, 0]
    second_blocks = w2_blocks[0, 0]
    second_coords = w2_coords[0, 0]
    second_listed = w2_count[0, 0]
    pre_part = apply_blocks(
        token_rows,
        first_blocks,
        first_coords[:, 0],
        first_coords[:, 1],
        first_listed,
        hidden_blocks,
        False,
    )
    preact = reduce_rows(pre_part)
    activation = jax.nn.silu(preact).astype(jnp.bfloat16)
    act_rows = gather_rows(activation)
    act_part = apply_blocks(
        cotan_rows,
        second_blocks,
        second_coords[:, 1],
        second_coords[:, 0],
        second_listed,
        hidden_blocks,
        True,
    )
    act_grad = reduce_rows(act_part)
    output_part = apply_blocks(
        act_rows,
        second_blocks,
        second_coords[:, 0],
        second_coords[:, 1],
        second_listed,
        feature_blocks,
        False,
    )
    sigmoid_pre = jax.nn.sigmoid(preact)
    pre_grad = (act_grad * sigmoid_pre * (1.0 + preact * (1.0 - sigmoid_pre))).astype(jnp.bfloat16)
    grad_rows = gather_rows(pre_grad)
    input_part = apply_blocks(
        grad_rows,
        first_blocks,
        first_coords[:, 1],
        first_coords[:, 0],
        first_listed,
        feature_blocks,
        True,
    )
    groups = lax.axis_size("col")
    moved_out, moved_in = (
        lax.all_to_all(
            output_part.astype(jnp.bfloat16), "col", split_axis=0, concat_axis=0, tiled=True
        ),
        lax.all_to_all(
            input_part.astype(jnp.bfloat16), "col", split_axis=0, concat_axis=0, tiled=True
        ),
    )
    output = moved_out.reshape(groups, -1, moved_out.shape[1]).astype(jnp.float32).sum(axis=0)
    input_grad = moved_in.reshape(groups, -1, moved_in.shape[1]).astype(jnp.float32).sum(axis=0)
    first_grad = block_grads(
        token_rows, grad_rows, first_coords[:, 0], first_coords[:, 1], first_listed
    )
    second_grad = block_grads(
        act_rows, cotan_rows, second_coords[:, 0], second_coords[:, 1], second_listed
    )
    first_total, second_total = (
        lax.psum(first_grad.astype(jnp.bfloat16), "tok").astype(jnp.float32),
        lax.psum(second_grad.astype(jnp.bfloat16), "tok").astype(jnp.float32),
    )
    return (
        output.astype(jnp.bfloat16),
        input_grad.astype(jnp.bfloat16),
        first_total.astype(jnp.bfloat16)[None, None],
        second_total.astype(jnp.bfloat16)[None, None],
    )


def solution(mesh):
    placed = (
        P(("tok", "col"), "row"),
        P("row", "col", None, None, None),
        P("row", "col", None, None),
        P("row", "col"),
        P("row", "col", None, None, None),
        P("row", "col", None, None),
        P("row", "col"),
        P(("tok", "col"), "row"),
    )
    return jax.shard_map(
        on_device,
        mesh=mesh,
        in_specs=placed,
        out_specs=(
            P(("tok", "col"), "row"),
            P(("tok", "col"), "row"),
            P("row", "col", None, None, None),
            P("row", "col", None, None, None),
        ),
        check_vma=False,
    )
```

profile of v0, /device:TPU:1, one launch (start us, length us, event | category | flops | bytes accessed | tf_op | source)
XLA Modules:
  0.0 466.5 jit_solution(9303839115386433764)
XLA Ops:
  7.2 0.0 reduce-scatter.7.cloned.1.call-start
  7.2 1.3 compare_and_fusion
  8.6 1.3 fusion.25
  9.8 32.0 %all_gather.12 = bf16[256,1024]{1,0:T(8,128)(2,1)S(1)} all-gather(bf16[16,1024]{1,0:T(8,128)(2,1)} %param.12), channel_id=1, replica_groups=mesh['tok'=2,'row'=16,'col'=16] {'col'}, dimensions={0}, use_global_device_ids=true | all-gather | bytes 557056 | tf_op jit(solution)/shard_map/all_gather | solution.py:46
  41.9 0.2 copy.48
  42.1 0.3 copy.49
  43.1 1.8 gather_fusion
  44.9 1.8 convolution_multiply_fusion.3
  46.7 2.4 broadcast.75.clone
  49.1 8.6 %scatter_fusion = f32[256,32,128]{2,0,1:T(8,128)} fusion(f32[256,32,128]{2,0,1:T(8,128)} %broadcast.75.clone, s32[18]{0:T(128)S(1)} %get-tuple-element.25, f32[18,256,128]{2,1,0:T(8,128)S(1)} %convolution_multiply_fusion.3), kind=kCustom, calls=%fused_computation.4 | custom fusion | flops 589824 | bytes 7077960 | tf_op jit(solution)/shard_map/scatter-add | solution.py:21
  57.7 2.5 convert_element_type.79
  60.2 3.0 copy.50
  63.2 4.1 copy.66
  67.3 0.0 reduce-scatter.9.cloned.1.call-start
  67.4 0.7 copy-done.8
  68.0 22.1 %all_gather.14 = bf16[256,1024]{1,0:T(8,128)(2,1)S(1)} all-gather(bf16[16,1024]{1,0:T(8,128)(2,1)S(1)} %copy-done.8), channel_id=1, replica_groups=mesh['tok'=2,'row'=16,'col'=16] {'col'}, dimensions={0}, use_global_device_ids=true | all-gather | bytes 557056 | tf_op jit(solution)/shard_map/all_gather | solution.py:47
  90.1 0.2 copy.55
  90.4 0.3 copy.56
  91.3 0.5 compare_and_fusion.1
  91.8 1.9 gather_fusion.2
  93.7 0.5 fusion.26
  94.3 1.8 convolution_multiply_fusion.1
  96.0 2.4 broadcast.75.clone.1
  98.5 8.6 %scatter_fusion.2 = f32[256,32,128]{2,0,1:T(8,128)} fusion(f32[256,32,128]{2,0,1:T(8,128)} %broadcast.75.clone.1, s32[18]{0:T(128)} %get-tuple-element.22, f32[18,256,128]{2,1,0:T(8,128)S(1)} %convolution_multiply_fusion.1), kind=kCustom, calls=%fused_computation.6 | custom fusion | flops 589824 | bytes 7077960 | tf_op jit(solution)/shard_map/scatter-add | solution.py:21
  107.1 2.6 convert_element_type.86
  109.6 2.9 copy.57
  112.6 4.2 copy.68
  116.8 0.0 all-gather.5.cloned.1.call-start
  116.8 42.0 %reduce-scatter.7.cloned.1.call-done = bf16[16,4096]{1,0:T(8,128)(2,1)} async-done(((bf16[256,4096]{1,0:T(8,128)(2,1)}), bf16[16,4096]{1,0:T(8,128)(2,1)}) %reduce-scatter.7.cloned.1.call-update) | async-done | bytes 131088 | tf_op jit(solution)/shard_map/reduce_scatter | solution.py:35
  158.8 93.8 %reduce-scatter.9.cloned.1.call-done = bf16[16,4096]{1,0:T(8,128)(2,1)} async-done(((bf16[256,4096]{1,0:T(8,128)(2,1)}), bf16[16,4096]{1,0:T(8,128)(2,1)}) %reduce-scatter.9.cloned.1.call-update) | async-done | bytes 131088 | tf_op jit(solution)/shard_map/reduce_scatter | solution.py:35
  252.7 1.8 fusion.22
  254.5 0.0 all-gather.3.cloned.1.call-start
  254.5 0.5 all-gather.3.cloned.1.call-update
  255.1 61.7 %all-gather.5.cloned.1.call-done = bf16[256,4096]{1,0:T(8,128)(2,1)} async-done(((bf16[16,4096]{1,0:T(8,128)(2,1)}), bf16[256,4096]{1,0:T(8,128)(2,1)}) %all-gather.5.cloned.1.call-update) | async-done | bytes 2097168 | tf_op jit(solution)/shard_map/all_gather | solution.py:41
  316.7 3.3 copy.59
  320.0 2.9 copy.60
  322.9 2.4 gather_fusion.3
  325.3 1.9 convolution_multiply_fusion
  327.3 0.1 broadcast.72.clone.1
  327.3 5.8 %scatter_fusion.3 = f32[256,8,128]{2,0,1:T(8,128)S(1)} fusion(f32[256,8,128]{2,0,1:T(8,128)S(1)} %broadcast.72.clone.1, s32[18]{0:T(128)S(1)} %copy-done.16, f32[18,256,128]{2,1,0:T(8,128)} %convolution_multiply_fusion), kind=kCustom, calls=%fused_computation.7 | custom fusion | flops 589824 | bytes 7077960 | tf_op jit(solution)/shard_map/scatter-add | solution.py:21
  333.1 0.1 convert_element_type.90
  333.2 0.3 copy.61
  333.6 1.0 convert_element_type.91
  334.6 12.1 %all-to-all-start.1 = ((bf16[16,16,1024]{2,1,0:T(8,128)(2,1)}), bf16[16,16,1024]{2,1,0:T(8,128)(2,1)}, u32[]{:S(2)}, u32[]{:S(2)}) async-start(bf16[16,16,1024]{2,1,0:T(8,128)(2,1)} %convert_element_type.91), calls=%async_computation.1 | async-start | bytes 1048576 | tf_op jit(solution)/shard_map/all_to_all | solution.py:105
  346.7 33.2 %all-gather.3.cloned.1.call-done = bf16[256,4096]{1,0:T(8,128)(2,1)} async-done(((bf16[16,4096]{1,0:T(8,128)(2,1)}), bf16[256,4096]{1,0:T(8,128)(2,1)}) %all-gather.3.cloned.1.call-update) | async-done | bytes 2097168 | tf_op jit(solution)/shard_map/all_gather | solution.py:41
  379.9 3.3 copy.52
  383.2 2.9 copy.53
  386.1 2.4 gather_fusion.1
  388.5 1.9 convolution_multiply_fusion.2
  390.4 0.1 broadcast.72.clone
  390.5 5.8 %scatter_fusion.1 = f32[256,8,128]{2,0,1:T(8,128)S(1)} fusion(f32[256,8,128]{2,0,1:T(8,128)S(1)} %broadcast.72.clone, s32[18]{0:T(128)S(1)} %copy-done.17, f32[18,256,128]{2,1,0:T(8,128)} %convolution_multiply_fusion.2), kind=kCustom, calls=%fused_computation.5 | custom fusion | flops 589824 | bytes 7077960 | tf_op jit(solution)/shard_map/scatter-add | solution.py:21
  396.3 0.1 convert_element_type.84
  396.4 0.3 copy.54
  396.8 1.0 convert_element_type.85
  397.8 12.0 %all-to-all-start = ((bf16[16,16,1024]{2,1,0:T(8,128)(2,1)}), bf16[16,16,1024]{2,1,0:T(8,128)(2,1)S(1)}, u32[]{:S(2)}, u32[]{:S(2)}) async-start(bf16[16,16,1024]{2,1,0:T(8,128)(2,1)} %convert_element_type.85), calls=%async_computation | async-start | bytes 1048576 | tf_op jit(solution)/shard_map/all_to_all | solution.py:102
  409.8 0.0 all-reduce.3.cloned.1.call-start
  409.9 2.9 fusion.2
  412.8 1.5 fusion.3
  414.3 1.7 reduce_sum.25
  416.0 16.4 %all-to-all-done = bf16[16,16,1024]{2,1,0:T(8,128)(2,1)S(1)} async-done(((bf16[16,16,1024]{2,1,0:T(8,128)(2,1)}), bf16[16,16,1024]{2,1,0:T(8,128)(2,1)S(1)}, u32[]{:S(2)}, u32[]{:S(2)}) %all-to-all-start) | async-done | bytes 524320 | tf_op jit(solution)/shard_map/all_to_all | solution.py:102
  432.4 0.7 reduce_sum.24
  433.1 24.1 %all-reduce.3.cloned.1.call-done = (bf16[1,1,18,128,128]{4,3,2,1,0:T(8,128)(2,1)}, bf16[1,1,18,128,128]{4,3,2,1,0:T(8,128)(2,1)}) async-done(((bf16[1,1,18,128,128]{4,3,2,1,0:T(8,128)(2,1)}, bf16[1,1,18,128,128]{4,3,2,1,0:T(8,128)(2,1)}), (bf16[1,1,18,128,128]{4,3,2,1,0:T(8,128)(2,1)}, bf16[1,1,18,128,128]{4,3,2,1,0:T(8,128)(2,1)})) %all-reduce.3.cloned.1.call-update) | async-done | bytes 1179664 | tf_op jit(solution)/shard_map/psum | solution.py:118
  457.2 2.0 copy.78
  459.2 0.8 copy.79
  (44 shorter events, 0.2 us)
Async XLA Ops:
  7.2 37.7 %copy-start = (bf16[1,1,18,128,128]{4,3,2,1,0:T(8,128)(2,1)S(1)}, bf16[1,1,18,128,128]{4,3,2,1,0:T(8,128)(2,1)}, u32[]{:S(2)}) copy-start(bf16[1,1,18,128,128]{4,3,2,1,0:T(8,128)(2,1)} %param.13) | copy-start | bytes 1769476
  7.2 151.7 %reduce-scatter.7.cloned.1.call-start = ((), (), s32[]{:S(2)}) async-start(), calls=%async_computation.6 | async-start | bytes 2228224 | tf_op jit(solution)/shard_map/reduce_scatter | solution.py:35
  8.6 36.3 %copy-start.12 = (pred[18]{0:T(512)(128)(4,1)}, pred[18]{0:T(512)(128)(4,1)S(1)}, u32[]{:S(2)}) copy-start(pred[18]{0:T(512)(128)(4,1)S(1)} %get-tuple-element.18) | copy-start | bytes 58
  67.3 0.8 copy-start.8
  67.3 185.4 %reduce-scatter.9.cloned.1.call-start = ((), (), s32[]{:S(2)}) async-start(), calls=%async_computation.7 | async-start | bytes 2228224 | tf_op jit(solution)/shard_map/reduce_scatter | solution.py:35
  90.1 1.1 copy-start.9
  91.8 2.4 copy-start.6
  116.8 200.0 %all-gather.5.cloned.1.call-start = ((), (), s32[]{:S(2)}) async-start(), calls=%async_computation.5 | async-start | bytes 2228224 | tf_op jit(solution)/shard_map/all_gather | solution.py:41
  254.5 125.4 %all-gather.3.cloned.1.call-start = ((), (), s32[]{:S(2)}) async-start(), calls=%async_computation.4 | async-start | bytes 2228224 | tf_op jit(solution)/shard_map/all_gather | solution.py:41
  322.9 2.4 copy-start.10
  325.3 2.0 copy-start.3
  325.3 2.0 copy-start.16
  334.6 63.2 %all-to-all-start.1 = ((bf16[16,16,1024]{2,1,0:T(8,128)(2,1)}), bf16[16,16,1024]{2,1,0:T(8,128)(2,1)}, u32[]{:S(2)}, u32[]{:S(2)}) async-start(bf16[16,16,1024]{2,1,0:T(8,128)(2,1)} %convert_element_type.91), calls=%async_computation.1 | async-start | bytes 1048576 | tf_op jit(solution)/shard_map/all_to_all | solution.py:105
  386.1 2.4 copy-start.15
  388.5 2.0 copy-start.5
  388.5 2.0 copy-start.17
  396.8 13.1 %copy-start.2 = (bf16[18,256,128]{2,1,0:T(8,128)(2,1)S(1)}, bf16[18,256,128]{2,1,0:T(8,128)(2,1)}, u32[]{:S(2)}) copy-start(bf16[18,256,128]{2,1,0:T(8,128)(2,1)} %gather_fusion.2) | copy-start | bytes 3538948
  396.8 13.1 %copy-start.14 = (pred[18]{0:T(512)(128)(4,1)S(1)}, pred[18]{0:T(512)(128)(4,1)}, u32[]{:S(2)}) copy-start(pred[18]{0:T(512)(128)(4,1)} %get-tuple-element.10) | copy-start | bytes 58
  397.8 34.6 %all-to-all-start = ((bf16[16,16,1024]{2,1,0:T(8,128)(2,1)}), bf16[16,16,1024]{2,1,0:T(8,128)(2,1)S(1)}, u32[]{:S(2)}, u32[]{:S(2)}) async-start(bf16[16,16,1024]{2,1,0:T(8,128)(2,1)} %convert_element_type.85), calls=%async_computation | async-start | bytes 1048576 | tf_op jit(solution)/shard_map/all_to_all | solution.py:102
  409.8 3.0 copy-start.1
  409.8 3.0 copy-start.11
  409.8 3.0 copy-start.13
  409.8 47.3 %all-reduce.3.cloned.1.call-start = ((), (), s32[]{:S(2)}) async-start(), calls=%async_computation.8 | async-start | bytes 2359296 | tf_op jit(solution)/shard_map/psum | solution.py:118
  409.9 2.9 copy-start.4
  457.2 2.0 copy-start.7
Sparse Core Ops, SparseCore 0:
  67.4 91.3 reduce-scatter.6
  163.5 89.0 reduce-scatter.8
  256.3 60.4 all-gather.4
  320.1 59.6 all-gather.2
  414.4 42.7 all-reduce.2
where the time goes:
time: 468 us; the launch traced here: 467 us
  waiting for transfers between devices  272 us (58%)
  blocking collectives  54.2 us (12%)
  local copies, waits for them, and re-layouts  47.2 us (10%)
  other arithmetic  41.9 us (9%)
  starting transfers between devices  24.3 us (5%)
  between operations  15.4 us (3%)
  matrix products  11.8 us (3%)
    reduce_scatter x2, waiting for transfers between devices, reduce_rows(): lax.psum_scatter(partial_value.astype(jnp.bfloat16), 'row', scatter_dimen...  136 us
    all_gather x2, waiting for transfers between devices, gather_rows(): return lax.all_gather(shares, 'row', axis=0, tiled=True)  94.9 us
    all_gather x1, blocking collectives, on_device(): lax.all_gather(tokens, 'col', axis=0, tiled=True)  32 us
    scatter-add x4, other arithmetic, apply_blocks(): placed = placed.at[:, target_index].add(products)  28.7 us
    psum x1, waiting for transfers between devices, on_device(): lax.psum(first_grad.astype(jnp.bfloat16), 'tok').astype(jnp.float32)  24.1 us
    all_gather x1, blocking collectives, on_device(): lax.all_gather(cotangent, 'col', axis=0, tiled=True)  22.1 us
    all_to_all x1, waiting for transfers between devices, on_device(): lax.all_to_all(output_part.astype(jnp.bfloat16), 'col', split_axis=0, con...  16.4 us
    all_to_all x1, starting transfers between devices, on_device(): lax.all_to_all(input_part.astype(jnp.bfloat16), 'col', split_axis=0, conc...  12.1 us
  transfers between devices with their start and end apart: 7, of which 6 were waited for; matrix products, arithmetic and copies ran while one was open for 15% of the time, Pallas kernels for 0%

commit v1 on v0

v1 whole, which is shorter than its diff:
```python
import functools

import jax
import jax.numpy as jnp
from jax import lax
from jax.experimental import pallas as pl
from jax.experimental.pallas import tpu as pltpu
from jax.sharding import PartitionSpec as P

F = 65536
BS = 128
ROWS = 16
VMEM_BYTES = 12 * 1024 * 1024

VMEM = functools.partial(pl.BlockSpec, memory_space=pltpu.VMEM)
SMEM = functools.partial(pl.BlockSpec, memory_space=pltpu.SMEM)


def call(body, in_specs, out_shapes, scratch=(), flops=0, nbytes=0):
    return pl.pallas_call(
        body,
        in_specs=in_specs,
        out_specs=jax.tree.map(lambda _: VMEM(), out_shapes),
        out_shape=out_shapes,
        scratch_shapes=list(scratch),
        compiler_params=pltpu.CompilerParams(vmem_limit_bytes=VMEM_BYTES),
        cost_estimate=pl.CostEstimate(flops=flops, bytes_accessed=nbytes, transcendentals=0),
    )


def slot_products(rows, blocks, source_index, transpose):
    peers, share, width = rows.shape
    slots = blocks.shape[0]
    dims = (((1,), (1,)), ((), ())) if transpose else (((1,), (0,)), ((), ()))

    def body(index_ref, rows_ref, blocks_ref, out_ref):
        for s in range(slots):
            start = pl.multiple_of(index_ref[s] * BS, BS)
            left = rows_ref[:, :, pl.ds(start, BS)].reshape(peers * share, BS)
            product = lax.dot_general(left, blocks_ref[s], dims, preferred_element_type=jnp.float32)
            out_ref[:, s] = product.astype(jnp.bfloat16).reshape(peers, share, BS)

    return call(
        body,
        [SMEM(), VMEM(), VMEM()],
        jax.ShapeDtypeStruct((peers, slots, share, BS), jnp.bfloat16),
        flops=2 * slots * peers * share * BS * BS,
        nbytes=4 * slots * peers * share * BS,
    )(source_index, rows, blocks)


def add_slots(index_ref, offset, parts_ref, total):
    peers, slots = parts_ref.shape[:2]
    total[...] = jnp.zeros_like(total)

    def step(p, carry):
        for s in range(slots):
            target = index_ref[p, offset + s]
            total[target] = total[target] + parts_ref[p, s].astype(jnp.float32)
        return carry

    lax.fori_loop(0, peers, step, 0)


def pick_slots(index_ref, offset, source, out_ref):
    peers, slots = out_ref.shape[:2]

    def step(p, carry):
        for s in range(slots):
            out_ref[p, s] = source[index_ref[p, offset + s]]
        return carry

    lax.fori_loop(0, peers, step, 0)


def activate(parts, index, hidden_blocks):
    peers, slots, share, width = parts.shape

    def body(index_ref, parts_ref, pre_ref, out_ref, total, source):
        add_slots(index_ref, 0, parts_ref, total)
        pre = total[:hidden_blocks]
        pre_ref[...] = pre
        source[:hidden_blocks] = (pre * (1.0 / (1.0 + jnp.exp(-pre)))).astype(jnp.bfloat16)
        source[hidden_blocks:] = jnp.zeros((1, share, width), jnp.bfloat16)
        pick_slots(index_ref, 64, source, out_ref)

    return call(
        body,
        [SMEM(), VMEM()],
        (
            jax.ShapeDtypeStruct((hidden_blocks, share, width), jnp.float32),
            jax.ShapeDtypeStruct(parts.shape, jnp.bfloat16),
        ),
        scratch=[
            pltpu.VMEM((hidden_blocks + 1, share, width), jnp.float32),
            pltpu.VMEM((hidden_blocks + 1, share, width), jnp.bfloat16),
        ],
        flops=4 * parts.size,
        nbytes=6 * parts.size,
    )(index, parts)


def pre_gradient(parts, pre, index):
    peers, slots, share, width = parts.shape
    hidden_blocks = pre.shape[0]

    def body(index_ref, parts_ref, pre_ref, out_ref, total, source):
        add_slots(index_ref, 64, parts_ref, total)
        pre = pre_ref[...]
        gate = 1.0 / (1.0 + jnp.exp(-pre))
        grad = total[:hidden_blocks] * gate * (1.0 + pre * (1.0 - gate))
        source[:hidden_blocks] = grad.astype(jnp.bfloat16)
        source[hidden_blocks:] = jnp.zeros((1, share, width), jnp.bfloat16)
        pick_slots(index_ref, 0, source, out_ref)

    return call(
        body,
        [SMEM(), VMEM(), VMEM()],
        jax.ShapeDtypeStruct(parts.shape, jnp.bfloat16),
        scratch=[
            pltpu.VMEM((hidden_blocks + 1, share, width), jnp.float32),
            pltpu.VMEM((hidden_blocks + 1, share, width), jnp.bfloat16),
        ],
        flops=4 * parts.size,
        nbytes=6 * parts.size,
    )(index, parts, pre)


def feature_sums(slots_in, blocks, target_index, feature_blocks, transpose):
    peers, slots, share, width = slots_in.shape
    dims = (((1,), (1,)), ((), ())) if transpose else (((1,), (0,)), ((), ()))

    def body(index_ref, in_ref, blocks_ref, out_ref, total):
        total[...] = jnp.zeros_like(total)
        for s in range(slots):
            left = in_ref[:, s].reshape(peers * share, width)
            product = lax.dot_general(left, blocks_ref[s], dims, preferred_element_type=jnp.float32)
            target = index_ref[s]
            total[target] = total[target] + product
        for k in range(feature_blocks):
            out_ref[:, k] = total[k].astype(jnp.bfloat16).reshape(peers, share, width)

    return call(
        body,
        [SMEM(), VMEM(), VMEM()],
        jax.ShapeDtypeStruct((peers, feature_blocks, share, width), jnp.bfloat16),
        scratch=[pltpu.VMEM((feature_blocks, peers * share, width), jnp.float32)],
        flops=2 * slots_in.size * BS,
        nbytes=4 * slots_in.size,
    )(target_index, slots_in, blocks)


def block_grads(rows, slots_in, feature_index, rows_first):
    peers, slots, share, width = slots_in.shape
    dims = (((0,), (0,)), ((), ()))

    def body(index_ref, rows_ref, in_ref, out_ref):
        for s in range(slots):
            start = pl.multiple_of(index_ref[s] * BS, BS)
            feature = rows_ref[:, :, pl.ds(start, BS)].reshape(peers * share, BS)
            hidden = in_ref[:, s].reshape(peers * share, width)
            pair = (feature, hidden) if rows_first else (hidden, feature)
            grad = lax.dot_general(*pair, dims, preferred_element_type=jnp.float32)
            out_ref[s] = grad.astype(jnp.bfloat16)

    return call(
        body,
        [SMEM(), VMEM(), VMEM()],
        jax.ShapeDtypeStruct((slots, BS, BS), jnp.bfloat16),
        flops=2 * slots_in.size * BS,
        nbytes=4 * slots_in.size,
    )(feature_index, rows, slots_in)


def owner_sum(parts):
    peers, feature_blocks, share, width = parts.shape

    def body(parts_ref, out_ref):
        for k in range(feature_blocks):
            total = parts_ref[0, k].astype(jnp.float32)
            for c in range(1, peers):
                total = total + parts_ref[c, k].astype(jnp.float32)
            out_ref[:, k * width : (k + 1) * width] = total.astype(jnp.bfloat16)

    return call(
        body,
        [VMEM()],
        jax.ShapeDtypeStruct((share, feature_blocks * width), jnp.bfloat16),
        flops=parts.size,
        nbytes=2 * parts.size,
    )(parts)


def swap(parts, axis):
    return lax.all_to_all(parts, axis, split_axis=0, concat_axis=0, tiled=True)


def gather_tokens(share):
    peers = lax.axis_size("col")
    return swap(jnp.broadcast_to(share[None], (peers,) + share.shape), "col")


def add_groups(grad):
    other = lax.ppermute(grad, "tok", [(0, 1), (1, 0)])
    total = grad.astype(jnp.float32) + other.astype(jnp.float32)
    return total.astype(jnp.bfloat16)[None, None]


def on_device(tokens, w1_blocks, w1_coords, w1_count, w2_blocks, w2_coords, w2_count, cotangent):
    first_blocks, second_blocks = w1_blocks[0, 0], w2_blocks[0, 0]
    first_coords, second_coords = w1_coords[0, 0], w2_coords[0, 0]
    slots = first_blocks.shape[0]
    feature_blocks = tokens.shape[1] // BS
    hidden_blocks = F // lax.axis_size("col") // BS

    live = jnp.arange(slots, dtype=jnp.int32)
    first_hidden = jnp.where(live < w1_count[0, 0], first_coords[:, 1], hidden_blocks)
    second_hidden = jnp.where(live < w2_count[0, 0], second_coords[:, 0], hidden_blocks)
    own = jnp.concatenate(
        [jnp.pad(first_hidden, (0, 64 - slots)), jnp.pad(second_hidden, (0, 64 - slots))]
    )
    rows = lax.axis_size("row")
    index = swap(jnp.broadcast_to(own[None], (rows, 128)), "row")
    first_feature, second_feature = first_coords[:, 0], second_coords[:, 1]

    token_rows = gather_tokens(tokens)
    cotan_rows = gather_tokens(cotangent)
    pre_parts = swap(slot_products(token_rows, first_blocks, first_feature, False), "row")
    act_parts = swap(slot_products(cotan_rows, second_blocks, second_feature, True), "row")
    pre, act_send = activate(pre_parts, index, hidden_blocks)
    act_slots = swap(act_send, "row")
    grad_slots = swap(pre_gradient(act_parts, pre, index), "row")
    out_parts = swap(
        feature_sums(act_slots, second_blocks, second_feature, feature_blocks, False), "col"
    )
    in_parts = swap(
        feature_sums(grad_slots, first_blocks, first_feature, feature_blocks, True), "col"
    )
    second_grad = add_groups(block_grads(cotan_rows, act_slots, second_feature, False))
    first_grad = add_groups(block_grads(token_rows, grad_slots, first_feature, True))
    return owner_sum(out_parts), owner_sum(in_parts), first_grad, second_grad


def solution(mesh):
    placed = (
        P(("tok", "col"), "row"),
        P("row", "col", None, None, None),
        P("row", "col", None, None),
        P("row", "col"),
        P("row", "col", None, None, None),
        P("row", "col", None, None),
        P("row", "col"),
        P(("tok", "col"), "row"),
    )
    return jax.shard_map(
        on_device,
        mesh=mesh,
        in_specs=placed,
        out_specs=(
            P(("tok", "col"), "row"),
            P(("tok", "col"), "row"),
            P("row", "col", None, None, None),
            P("row", "col", None, None, None),
        ),
        check_vma=False,
    )
```

time: 468 us -> 254 us (0.54)
  the two profiles are of different devices: /device:TPU:1 before, /device:TPU:32 now
where the time goes in v1:
time: 254 us; the launch traced here: 252 us
  waiting for transfers between devices  96 us (38%)
  blocking collectives  73.6 us (29%)
  starting transfers between devices  52.2 us (21%)
  Pallas kernels  17.1 us (7%)
  local copies, waits for them, and re-layouts  8.08 us (3%)
  other arithmetic  3.43 us (1%)
    all_to_all x6, waiting for transfers between devices, swap(): return lax.all_to_all(parts, axis, split_axis=0, concat_axis=0, tiled=True)  95.3 us
    all_to_all x3, blocking collectives, swap(): return lax.all_to_all(parts, axis, split_axis=0, concat_axis=0, tiled=True)  73.6 us
    all_to_all x6, starting transfers between devices, swap(): return lax.all_to_all(parts, axis, split_axis=0, concat_axis=0, tiled=True)  47.8 us
    unnamed x24, local copies, waits for them, and re-layouts  6.41 us
  transfers between devices with their start and end apart: 8, of which 7 were waited for; matrix products, arithmetic and copies ran while one was open for 1% of the time, Pallas kernels for 5%

profile of v1, /device:TPU:32, one launch (start us, length us, event | category | flops | bytes accessed | tf_op | source)
XLA Modules:
  0.0 252.4 jit_solution(11326676402887784592)
XLA Ops:
  0.6 0.0 copy-start.9
  1.9 0.7 compare_select_fusion
  2.6 0.7 compare_select_fusion.1
  3.3 0.1 pad_add_fusion
  3.4 14.4 %all_to_all.48 = s32[16,1,128]{2,1,0:T(1,128)S(1)} all-to-all(s32[16,1,128]{2,1,0:T(1,128)S(1)} %broadcast_in_dim.30), channel_id=1, replica_groups=mesh['tok'=2,'row'=16,'col'=16] {'row'}, dimensions={0} | all-to-all | bytes 16384 | tf_op jit(solution)/shard_map/all_to_all | solution.py:195
  17.8 0.8 broadcast_in_dim.31
  18.6 0.0 copy-start.10
  18.6 0.0 copy-start
  18.6 42.3 %all_to_all.49.rows_ref = bf16[16,16,1024]{2,1,0:T(8,128)(2,1)S(1)} all-to-all(bf16[16,16,1024]{2,1,0:T(8,128)(2,1)S(1)} %broadcast_in_dim.31), channel_id=1, replica_groups=mesh['tok'=2,'row'=16,'col'=16] {'col'}, dimensions={0} | all-to-all | bytes 1048576 | tf_op jit(solution)/shard_map/all_to_all | solution.py:195
  61.0 0.0 copy-done.9
  61.0 0.9 broadcast_in_dim.32
  61.8 6.8 %all-to-all-start.5 = ((bf16[16,16,1024]{2,1,0:T(8,128)(2,1)}), bf16[16,16,1024]{2,1,0:T(8,128)(2,1)S(1)}, u32[]{:S(2)}, u32[]{:S(2)}) async-start(bf16[16,16,1024]{2,1,0:T(8,128)(2,1)} %broadcast_in_dim.32), calls=%async_computation.5 | async-start | bytes 1048576 | tf_op jit(solution)/shard_map/all_to_all | solution.py:195
  68.6 0.0 copy-done.10
  68.6 0.0 copy-done
  68.6 2.0 shard_map.111
  70.6 0.0 copy-start.11
  70.6 0.0 copy-start.2
  70.6 25.6 %all-to-all-done.5.rows_ref = bf16[16,16,1024]{2,1,0:T(8,128)(2,1)S(1)} async-done(((bf16[16,16,1024]{2,1,0:T(8,128)(2,1)}), bf16[16,16,1024]{2,1,0:T(8,128)(2,1)S(1)}, u32[]{:S(2)}, u32[]{:S(2)}) %all-to-all-start.5) | async-done | bytes 524320 | tf_op jit(solution)/shard_map/all_to_all | solution.py:195
  96.2 3.7 %all-to-all-start.2 = ((bf16[16,18,16,128]{3,2,1,0:T(8,128)(2,1)}), bf16[16,18,16,128]{3,2,1,0:T(8,128)(2,1)S(1)}, u32[]{:S(2)}, u32[]{:S(2)}) async-start(bf16[16,18,16,128]{3,2,1,0:T(8,128)(2,1)} %shard_map.111), calls=%async_computation.2 | async-start | bytes 2359296 | tf_op jit(solution)/shard_map/all_to_all | solution.py:195
  100.0 0.0 copy-done.11
  100.0 0.0 copy-done.2
  100.0 2.1 shard_map.115
  102.1 12.3 %all-to-all-done.2.parts_ref = bf16[16,18,16,128]{3,2,1,0:T(8,128)(2,1)S(1)} async-done(((bf16[16,18,16,128]{3,2,1,0:T(8,128)(2,1)}), bf16[16,18,16,128]{3,2,1,0:T(8,128)(2,1)S(1)}, u32[]{:S(2)}, u32[]{:S(2)}) %all-to-all-start.2) | async-done | bytes 1179680 | tf_op jit(solution)/shard_map/all_to_all | solution.py:195
  114.4 3.7 %all-to-all-start.6 = ((bf16[16,18,16,128]{3,2,1,0:T(8,128)(2,1)}), bf16[16,18,16,128]{3,2,1,0:T(8,128)(2,1)S(1)}, u32[]{:S(2)}, u32[]{:S(2)}) async-start(bf16[16,18,16,128]{3,2,1,0:T(8,128)(2,1)} %shard_map.115), calls=%async_computation.6 | async-start | bytes 2359296 | tf_op jit(solution)/shard_map/all_to_all | solution.py:195
  118.1 2.5 shard_map.112
  120.6 0.0 copy-start.6
  120.6 1.0 copy-done.6
  121.6 0.0 copy-start.7
  121.6 0.7 copy-done.7
  122.3 9.4 %all-to-all-done.6.parts_ref = bf16[16,18,16,128]{3,2,1,0:T(8,128)(2,1)S(1)} async-done(((bf16[16,18,16,128]{3,2,1,0:T(8,128)(2,1)}), bf16[16,18,16,128]{3,2,1,0:T(8,128)(2,1)S(1)}, u32[]{:S(2)}, u32[]{:S(2)}) %all-to-all-start.6) | async-done | bytes 1179680 | tf_op jit(solution)/shard_map/all_to_all | solution.py:195
  131.8 0.0 copy-start.8
  131.8 0.9 copy-done.8
  132.7 2.6 %shard_map.116 = bf16[16,18,16,128]{3,2,1,0:T(8,128)(2,1)S(1)} custom-call(s32[16,128]{1,0:T(8,128)S(1)} %bitcast.26, bf16[16,18,16,128]{3,2,1,0:T(8,128)(2,1)S(1)} %all-to-all-done.6.parts_ref, f32[32,16,128]{2,1,0:T(8,128)S(1)} %copy-done.8), custom_call_target="tpu_custom_call" | custom-call | flops 2359296 | bytes 3538944 | tf_op jit(solution)/shard_map/pallas_call | solution.py:116
  135.3 16.8 %all_to_all.50.in_ref = bf16[16,18,16,128]{3,2,1,0:T(8,128)(2,1)S(1)} all-to-all(bf16[16,18,16,128]{3,2,1,0:T(8,128)(2,1)S(1)} %shard_map.116), channel_id=1, replica_groups=mesh['tok'=2,'row'=16,'col'=16] {'row'}, dimensions={0} | all-to-all | bytes 2359296 | tf_op jit(solution)/shard_map/all_to_all | solution.py:195
  152.2 3.7 %all-to-all-start.3 = ((bf16[16,18,16,128]{3,2,1,0:T(8,128)(2,1)}), bf16[16,18,16,128]{3,2,1,0:T(8,128)(2,1)S(1)}, u32[]{:S(2)}, u32[]{:S(2)}) async-start(bf16[16,18,16,128]{3,2,1,0:T(8,128)(2,1)} %copy-done.6), calls=%async_computation.3 | async-start | bytes 2359296 | tf_op jit(solution)/shard_map/all_to_all | solution.py:195
  155.9 0.0 copy-start.1
  155.9 1.1 copy-done.1
  156.9 1.1 shard_map.117
  158.0 0.0 copy-start.5
  158.1 0.8 copy-done.5
  158.8 10.6 %all-to-all-done.3.in_ref = bf16[16,18,16,128]{3,2,1,0:T(8,128)(2,1)S(1)} async-done(((bf16[16,18,16,128]{3,2,1,0:T(8,128)(2,1)}), bf16[16,18,16,128]{3,2,1,0:T(8,128)(2,1)S(1)}, u32[]{:S(2)}, u32[]{:S(2)}) %all-to-all-start.3) | async-done | bytes 1179680 | tf_op jit(solution)/shard_map/all_to_all | solution.py:195
  169.5 21.4 %all-to-all-start.8 = ((bf16[16,8,16,128]{3,2,1,0:T(8,128)(2,1)}), bf16[16,8,16,128]{3,2,1,0:T(8,128)(2,1)}, u32[]{:S(2)}, u32[]{:S(2)}) async-start(bf16[16,8,16,128]{3,2,1,0:T(8,128)(2,1)} %copy-done.5), calls=%async_computation.8 | async-start | bytes 1048576 | tf_op jit(solution)/shard_map/all_to_all | solution.py:195
  190.8 0.0 copy-start.3
  190.8 1.1 copy-done.3
  191.9 1.1 shard_map.113
  193.0 0.0 copy-start.4
  193.0 0.8 copy-done.4
  193.8 20.8 %all-to-all-done.8.parts_ref = bf16[16,8,16,128]{3,2,1,0:T(8,128)(2,1)} async-done(((bf16[16,8,16,128]{3,2,1,0:T(8,128)(2,1)}), bf16[16,8,16,128]{3,2,1,0:T(8,128)(2,1)}, u32[]{:S(2)}, u32[]{:S(2)}) %all-to-all-start.8) | async-done | bytes 524320 | tf_op jit(solution)/shard_map/all_to_all | solution.py:195
  214.6 8.6 %all-to-all-start.4 = ((bf16[16,8,16,128]{3,2,1,0:T(8,128)(2,1)}), bf16[16,8,16,128]{3,2,1,0:T(8,128)(2,1)}, u32[]{:S(2)}, u32[]{:S(2)}) async-start(bf16[16,8,16,128]{3,2,1,0:T(8,128)(2,1)} %copy-done.4), calls=%async_computation.4 | async-start | bytes 1048576 | tf_op jit(solution)/shard_map/all_to_all | solution.py:195
  223.2 1.1 shard_map.120
  224.3 1.9 collective-permute-start.1
  226.2 1.1 shard_map.119
  227.4 2.4 collective-permute-start
  229.8 0.0 collective-permute-done.1
  229.8 1.0 fusion.1
  230.8 0.6 collective-permute-done
  231.4 1.0 fusion
  232.4 1.7 shard_map.118
  234.1 16.6 %all-to-all-done.4.parts_ref = bf16[16,8,16,128]{3,2,1,0:T(8,128)(2,1)} async-done(((bf16[16,8,16,128]{3,2,1,0:T(8,128)(2,1)}), bf16[16,8,16,128]{3,2,1,0:T(8,128)(2,1)}, u32[]{:S(2)}, u32[]{:S(2)}) %all-to-all-start.4) | async-done | bytes 524320 | tf_op jit(solution)/shard_map/all_to_all | solution.py:195
  250.7 1.7 shard_map.114
  (3 shorter events, 0.0 us)
Async XLA Ops:
  0.6 60.3 %copy-start.9 = (bf16[16,1024]{1,0:T(8,128)(2,1)S(1)}, bf16[16,1024]{1,0:T(8,128)(2,1)}, u32[]{:S(2)}) copy-start(bf16[16,1024]{1,0:T(8,128)(2,1)} %param.15) | copy-start | bytes 98308
  18.6 50.0 %copy-start.10 = (s32[1,1,18,2]{2,3,1,0:T(2,128)S(1)}, s32[1,1,18,2]{2,3,1,0:T(2,128)}, u32[]{:S(2)}) copy-start(s32[1,1,18,2]{2,3,1,0:T(2,128)} %param.10) | copy-start | bytes 436
  18.6 50.0 %copy-start = (bf16[1,1,18,128,128]{4,3,2,1,0:T(8,128)(2,1)S(1)}, bf16[1,1,18,128,128]{4,3,2,1,0:T(8,128)(2,1)}, u32[]{:S(2)}) copy-start(bf16[1,1,18,128,128]{4,3,2,1,0:T(8,128)(2,1)} %param.9) | copy-start | bytes 1769476
  61.8 34.4 %all-to-all-start.5 = ((bf16[16,16,1024]{2,1,0:T(8,128)(2,1)}), bf16[16,16,1024]{2,1,0:T(8,128)(2,1)S(1)}, u32[]{:S(2)}, u32[]{:S(2)}) async-start(bf16[16,16,1024]{2,1,0:T(8,128)(2,1)} %broadcast_in_dim.32), calls=%async_computation.5 | async-start | bytes 1048576 | tf_op jit(solution)/shard_map/all_to_all | solution.py:195
  70.6 29.3 %copy-start.11 = (s32[1,1,18,2]{2,3,1,0:T(2,128)S(1)}, s32[1,1,18,2]{2,3,1,0:T(2,128)}, u32[]{:S(2)}) copy-start(s32[1,1,18,2]{2,3,1,0:T(2,128)} %param.13) | copy-start | bytes 436
  70.6 29.3 %copy-start.2 = (bf16[1,1,18,128,128]{4,3,2,1,0:T(8,128)(2,1)S(1)}, bf16[1,1,18,128,128]{4,3,2,1,0:T(8,128)(2,1)}, u32[]{:S(2)}) copy-start(bf16[1,1,18,128,128]{4,3,2,1,0:T(8,128)(2,1)} %param.12) | copy-start | bytes 1769476
  96.2 18.2 %all-to-all-start.2 = ((bf16[16,18,16,128]{3,2,1,0:T(8,128)(2,1)}), bf16[16,18,16,128]{3,2,1,0:T(8,128)(2,1)S(1)}, u32[]{:S(2)}, u32[]{:S(2)}) async-start(bf16[16,18,16,128]{3,2,1,0:T(8,128)(2,1)} %shard_map.111), calls=%async_computation.2 | async-start | bytes 2359296 | tf_op jit(solution)/shard_map/all_to_all | solution.py:195
  114.4 17.4 %all-to-all-start.6 = ((bf16[16,18,16,128]{3,2,1,0:T(8,128)(2,1)}), bf16[16,18,16,128]{3,2,1,0:T(8,128)(2,1)S(1)}, u32[]{:S(2)}, u32[]{:S(2)}) async-start(bf16[16,18,16,128]{3,2,1,0:T(8,128)(2,1)} %shard_map.115), calls=%async_computation.6 | async-start | bytes 2359296 | tf_op jit(solution)/shard_map/all_to_all | solution.py:195
  120.6 1.0 copy-start.6
  121.6 0.7 copy-start.7
  131.8 1.0 copy-start.8
  152.2 17.3 %all-to-all-start.3 = ((bf16[16,18,16,128]{3,2,1,0:T(8,128)(2,1)}), bf16[16,18,16,128]{3,2,1,0:T(8,128)(2,1)S(1)}, u32[]{:S(2)}, u32[]{:S(2)}) async-start(bf16[16,18,16,128]{3,2,1,0:T(8,128)(2,1)} %copy-done.6), calls=%async_computation.3 | async-start | bytes 2359296 | tf_op jit(solution)/shard_map/all_to_all | solution.py:195
  155.9 1.1 copy-start.1
  158.0 0.8 copy-start.5
  169.5 45.1 %all-to-all-start.8 = ((bf16[16,8,16,128]{3,2,1,0:T(8,128)(2,1)}), bf16[16,8,16,128]{3,2,1,0:T(8,128)(2,1)}, u32[]{:S(2)}, u32[]{:S(2)}) async-start(bf16[16,8,16,128]{3,2,1,0:T(8,128)(2,1)} %copy-done.5), calls=%async_computation.8 | async-start | bytes 1048576 | tf_op jit(solution)/shard_map/all_to_all | solution.py:195
  190.8 1.1 copy-start.3
  193.0 0.8 copy-start.4
  214.6 36.1 %all-to-all-start.4 = ((bf16[16,8,16,128]{3,2,1,0:T(8,128)(2,1)}), bf16[16,8,16,128]{3,2,1,0:T(8,128)(2,1)}, u32[]{:S(2)}, u32[]{:S(2)}) async-start(bf16[16,8,16,128]{3,2,1,0:T(8,128)(2,1)} %copy-done.4), calls=%async_computation.4 | async-start | bytes 1048576 | tf_op jit(solution)/shard_map/all_to_all | solution.py:195
  224.3 5.5 %collective-permute-start.1 = (bf16[18,128,128]{2,1,0:T(8,128)(2,1)S(1)}, bf16[18,128,128]{2,1,0:T(8,128)(2,1)S(1)}, u32[]{:S(2)}, u32[]{:S(2)}) collective-permute-start(bf16[18,128,128]{2,1,0:T(8,128)(2,1)S(1)} %shard_map.120), channel_id=1, source_target_pairs={{0,256},{256,0},{1,257},{257,1},{2,258},{258,2},{3,259},{259,3},{4... | collective-permute-start | bytes 1769480 | tf_op jit(solution)/shard_map/ppermute | solution.py:204
  227.4 4.0 %collective-permute-start = (bf16[18,128,128]{2,1,0:T(8,128)(2,1)S(1)}, bf16[18,128,128]{2,1,0:T(8,128)(2,1)S(1)}, u32[]{:S(2)}, u32[]{:S(2)}) collective-permute-start(bf16[18,128,128]{2,1,0:T(8,128)(2,1)S(1)} %shard_map.119), channel_id=1, source_target_pairs={{0,256},{256,0},{1,257},{257,1},{2,258},{258,2},{3,259},{259,3},{4... | collective-permute-start | bytes 1769480 | tf_op jit(solution)/shard_map/ppermute | solution.py:204

commit v2 on v0

v2 whole, which is shorter than its diff:
```python
import functools

import jax
import jax.numpy as jnp
from jax import lax
from jax.experimental import pallas as pl
from jax.experimental.pallas import tpu as pltpu
from jax.sharding import PartitionSpec as P

F = 65536
BS = 128
ROWS = 16
VMEM_BYTES = 12 * 1024 * 1024

VMEM = functools.partial(pl.BlockSpec, memory_space=pltpu.VMEM)
SMEM = functools.partial(pl.BlockSpec, memory_space=pltpu.SMEM)


def call(body, in_specs, out_shapes, scratch=(), flops=0, nbytes=0):
    return pl.pallas_call(
        body,
        in_specs=in_specs,
        out_specs=jax.tree.map(lambda _: VMEM(), out_shapes),
        out_shape=out_shapes,
        scratch_shapes=list(scratch),
        compiler_params=pltpu.CompilerParams(vmem_limit_bytes=VMEM_BYTES),
        cost_estimate=pl.CostEstimate(flops=flops, bytes_accessed=nbytes, transcendentals=0),
    )


def product_dims(transpose):
    return (((1,), (1,)), ((), ())) if transpose else (((1,), (0,)), ((), ()))


def slot_products(tokens, cotangent, first, second, first_feature, second_feature, table):
    peers, share, width = tokens.shape
    slots = first.shape[0]

    def body(i1_ref, i2_ref, x_ref, g_ref, w1_ref, w2_ref, table_ref, out_ref):
        for base, index_ref, rows_ref, blocks_ref in (
            (0, i1_ref, x_ref, w1_ref),
            (slots, i2_ref, g_ref, w2_ref),
        ):
            for s in range(slots):
                start = pl.multiple_of(index_ref[s] * BS, BS)
                left = rows_ref[:, :, pl.ds(start, BS)].reshape(peers * share, BS)
                product = lax.dot_general(
                    left, blocks_ref[s], product_dims(base > 0), preferred_element_type=jnp.float32
                )
                out_ref[:, base + s] = product.astype(jnp.bfloat16).reshape(peers, share, BS)
        for p in range(peers):
            out_ref[p, 2 * slots] = table_ref[...]

    return call(
        body,
        [SMEM()] * 2 + [VMEM()] * 5,
        jax.ShapeDtypeStruct((peers, 2 * slots + 1, share, BS), jnp.bfloat16),
        flops=4 * slots * peers * share * BS * BS,
        nbytes=8 * slots * peers * share * BS,
    )(first_feature, second_feature, tokens, cotangent, first, second, table)


def hidden_step(parts, hidden_blocks):
    peers, width = parts.shape[0], parts.shape[3]
    slots = parts.shape[1] // 2
    share = parts.shape[2]

    def body(parts_ref, out_ref, pre, grad, act_blocks, grad_blocks, table, index, sem):
        row = lax.broadcasted_iota(jnp.int32, (peers, width), 0)
        lines = jnp.zeros((peers, width), jnp.float32)
        for p in range(peers):
            lines = jnp.where(row == p, parts_ref[p, 2 * slots].astype(jnp.float32), lines)
        table[...] = lines.astype(jnp.int32)
        copy = pltpu.make_async_copy(table, index, sem)
        copy.start()
        pre[...] = jnp.zeros_like(pre)
        grad[...] = jnp.zeros_like(grad)
        act_blocks[hidden_blocks:] = jnp.zeros((1, share, width), jnp.bfloat16)
        grad_blocks[hidden_blocks:] = jnp.zeros((1, share, width), jnp.bfloat16)
        copy.wait()

        def add(p, carry):
            for s in range(slots):
                i, j = index[p, s], index[p, 64 + s]
                pre[i] = pre[i] + parts_ref[p, s].astype(jnp.float32)
                grad[j] = grad[j] + parts_ref[p, slots + s].astype(jnp.float32)
            return carry

        lax.fori_loop(0, peers, add, 0)

        def point(h, carry):
            value = pre[h]
            gate = 1.0 / (1.0 + jnp.exp(-value))
            act_blocks[h] = (value * gate).astype(jnp.bfloat16)
            grad_blocks[h] = (grad[h] * gate * (1.0 + value * (1.0 - gate))).astype(jnp.bfloat16)
            return carry

        lax.fori_loop(0, hidden_blocks, point, 0, unroll=8)

        def pick(p, carry):
            for s in range(slots):
                out_ref[p, s] = act_blocks[index[p, 64 + s]]
                out_ref[p, slots + s] = grad_blocks[index[p, s]]
            return carry

        lax.fori_loop(0, peers, pick, 0)

    return call(
        body,
        [VMEM()],
        jax.ShapeDtypeStruct((peers, 2 * slots, share, width), jnp.bfloat16),
        scratch=[
            pltpu.VMEM((hidden_blocks + 1, share, width), jnp.float32),
            pltpu.VMEM((hidden_blocks + 1, share, width), jnp.float32),
            pltpu.VMEM((hidden_blocks + 1, share, width), jnp.bfloat16),
            pltpu.VMEM((hidden_blocks + 1, share, width), jnp.bfloat16),
            pltpu.VMEM((peers, width), jnp.int32),
            pltpu.SMEM((peers, width), jnp.int32),
            pltpu.SemaphoreType.DMA,
        ],
        flops=4 * parts.size,
        nbytes=6 * parts.size,
    )(parts)


def feature_sums(slots_in, first, second, first_feature, second_feature, feature_blocks):
    peers, both, share, width = slots_in.shape
    slots = both // 2

    def body(i1_ref, i2_ref, in_ref, w1_ref, w2_ref, out_ref, total):
        for base, index_ref, blocks_ref in ((0, i2_ref, w2_ref), (slots, i1_ref, w1_ref)):
            total[...] = jnp.zeros_like(total)
            for s in range(slots):
                left = in_ref[:, base + s].reshape(peers * share, width)
                product = lax.dot_general(
                    left, blocks_ref[s], product_dims(base > 0), preferred_element_type=jnp.float32
                )
                target = index_ref[s]
                total[target] = total[target] + product
            place = feature_blocks if base else 0
            for k in range(feature_blocks):
                out_ref[:, place + k] = total[k].astype(jnp.bfloat16).reshape(peers, share, width)

    return call(
        body,
        [SMEM()] * 2 + [VMEM()] * 3,
        jax.ShapeDtypeStruct((peers, 2 * feature_blocks, share, width), jnp.bfloat16),
        scratch=[pltpu.VMEM((feature_blocks, peers * share, width), jnp.float32)],
        flops=2 * slots_in.size * BS,
        nbytes=4 * slots_in.size,
    )(first_feature, second_feature, slots_in, first, second)


def block_grads(tokens, cotangent, slots_in, first_feature, second_feature):
    peers, both, share, width = slots_in.shape
    slots = both // 2
    dims = (((0,), (0,)), ((), ()))

    def body(i1_ref, i2_ref, x_ref, g_ref, in_ref, out_ref):
        for s in range(slots):
            start = pl.multiple_of(i1_ref[s] * BS, BS)
            feature = x_ref[:, :, pl.ds(start, BS)].reshape(peers * share, BS)
            hidden = in_ref[:, slots + s].reshape(peers * share, width)
            grad = lax.dot_general(feature, hidden, dims, preferred_element_type=jnp.float32)
            out_ref[s] = grad.astype(jnp.bfloat16)
        for s in range(slots):
            start = pl.multiple_of(i2_ref[s] * BS, BS)
            feature = g_ref[:, :, pl.ds(start, BS)].reshape(peers * share, BS)
            hidden = in_ref[:, s].reshape(peers * share, width)
            grad = lax.dot_general(hidden, feature, dims, preferred_element_type=jnp.float32)
            out_ref[slots + s] = grad.astype(jnp.bfloat16)

    return call(
        body,
        [SMEM()] * 2 + [VMEM()] * 3,
        jax.ShapeDtypeStruct((both, BS, BS), jnp.bfloat16),
        flops=2 * slots_in.size * BS,
        nbytes=4 * slots_in.size,
    )(first_feature, second_feature, tokens, cotangent, slots_in)


def owner_sums(parts):
    peers, both, share, width = parts.shape
    feature_blocks = both // 2

    def body(parts_ref, out_ref, in_ref):
        for k in range(both):
            total = parts_ref[0, k].astype(jnp.float32)
            for c in range(1, peers):
                total = total + parts_ref[c, k].astype(jnp.float32)
            target, place = (out_ref, k) if k < feature_blocks else (in_ref, k - feature_blocks)
            target[:, place * width : (place + 1) * width] = total.astype(jnp.bfloat16)

    shape = jax.ShapeDtypeStruct((share, feature_blocks * width), jnp.bfloat16)
    return call(body, [VMEM()], (shape, shape), flops=parts.size, nbytes=2 * parts.size)(parts)


def swap(parts, axis):
    return lax.all_to_all(parts, axis, split_axis=0, concat_axis=0, tiled=True)


def on_device(tokens, w1_blocks, w1_coords, w1_count, w2_blocks, w2_coords, w2_count, cotangent):
    first, second = w1_blocks[0, 0], w2_blocks[0, 0]
    first_coords, second_coords = w1_coords[0, 0], w2_coords[0, 0]
    slots = first.shape[0]
    feature_blocks = tokens.shape[1] // BS
    hidden_blocks = F // lax.axis_size("col") // BS
    first_feature, second_feature = first_coords[:, 0], second_coords[:, 1]

    live = jnp.arange(slots, dtype=jnp.int32)
    first_hidden = jnp.where(live < w1_count[0, 0], first_coords[:, 1], hidden_blocks)
    second_hidden = jnp.where(live < w2_count[0, 0], second_coords[:, 0], hidden_blocks)
    line = jnp.pad(first_hidden, (0, BS - slots)) + jnp.pad(second_hidden, (64, 64 - slots))
    table = jnp.broadcast_to(line.astype(jnp.bfloat16), (tokens.shape[0], BS))

    peers = lax.axis_size("col")
    cotan_rows = swap(jnp.broadcast_to(cotangent[None], (peers,) + cotangent.shape), "col")
    token_rows = lax.all_gather(tokens, "col", axis=0, tiled=True).reshape(cotan_rows.shape)
    parts = swap(
        slot_products(token_rows, cotan_rows, first, second, first_feature, second_feature, table),
        "row",
    )
    slots_in = swap(hidden_step(parts, hidden_blocks), "row")
    sums = swap(
        feature_sums(slots_in, first, second, first_feature, second_feature, feature_blocks), "col"
    )
    grads = block_grads(token_rows, cotan_rows, slots_in, first_feature, second_feature)
    others = lax.ppermute(grads, "tok", [(0, 1), (1, 0)])
    grads = (grads.astype(jnp.float32) + others.astype(jnp.float32)).astype(jnp.bfloat16)
    output, input_grad = owner_sums(sums)
    return output, input_grad, grads[None, None, :slots], grads[None, None, slots:]


def solution(mesh):
    placed = (
        P(("tok", "col"), "row"),
        P("row", "col", None, None, None),
        P("row", "col", None, None),
        P("row", "col"),
        P("row", "col", None, None, None),
        P("row", "col", None, None),
        P("row", "col"),
        P(("tok", "col"), "row"),
    )
    return jax.shard_map(
        on_device,
        mesh=mesh,
        in_specs=placed,
        out_specs=(
            P(("tok", "col"), "row"),
            P(("tok", "col"), "row"),
            P("row", "col", None, None, None),
            P("row", "col", None, None, None),
        ),
        check_vma=False,
    )
```

time: 468 us -> 189 us (0.40)
  the two profiles are of different devices: /device:TPU:1 before, /device:TPU:64 now
where the time goes in v2:
time: 189 us
  blocking collectives  109 us (58%)
  waiting for transfers between devices  35.5 us (19%)
  starting transfers between devices  26.6 us (14%)
  Pallas kernels  9.54 us (5%)
  local copies, waits for them, and re-layouts  4.51 us (2%)
  between operations  2.03 us (1%)
    all_to_all x2, blocking collectives, swap(): return lax.all_to_all(parts, axis, split_axis=0, concat_axis=0, tiled=True)  61.5 us
    all_gather x1, blocking collectives, on_device(): lax.all_gather(tokens, 'col', axis=0, tiled=True).reshape(cotan_rows.shape)  47.5 us
    all_to_all x2, waiting for transfers between devices, swap(): return lax.all_to_all(parts, axis, split_axis=0, concat_axis=0, tiled=True)  32.7 us
    all_to_all x2, starting transfers between devices, swap(): return lax.all_to_all(parts, axis, split_axis=0, concat_axis=0, tiled=True)  24.7 us
  transfers between devices with their start and end apart: 3, of which 2 were waited for; matrix products, arithmetic and copies ran while one was open for 2% of the time, Pallas kernels for 1%

profile of v2, /device:TPU:64, one launch (start us, length us, event | category | flops | bytes accessed | tf_op | source)
XLA Modules:
  0.0 188.5 jit_solution(1651401650545499805)
XLA Ops:
  0.6 0.0 copy-start.3
  0.6 0.0 copy-start.1
  0.7 1.7 broadcast_in_dim.20
  2.4 14.8 %all-to-all-start = ((bf16[16,16,1024]{2,1,0:T(8,128)(2,1)}), bf16[16,16,1024]{2,1,0:T(8,128)(2,1)S(1)}, u32[]{:S(2)}, u32[]{:S(2)}) async-start(bf16[16,16,1024]{2,1,0:T(8,128)(2,1)} %broadcast_in_dim.20), calls=%async_computation | async-start | bytes 1048576 | tf_op jit(solution)/shard_map/all_to_all | solution.py:199
  18.4 0.7 compare_select_fusion
  19.1 0.1 add_convert_fusion.1
  19.2 0.7 slice_bitcast_fusion.2
  19.9 47.5 %all_gather.3 = bf16[256,1024]{1,0:T(8,128)(2,1)S(1)} all-gather(bf16[16,1024]{1,0:T(8,128)(2,1)} %param.8), channel_id=1, replica_groups=mesh['tok'=2,'row'=16,'col'=16] {'col'}, dimensions={0}, use_global_device_ids=true | all-gather | bytes 557056 | tf_op jit(solution)/shard_map/all_gather | solution.py:218
  67.4 0.0 all-to-all-done.g_ref
  67.4 0.0 copy-done.3
  67.4 0.0 copy-done.1
  67.4 1.4 shard_map.111
  68.8 32.7 %all_to_all.20.parts_ref = bf16[16,37,16,128]{3,2,1,0:T(8,128)(2,1)S(1)} all-to-all(bf16[16,37,16,128]{3,2,1,0:T(8,128)(2,1)S(1)} %shard_map.111), channel_id=1, replica_groups=mesh['tok'=2,'row'=16,'col'=16] {'row'}, dimensions={0} | all-to-all | bytes 4849664 | tf_op jit(solution)/shard_map/all_to_all | solution.py:199
  101.5 3.2 %shard_map.112 = bf16[16,36,16,128]{3,2,1,0:T(8,128)(2,1)S(1)} custom-call(bf16[16,37,16,128]{3,2,1,0:T(8,128)(2,1)S(1)} %all_to_all.20.parts_ref), custom_call_target="tpu_custom_call" | custom-call | flops 4849664 | bytes 7274496 | tf_op jit(solution)/shard_map/pallas_call | solution.py:108
  104.7 0.0 copy-start.2
  104.7 0.0 copy-start.4
  104.7 28.7 %all_to_all.21.in_ref = bf16[16,36,16,128]{3,2,1,0:T(8,128)(2,1)S(1)} all-to-all(bf16[16,36,16,128]{3,2,1,0:T(8,128)(2,1)S(1)} %shard_map.112), channel_id=1, replica_groups=mesh['tok'=2,'row'=16,'col'=16] {'row'}, dimensions={0} | all-to-all | bytes 4718592 | tf_op jit(solution)/shard_map/all_to_all | solution.py:199
  133.5 0.0 copy-done.2
  133.5 0.0 copy-done.4
  133.5 1.5 shard_map.113
  135.0 0.0 copy-start
  135.0 1.0 copy-done
  136.0 9.9 %all-to-all-start.3 = ((bf16[16,16,16,128]{3,2,1,0:T(8,128)(2,1)}), bf16[16,16,16,128]{3,2,1,0:T(8,128)(2,1)}, u32[]{:S(2)}, u32[]{:S(2)}) async-start(bf16[16,16,16,128]{3,2,1,0:T(8,128)(2,1)} %copy-done), calls=%async_computation.3 | async-start | bytes 2097152 | tf_op jit(solution)/shard_map/all_to_all | solution.py:199
  146.0 1.5 shard_map.115
  147.4 1.9 %collective-permute-start = (bf16[36,128,128]{2,1,0:T(8,128)(2,1)S(1)}, bf16[36,128,128]{2,1,0:T(8,128)(2,1)S(1)}, u32[]{:S(2)}, u32[]{:S(2)}) collective-permute-start(bf16[36,128,128]{2,1,0:T(8,128)(2,1)S(1)} %shard_map.115), channel_id=1, source_target_pairs={{0,256},{256,0},{1,257},{257,1},{2,258},{258,2},{3,259},{259,3},{4... | collective-permute-start | bytes 3538952 | tf_op jit(solution)/shard_map/ppermute | solution.py:228
  149.4 2.8 %collective-permute-done = bf16[36,128,128]{2,1,0:T(8,128)(2,1)S(1)} collective-permute-done((bf16[36,128,128]{2,1,0:T(8,128)(2,1)S(1)}, bf16[36,128,128]{2,1,0:T(8,128)(2,1)S(1)}, u32[]{:S(2)}, u32[]{:S(2)}) %collective-permute-start) | collective-permute-done | bytes 1179680 | tf_op jit(solution)/shard_map/ppermute | solution.py:228
  152.2 0.5 add_convert_fusion
  152.7 1.1 slice_bitcast_fusion
  153.8 32.7 %all-to-all-done.3.parts_ref = bf16[16,16,16,128]{3,2,1,0:T(8,128)(2,1)} async-done(((bf16[16,16,16,128]{3,2,1,0:T(8,128)(2,1)}), bf16[16,16,16,128]{3,2,1,0:T(8,128)(2,1)}, u32[]{:S(2)}, u32[]{:S(2)}) %all-to-all-start.3) | async-done | bytes 1048608 | tf_op jit(solution)/shard_map/all_to_all | solution.py:199
  186.5 2.0 %shard_map.114 = (bf16[16,1024]{1,0:T(8,128)(2,1)}, bf16[16,1024]{1,0:T(8,128)(2,1)}) custom-call(bf16[16,16,16,128]{3,2,1,0:T(8,128)(2,1)} %all-to-all-done.3.parts_ref), custom_call_target="tpu_custom_call" | custom-call | flops 524288 | bytes 1048576 | tf_op jit(solution)/shard_map/pallas_call | solution.py:195
  (1 shorter events, 0.0 us)
Async XLA Ops:
  0.6 66.8 %copy-start.3 = (bf16[1,1,18,128,128]{4,3,2,1,0:T(8,128)(2,1)S(1)}, bf16[1,1,18,128,128]{4,3,2,1,0:T(8,128)(2,1)}, u32[]{:S(2)}) copy-start(bf16[1,1,18,128,128]{4,3,2,1,0:T(8,128)(2,1)} %param.12) | copy-start | bytes 1769476
  0.6 66.7 %copy-start.1 = (bf16[1,1,18,128,128]{4,3,2,1,0:T(8,128)(2,1)S(1)}, bf16[1,1,18,128,128]{4,3,2,1,0:T(8,128)(2,1)}, u32[]{:S(2)}) copy-start(bf16[1,1,18,128,128]{4,3,2,1,0:T(8,128)(2,1)} %param.9) | copy-start | bytes 1769476
  2.4 65.0 %all-to-all-start = ((bf16[16,16,1024]{2,1,0:T(8,128)(2,1)}), bf16[16,16,1024]{2,1,0:T(8,128)(2,1)S(1)}, u32[]{:S(2)}, u32[]{:S(2)}) async-start(bf16[16,16,1024]{2,1,0:T(8,128)(2,1)} %broadcast_in_dim.20), calls=%async_computation | async-start | bytes 1048576 | tf_op jit(solution)/shard_map/all_to_all | solution.py:199
  104.7 28.8 %copy-start.2 = (bf16[1,1,18,128,128]{4,3,2,1,0:T(8,128)(2,1)S(1)}, bf16[1,1,18,128,128]{4,3,2,1,0:T(8,128)(2,1)}, u32[]{:S(2)}) copy-start(bf16[1,1,18,128,128]{4,3,2,1,0:T(8,128)(2,1)} %param.9) | copy-start | bytes 1769476
  104.7 28.8 %copy-start.4 = (bf16[1,1,18,128,128]{4,3,2,1,0:T(8,128)(2,1)S(1)}, bf16[1,1,18,128,128]{4,3,2,1,0:T(8,128)(2,1)}, u32[]{:S(2)}) copy-start(bf16[1,1,18,128,128]{4,3,2,1,0:T(8,128)(2,1)} %param.12) | copy-start | bytes 1769476
  135.0 1.0 copy-start
  136.0 50.5 %all-to-all-start.3 = ((bf16[16,16,16,128]{3,2,1,0:T(8,128)(2,1)}), bf16[16,16,16,128]{3,2,1,0:T(8,128)(2,1)}, u32[]{:S(2)}, u32[]{:S(2)}) async-start(bf16[16,16,16,128]{3,2,1,0:T(8,128)(2,1)} %copy-done), calls=%async_computation.3 | async-start | bytes 2097152 | tf_op jit(solution)/shard_map/all_to_all | solution.py:199
  147.4 4.7 %collective-permute-start = (bf16[36,128,128]{2,1,0:T(8,128)(2,1)S(1)}, bf16[36,128,128]{2,1,0:T(8,128)(2,1)S(1)}, u32[]{:S(2)}, u32[]{:S(2)}) collective-permute-start(bf16[36,128,128]{2,1,0:T(8,128)(2,1)S(1)} %shard_map.115), channel_id=1, source_target_pairs={{0,256},{256,0},{1,257},{257,1},{2,258},{258,2},{3,259},{259,3},{4... | collective-permute-start | bytes 3538952 | tf_op jit(solution)/shard_map/ppermute | solution.py:228

commit v3 on v2

v3 whole, which is shorter than its diff:
```python
import functools

import jax
import jax.numpy as jnp
from jax import lax
from jax.experimental import pallas as pl
from jax.experimental.pallas import tpu as pltpu
from jax.sharding import PartitionSpec as P

BS = 128
FEATURE = 8
HIDDEN = 32
VMEM_BYTES = 12 * 1024 * 1024

VMEM = functools.partial(pl.BlockSpec, memory_space=pltpu.VMEM)
SMEM = functools.partial(pl.BlockSpec, memory_space=pltpu.SMEM)


def call(body, in_specs, out_shapes, scratch=(), flops=0, nbytes=0):
    return pl.pallas_call(
        body,
        in_specs=in_specs,
        out_specs=jax.tree.map(lambda _: VMEM(), out_shapes),
        out_shape=out_shapes,
        scratch_shapes=list(scratch),
        compiler_params=pltpu.CompilerParams(vmem_limit_bytes=VMEM_BYTES),
        cost_estimate=pl.CostEstimate(flops=flops, bytes_accessed=nbytes, transcendentals=0),
    )


def product_dims(transpose):
    return (((1,), (1,)), ((), ())) if transpose else (((1,), (0,)), ((), ()))


def slot_products(rows, first, second, first_coords, second_coords, first_count, second_count):
    peers, both, share, width = rows.shape
    slots = first.shape[0]

    def body(c1_ref, c2_ref, n1_ref, n2_ref, rows_ref, w1_ref, w2_ref, out_ref):
        lane = lax.broadcasted_iota(jnp.int32, (share, BS), 1)
        table = jnp.zeros((share, BS), jnp.int32)
        for s in range(slots):
            i = jnp.where(s < n1_ref[0, 0], c1_ref[1, s], HIDDEN)
            j = jnp.where(s < n2_ref[0, 0], c2_ref[0, s], HIDDEN)
            table = jnp.where(lane == s, i, jnp.where(lane == 64 + s, j, table))
        table = table.astype(jnp.float32).astype(jnp.bfloat16)
        for p in range(peers):
            out_ref[p, 2 * slots] = table
        for base, line, index_ref, blocks_ref in ((0, 0, c1_ref, w1_ref), (slots, 1, c2_ref, w2_ref)):
            for s in range(slots):
                start = pl.multiple_of(index_ref[line, s] * BS, BS)
                left = rows_ref[:, line, :, pl.ds(start, BS)].reshape(peers * share, BS)
                product = lax.dot_general(
                    left, blocks_ref[s], product_dims(line > 0), preferred_element_type=jnp.float32
                )
                out_ref[:, base + s] = product.astype(jnp.bfloat16).reshape(peers, share, BS)

    return call(
        body,
        [SMEM()] * 4 + [VMEM()] * 3,
        jax.ShapeDtypeStruct((peers, 2 * slots + 1, share, BS), jnp.bfloat16),
        flops=4 * slots * peers * share * BS * BS,
        nbytes=8 * slots * peers * share * BS,
    )(first_coords, second_coords, first_count, second_count, rows, first, second)


def hidden_step(parts):
    peers, width = parts.shape[0], parts.shape[3]
    slots = parts.shape[1] // 2
    share = parts.shape[2]
    hidden_blocks = HIDDEN

    def body(parts_ref, out_ref, pre, grad, act_blocks, grad_blocks, table, index, sem):
        row = lax.broadcasted_iota(jnp.int32, (peers, width), 0)
        lines = jnp.zeros((peers, width), jnp.float32)
        for p in range(peers):
            lines = jnp.where(row == p, parts_ref[p, 2 * slots].astype(jnp.float32), lines)
        table[...] = lines.astype(jnp.int32)
        copy = pltpu.make_async_copy(table, index, sem)
        copy.start()
        pre[...] = jnp.zeros_like(pre)
        grad[...] = jnp.zeros_like(grad)
        act_blocks[hidden_blocks:] = jnp.zeros((1, share, width), jnp.bfloat16)
        grad_blocks[hidden_blocks:] = jnp.zeros((1, share, width), jnp.bfloat16)
        copy.wait()

        def add(p, carry):
            for s in range(slots):
                i, j = index[p, s], index[p, 64 + s]
                pre[i] = pre[i] + parts_ref[p, s].astype(jnp.float32)
                grad[j] = grad[j] + parts_ref[p, slots + s].astype(jnp.float32)
            return carry

        lax.fori_loop(0, peers, add, 0)

        def point(h, carry):
            value = pre[h]
            gate = 1.0 / (1.0 + jnp.exp(-value))
            act_blocks[h] = (value * gate).astype(jnp.bfloat16)
            grad_blocks[h] = (grad[h] * gate * (1.0 + value * (1.0 - gate))).astype(jnp.bfloat16)
            return carry

        lax.fori_loop(0, hidden_blocks, point, 0, unroll=8)

        def pick(p, carry):
            for s in range(slots):
                out_ref[p, s] = act_blocks[index[p, 64 + s]]
                out_ref[p, slots + s] = grad_blocks[index[p, s]]
            return carry

        lax.fori_loop(0, peers, pick, 0)

    return call(
        body,
        [VMEM()],
        jax.ShapeDtypeStruct((peers, 2 * slots, share, width), jnp.bfloat16),
        scratch=[
            pltpu.VMEM((hidden_blocks + 1, share, width), jnp.float32),
            pltpu.VMEM((hidden_blocks + 1, share, width), jnp.float32),
            pltpu.VMEM((hidden_blocks + 1, share, width), jnp.bfloat16),
            pltpu.VMEM((hidden_blocks + 1, share, width), jnp.bfloat16),
            pltpu.VMEM((peers, width), jnp.int32),
            pltpu.SMEM((peers, width), jnp.int32),
            pltpu.SemaphoreType.DMA,
        ],
        flops=4 * parts.size,
        nbytes=6 * parts.size,
    )(parts)


def feature_sums(slots_in, first, second, first_coords, second_coords):
    peers, both, share, width = slots_in.shape
    slots = both // 2

    def body(c1_ref, c2_ref, in_ref, w1_ref, w2_ref, out_ref, total):
        for base, line, index_ref, blocks_ref in ((0, 1, c2_ref, w2_ref), (slots, 0, c1_ref, w1_ref)):
            total[...] = jnp.zeros_like(total)
            for s in range(slots):
                left = in_ref[:, base + s].reshape(peers * share, width)
                product = lax.dot_general(
                    left, blocks_ref[s], product_dims(base > 0), preferred_element_type=jnp.float32
                )
                target = index_ref[line, s]
                total[target] = total[target] + product
            place = FEATURE if base else 0
            for k in range(FEATURE):
                out_ref[:, place + k] = total[k].astype(jnp.bfloat16).reshape(peers, share, width)

    return call(
        body,
        [SMEM()] * 2 + [VMEM()] * 3,
        jax.ShapeDtypeStruct((peers, 2 * FEATURE, share, width), jnp.bfloat16),
        scratch=[pltpu.VMEM((FEATURE, peers * share, width), jnp.float32)],
        flops=2 * slots_in.size * BS,
        nbytes=4 * slots_in.size,
    )(first_coords, second_coords, slots_in, first, second)


def block_grads(rows, slots_in, first_coords, second_coords):
    peers, both, share, width = slots_in.shape
    slots = both // 2
    dims = (((0,), (0,)), ((), ()))

    def body(c1_ref, c2_ref, rows_ref, in_ref, out_ref):
        for s in range(slots):
            start = pl.multiple_of(c1_ref[0, s] * BS, BS)
            feature = rows_ref[:, 0, :, pl.ds(start, BS)].reshape(peers * share, BS)
            hidden = in_ref[:, slots + s].reshape(peers * share, width)
            grad = lax.dot_general(feature, hidden, dims, preferred_element_type=jnp.float32)
            out_ref[s] = grad.astype(jnp.bfloat16)
        for s in range(slots):
            start = pl.multiple_of(c2_ref[1, s] * BS, BS)
            feature = rows_ref[:, 1, :, pl.ds(start, BS)].reshape(peers * share, BS)
            hidden = in_ref[:, s].reshape(peers * share, width)
            grad = lax.dot_general(hidden, feature, dims, preferred_element_type=jnp.float32)
            out_ref[slots + s] = grad.astype(jnp.bfloat16)

    return call(
        body,
        [SMEM()] * 2 + [VMEM()] * 2,
        jax.ShapeDtypeStruct((both, BS, BS), jnp.bfloat16),
        flops=2 * slots_in.size * BS,
        nbytes=4 * slots_in.size,
    )(first_coords, second_coords, rows, slots_in)


def final_sums(parts, grads, others):
    peers, both, share, width = parts.shape
    slots = grads.shape[0] // 2

    def body(parts_ref, grads_ref, others_ref, out_ref, in_ref, w1_ref, w2_ref):
        for s in range(2 * slots):
            total = grads_ref[s].astype(jnp.float32) + others_ref[s].astype(jnp.float32)
            target = w1_ref if s < slots else w2_ref
            target[0, 0, s % slots] = total.astype(jnp.bfloat16)
        for k in range(both):
            total = parts_ref[0, k].astype(jnp.float32)
            for c in range(1, peers):
                total = total + parts_ref[c, k].astype(jnp.float32)
            target, place = (out_ref, k) if k < FEATURE else (in_ref, k - FEATURE)
            target[:, place * width : (place + 1) * width] = total.astype(jnp.bfloat16)

    row = jax.ShapeDtypeStruct((share, FEATURE * width), jnp.bfloat16)
    grad = jax.ShapeDtypeStruct((1, 1, slots, BS, BS), jnp.bfloat16)
    return call(
        body, [VMEM()] * 3, (row, row, grad, grad), flops=parts.size, nbytes=2 * parts.size
    )(parts, grads, others)


def swap(parts, axis):
    return lax.all_to_all(parts, axis, split_axis=0, concat_axis=0, tiled=True)


def on_device(tokens, w1_blocks, w1_coords, w1_count, w2_blocks, w2_coords, w2_count, cotangent):
    first, second = w1_blocks[0, 0], w2_blocks[0, 0]
    first_coords, second_coords = w1_coords[0, 0].T, w2_coords[0, 0].T
    peers = lax.axis_size("col")
    rows = jnp.stack([tokens, cotangent])
    rows = swap(jnp.broadcast_to(rows[None], (peers,) + rows.shape), "col")
    parts = swap(
        slot_products(rows, first, second, first_coords, second_coords, w1_count, w2_count), "row"
    )
    slots_in = swap(hidden_step(parts), "row")
    grads = block_grads(rows, slots_in, first_coords, second_coords)
    grads, slots_in = lax.optimization_barrier((grads, slots_in))
    others = lax.ppermute(grads, "tok", [(0, 1), (1, 0)])
    sums = swap(feature_sums(slots_in, first, second, first_coords, second_coords), "col")
    return final_sums(sums, grads, others)


def solution(mesh):
    placed = (
        P(("tok", "col"), "row"),
        P("row", "col", None, None, None),
        P("row", "col", None, None),
        P("row", "col"),
        P("row", "col", None, None, None),
        P("row", "col", None, None),
        P("row", "col"),
        P(("tok", "col"), "row"),
    )
    return jax.shard_map(
        on_device,
        mesh=mesh,
        in_specs=placed,
        out_specs=(
            P(("tok", "col"), "row"),
            P(("tok", "col"), "row"),
            P("row", "col", None, None, None),
            P("row", "col", None, None, None),
        ),
        check_vma=False,
    )
```

time: 189 us -> 205 us (1.085)
  waiting for transfers between devices: 35.5 us -> 92.8 us
  blocking collectives: 109 us -> 62.8 us
  starting transfers between devices: 26.6 us -> 34.5 us
  local copies, waits for them, and re-layouts: 4.51 us -> 1.11 us
    all_to_all x2, waiting for transfers between devices: 32.7 us -> 90 us  [swap(): return lax.all_to_all(parts, axis, split_axis=0, concat_axis=0, tiled=True)]
    all_gather x1 -> x0, blocking collectives: 47.5 us -> none  [on_device(): lax.all_gather(tokens, 'col', axis=0, tiled=True).reshape(cotan_rows.shape)]
    all_to_all x2, starting transfers between devices: 24.7 us -> 32.6 us  [swap(): return lax.all_to_all(parts, axis, split_axis=0, concat_axis=0, tiled=True)]
  transfers between devices with their start and end apart: 3 -> 3, of which waited for: 2 -> 3; matrix products, arithmetic and copies ran while one was open for 2% -> 0% of each run, Pallas kernels for 1% -> 0%
where the time goes in v3:
time: 205 us; the launch traced here: 204 us
  waiting for transfers between devices  92.8 us (45%)
  blocking collectives  62.8 us (31%)
  starting transfers between devices  34.5 us (17%)
  Pallas kernels  10 us (5%)
    all_to_all x2, waiting for transfers between devices, swap(): return lax.all_to_all(parts, axis, split_axis=0, concat_axis=0, tiled=True)  90 us
    all_to_all x2, blocking collectives, swap(): return lax.all_to_all(parts, axis, split_axis=0, concat_axis=0, tiled=True)  62.8 us
    all_to_all x2, starting transfers between devices, swap(): return lax.all_to_all(parts, axis, split_axis=0, concat_axis=0, tiled=True)  32.6 us
  transfers between devices with their start and end apart: 3, of which 3 were waited for; matrix products, arithmetic and copies ran while one was open for 0% of the time, Pallas kernels for 0%

profile of v3, /device:TPU:64, one launch (start us, length us, event | category | flops | bytes accessed | tf_op | source)
XLA Modules:
  0.0 204.2 jit_solution(2070163203416005124)
XLA Ops:
  0.6 0.0 copy-start.3
  0.6 0.0 copy-start.1
  0.7 0.0 copy-start.2
  0.7 0.0 copy-start
  0.7 0.9 pad_maximum_fusion
  1.5 1.1 broadcast_in_dim.2
  2.6 14.8 %all-to-all-start = ((bf16[16,2,16,1024]{3,2,1,0:T(8,128)(2,1)}), bf16[16,2,16,1024]{3,2,1,0:T(8,128)(2,1)S(1)}, u32[]{:S(2)}, u32[]{:S(2)}) async-start(bf16[16,2,16,1024]{3,2,1,0:T(8,128)(2,1)} %broadcast_in_dim.2), calls=%async_computation | async-start | bytes 2097152 | tf_op jit(solution)/shard_map/all_to_all | solution.py:211
  18.7 48.3 %all-to-all-done.rows_ref = bf16[16,2,16,1024]{3,2,1,0:T(8,128)(2,1)S(1)} async-done(((bf16[16,2,16,1024]{3,2,1,0:T(8,128)(2,1)}), bf16[16,2,16,1024]{3,2,1,0:T(8,128)(2,1)S(1)}, u32[]{:S(2)}, u32[]{:S(2)}) %all-to-all-start) | async-done | bytes 1048608 | tf_op jit(solution)/shard_map/all_to_all | solution.py:211
  67.0 0.0 copy-done.3
  67.0 0.0 copy-done.1
  67.0 0.0 copy-done.2
  67.0 0.0 copy-done
  67.0 1.4 shard_map.111
  68.4 34.0 %all_to_all.20.parts_ref = bf16[16,37,16,128]{3,2,1,0:T(8,128)(2,1)S(1)} all-to-all(bf16[16,37,16,128]{3,2,1,0:T(8,128)(2,1)S(1)} %shard_map.111), channel_id=1, replica_groups=mesh['tok'=2,'row'=16,'col'=16] {'row'}, dimensions={0} | all-to-all | bytes 4849664 | tf_op jit(solution)/shard_map/all_to_all | solution.py:211
  102.5 3.2 %shard_map.112 = bf16[16,36,16,128]{3,2,1,0:T(8,128)(2,1)S(1)} custom-call(bf16[16,37,16,128]{3,2,1,0:T(8,128)(2,1)S(1)} %all_to_all.20.parts_ref), custom_call_target="tpu_custom_call" | custom-call | flops 4849664 | bytes 7274496 | tf_op jit(solution)/shard_map/pallas_call | solution.py:113
  105.6 28.8 %all_to_all.21.in_ref = bf16[16,36,16,128]{3,2,1,0:T(8,128)(2,1)S(1)} all-to-all(bf16[16,36,16,128]{3,2,1,0:T(8,128)(2,1)S(1)} %shard_map.112), channel_id=1, replica_groups=mesh['tok'=2,'row'=16,'col'=16] {'row'}, dimensions={0} | all-to-all | bytes 4718592 | tf_op jit(solution)/shard_map/all_to_all | solution.py:211
  134.5 1.5 shard_map.113.grads_ref
  136.0 2.6 %shard_map.114 = bf16[16,16,16,128]{3,2,1,0:T(8,128)(2,1)} custom-call(s32[2,18]{1,0:T(2,128)S(1)} %bitcast.16, s32[2,18]{1,0:T(2,128)S(1)} %bitcast.19, bf16[16,36,16,128]{3,2,1,0:T(8,128)(2,1)S(1)} %all_to_all.21.in_ref, bf16[18,128,128]{2,1,0:T(8,128)(2,1)S(1)} %bitcast.11, bf16[18,128,128]{2,1,0:T(8,128)(2,1)S(1)} %bitcast.13), custom_call_target="tpu_custom_call" | custom-call | flops 301989888 | bytes 4718592 | tf_op jit(solution)/shard_map/pallas_call | solution.py:149
  138.6 17.9 %all-to-all-start.3 = ((bf16[16,16,16,128]{3,2,1,0:T(8,128)(2,1)}), bf16[16,16,16,128]{3,2,1,0:T(8,128)(2,1)S(1)}, u32[]{:S(2)}, u32[]{:S(2)}) async-start(bf16[16,16,16,128]{3,2,1,0:T(8,128)(2,1)} %shard_map.114), calls=%async_computation.3 | async-start | bytes 2097152 | tf_op jit(solution)/shard_map/all_to_all | solution.py:211
  156.5 1.9 collective-permute-start
  158.4 2.8 %collective-permute-done.others_ref = bf16[36,128,128]{2,1,0:T(8,128)(2,1)S(1)} collective-permute-done((bf16[36,128,128]{2,1,0:T(8,128)(2,1)S(1)}, bf16[36,128,128]{2,1,0:T(8,128)(2,1)S(1)}, u32[]{:S(2)}, u32[]{:S(2)}) %collective-permute-start) | collective-permute-done | bytes 1179680 | tf_op jit(solution)/shard_map/ppermute | solution.py:226
  161.2 41.7 %all-to-all-done.3.parts_ref = bf16[16,16,16,128]{3,2,1,0:T(8,128)(2,1)S(1)} async-done(((bf16[16,16,16,128]{3,2,1,0:T(8,128)(2,1)}), bf16[16,16,16,128]{3,2,1,0:T(8,128)(2,1)S(1)}, u32[]{:S(2)}, u32[]{:S(2)}) %all-to-all-start.3) | async-done | bytes 1048608 | tf_op jit(solution)/shard_map/all_to_all | solution.py:211
  202.9 1.3 shard_map.115
Async XLA Ops:
  0.6 66.4 %copy-start.3 = (s32[1,1,18,2]{2,3,1,0:T(2,128)S(1)}, s32[1,1,18,2]{2,3,1,0:T(2,128)}, u32[]{:S(2)}) copy-start(s32[1,1,18,2]{2,3,1,0:T(2,128)} %param.13) | copy-start | bytes 436
  0.6 66.4 %copy-start.1 = (bf16[1,1,18,128,128]{4,3,2,1,0:T(8,128)(2,1)S(1)}, bf16[1,1,18,128,128]{4,3,2,1,0:T(8,128)(2,1)}, u32[]{:S(2)}) copy-start(bf16[1,1,18,128,128]{4,3,2,1,0:T(8,128)(2,1)} %param.12) | copy-start | bytes 1769476
  0.7 66.4 %copy-start.2 = (s32[1,1,18,2]{2,3,1,0:T(2,128)S(1)}, s32[1,1,18,2]{2,3,1,0:T(2,128)}, u32[]{:S(2)}) copy-start(s32[1,1,18,2]{2,3,1,0:T(2,128)} %param.10) | copy-start | bytes 436
  0.7 66.4 %copy-start = (bf16[1,1,18,128,128]{4,3,2,1,0:T(8,128)(2,1)S(1)}, bf16[1,1,18,128,128]{4,3,2,1,0:T(8,128)(2,1)}, u32[]{:S(2)}) copy-start(bf16[1,1,18,128,128]{4,3,2,1,0:T(8,128)(2,1)} %param.9) | copy-start | bytes 1769476
  2.6 64.4 %all-to-all-start = ((bf16[16,2,16,1024]{3,2,1,0:T(8,128)(2,1)}), bf16[16,2,16,1024]{3,2,1,0:T(8,128)(2,1)S(1)}, u32[]{:S(2)}, u32[]{:S(2)}) async-start(bf16[16,2,16,1024]{3,2,1,0:T(8,128)(2,1)} %broadcast_in_dim.2), calls=%async_computation | async-start | bytes 2097152 | tf_op jit(solution)/shard_map/all_to_all | solution.py:211
  138.6 64.3 %all-to-all-start.3 = ((bf16[16,16,16,128]{3,2,1,0:T(8,128)(2,1)}), bf16[16,16,16,128]{3,2,1,0:T(8,128)(2,1)S(1)}, u32[]{:S(2)}, u32[]{:S(2)}) async-start(bf16[16,16,16,128]{3,2,1,0:T(8,128)(2,1)} %shard_map.114), calls=%async_computation.3 | async-start | bytes 2097152 | tf_op jit(solution)/shard_map/all_to_all | solution.py:211
  156.5 4.7 %collective-permute-start = (bf16[36,128,128]{2,1,0:T(8,128)(2,1)S(1)}, bf16[36,128,128]{2,1,0:T(8,128)(2,1)S(1)}, u32[]{:S(2)}, u32[]{:S(2)}) collective-permute-start(bf16[36,128,128]{2,1,0:T(8,128)(2,1)S(1)} %shard_map.113.grads_ref), channel_id=1, source_target_pairs={{0,256},{256,0},{1,257},{257,1},{2,258},{258,2},{3,259},{259,3},{4... | collective-permute-start | bytes 3538952 | tf_op jit(solution)/shard_map/ppermute | solution.py:226

commit v4 on v3

--- a/solution.py
+++ b/solution.py
@@ -10,6 +10,7 @@
 BS = 128
 FEATURE = 8
 HIDDEN = 32
+NEAR = 4
 VMEM_BYTES = 12 * 1024 * 1024
 
 VMEM = functools.partial(pl.BlockSpec, memory_space=pltpu.VMEM)
@@ -32,11 +33,19 @@
     return (((1,), (1,)), ((), ())) if transpose else (((1,), (0,)), ((), ()))
 
 
+def block_column(rows_refs, line, index):
+    start = pl.multiple_of(index * BS, BS)
+    parts = [ref[:, line, :, pl.ds(start, BS)] for ref in rows_refs]
+    return jnp.concatenate(parts, axis=0).reshape(-1, BS)
+
+
 def slot_products(rows, first, second, first_coords, second_coords, first_count, second_count):
-    peers, both, share, width = rows.shape
+    group, both, share, width = rows[0].shape
+    peers = group * len(rows)
     slots = first.shape[0]
 
-    def body(c1_ref, c2_ref, n1_ref, n2_ref, rows_ref, w1_ref, w2_ref, out_ref):
+    def body(c1_ref, c2_ref, n1_ref, n2_ref, *refs):
+        rows_refs, (w1_ref, w2_ref, out_ref) = refs[: len(rows)], refs[len(rows) :]
         lane = lax.broadcasted_iota(jnp.int32, (share, BS), 1)
         table = jnp.zeros((share, BS), jnp.int32)
         for s in range(slots):
@@ -48,8 +57,7 @@
             out_ref[p, 2 * slots] = table
         for base, line, index_ref, blocks_ref in ((0, 0, c1_ref, w1_ref), (slots, 1, c2_ref, w2_ref)):
             for s in range(slots):
-                start = pl.multiple_of(index_ref[line, s] * BS, BS)
-                left = rows_ref[:, line, :, pl.ds(start, BS)].reshape(peers * share, BS)
+                left = block_column(rows_refs, line, index_ref[line, s])
                 product = lax.dot_general(
                     left, blocks_ref[s], product_dims(line > 0), preferred_element_type=jnp.float32
                 )
@@ -57,11 +65,11 @@
 
     return call(
         body,
-        [SMEM()] * 4 + [VMEM()] * 3,
+        [SMEM()] * 4 + [VMEM()] * (len(rows) + 2),
         jax.ShapeDtypeStruct((peers, 2 * slots + 1, share, BS), jnp.bfloat16),
         flops=4 * slots * peers * share * BS * BS,
         nbytes=8 * slots * peers * share * BS,
-    )(first_coords, second_coords, first_count, second_count, rows, first, second)
+    )(first_coords, second_coords, first_count, second_count, *rows, first, second)
 
 
 def hidden_step(parts):
@@ -131,8 +139,10 @@
 def feature_sums(slots_in, first, second, first_coords, second_coords):
     peers, both, share, width = slots_in.shape
     slots = both // 2
-
-    def body(c1_ref, c2_ref, in_ref, w1_ref, w2_ref, out_ref, total):
+    group = peers // NEAR
+
+    def body(c1_ref, c2_ref, in_ref, w1_ref, w2_ref, *refs):
+        out_refs, total = refs[:NEAR], refs[NEAR]
         for base, line, index_ref, blocks_ref in ((0, 1, c2_ref, w2_ref), (slots, 0, c1_ref, w1_ref)):
             total[...] = jnp.zeros_like(total)
             for s in range(slots):
@@ -144,12 +154,14 @@
                 total[target] = total[target] + product
             place = FEATURE if base else 0
             for k in range(FEATURE):
-                out_ref[:, place + k] = total[k].astype(jnp.bfloat16).reshape(peers, share, width)
+                value = total[k].astype(jnp.bfloat16).reshape(NEAR, group, share, width)
+                for n in range(NEAR):
+                    out_refs[n][:, place + k] = value[n]
 
     return call(
         body,
         [SMEM()] * 2 + [VMEM()] * 3,
-        jax.ShapeDtypeStruct((peers, 2 * FEATURE, share, width), jnp.bfloat16),
+        (jax.ShapeDtypeStruct((group, 2 * FEATURE, share, width), jnp.bfloat16),) * NEAR,
         scratch=[pltpu.VMEM((FEATURE, peers * share, width), jnp.float32)],
         flops=2 * slots_in.size * BS,
         nbytes=4 * slots_in.size,
@@ -161,70 +173,111 @@
     slots = both // 2
     dims = (((0,), (0,)), ((), ()))
 
-    def body(c1_ref, c2_ref, rows_ref, in_ref, out_ref):
+    def body(c1_ref, c2_ref, *refs):
+        rows_refs, (in_ref, out_ref) = refs[: len(rows)], refs[len(rows) :]
         for s in range(slots):
-            start = pl.multiple_of(c1_ref[0, s] * BS, BS)
-            feature = rows_ref[:, 0, :, pl.ds(start, BS)].reshape(peers * share, BS)
+            feature = block_column(rows_refs, 0, c1_ref[0, s])
             hidden = in_ref[:, slots + s].reshape(peers * share, width)
             grad = lax.dot_general(feature, hidden, dims, preferred_element_type=jnp.float32)
             out_ref[s] = grad.astype(jnp.bfloat16)
         for s in range(slots):
-            start = pl.multiple_of(c2_ref[1, s] * BS, BS)
-            feature = rows_ref[:, 1, :, pl.ds(start, BS)].reshape(peers * share, BS)
+            feature = block_column(rows_refs, 1, c2_ref[1, s])
             hidden = in_ref[:, s].reshape(peers * share, width)
             grad = lax.dot_general(hidden, feature, dims, preferred_element_type=jnp.float32)
             out_ref[slots + s] = grad.astype(jnp.bfloat16)
 
     return call(
         body,
-        [SMEM()] * 2 + [VMEM()] * 2,
+        [SMEM()] * 2 + [VMEM()] * (len(rows) + 1),
         jax.ShapeDtypeStruct((both, BS, BS), jnp.bfloat16),
         flops=2 * slots_in.size * BS,
         nbytes=4 * slots_in.size,
-    )(first_coords, second_coords, rows, slots_in)
+    )(first_coords, second_coords, *rows, slots_in)
+
+
+def near_sums(parts, far_place):
+    group, blocks, share, width = parts[0].shape
+
+    def body(place_ref, *refs):
+        part_refs, out_refs = refs[:NEAR], refs[NEAR:]
+        for step in range(group):
+            k = lax.rem(place_ref[0] + step, group)
+
+            def add(b, carry):
+                total = part_refs[0][k, b].astype(jnp.float32)
+                for ref in part_refs[1:]:
+                    total = total + ref[k, b].astype(jnp.float32)
+                out_refs[step][b] = total.astype(jnp.bfloat16)
+                return carry
+
+            lax.fori_loop(0, blocks, add, 0, unroll=True)
+
+    return call(
+        body,
+        [SMEM()] + [VMEM()] * NEAR,
+        (jax.ShapeDtypeStruct((blocks, share, width), jnp.bfloat16),) * group,
+        flops=4 * parts[0].size,
+        nbytes=8 * parts[0].size,
+    )(far_place, *parts)
 
 
 def final_sums(parts, grads, others):
-    peers, both, share, width = parts.shape
+    both, share, width = parts[0].shape
     slots = grads.shape[0] // 2
 
-    def body(parts_ref, grads_ref, others_ref, out_ref, in_ref, w1_ref, w2_ref):
+    def body(*refs):
+        part_refs, refs = refs[: len(parts)], refs[len(parts) :]
+        grads_ref, others_ref, out_ref, in_ref, w1_ref, w2_ref = refs
         for s in range(2 * slots):
             total = grads_ref[s].astype(jnp.float32) + others_ref[s].astype(jnp.float32)
             target = w1_ref if s < slots else w2_ref
             target[0, 0, s % slots] = total.astype(jnp.bfloat16)
         for k in range(both):
-            total = parts_ref[0, k].astype(jnp.float32)
-            for c in range(1, peers):
-                total = total + parts_ref[c, k].astype(jnp.float32)
+            total = part_refs[0][k].astype(jnp.float32)
+            for ref in part_refs[1:]:
+                total = total + ref[k].astype(jnp.float32)
             target, place = (out_ref, k) if k < FEATURE else (in_ref, k - FEATURE)
             target[:, place * width : (place + 1) * width] = total.astype(jnp.bfloat16)
 
     row = jax.ShapeDtypeStruct((share, FEATURE * width), jnp.bfloat16)
     grad = jax.ShapeDtypeStruct((1, 1, slots, BS, BS), jnp.bfloat16)
     return call(
-        body, [VMEM()] * 3, (row, row, grad, grad), flops=parts.size, nbytes=2 * parts.size
-    )(parts, grads, others)
+        body,
+        [VMEM()] * (len(parts) + 2),
+        (row, row, grad, grad),
+        flops=grads.size,
+        nbytes=6 * grads.size,
+    )(*parts, grads, others)
 
 
 def swap(parts, axis):
     return lax.all_to_all(parts, axis, split_axis=0, concat_axis=0, tiled=True)
+
+
+def send_on(value, hops):
+    peers = lax.axis_size("col")
+    return lax.ppermute(value, "col", [(c, (c + hops) % peers) for c in range(peers)])
 
 
 def on_device(tokens, w1_blocks, w1_coords, w1_count, w2_blocks, w2_coords, w2_count, cotangent):
     first, second = w1_blocks[0, 0], w2_blocks[0, 0]
     first_coords, second_coords = w1_coords[0, 0].T, w2_coords[0, 0].T
     peers = lax.axis_size("col")
-    rows = jnp.stack([tokens, cotangent])
-    rows = swap(jnp.broadcast_to(rows[None], (peers,) + rows.shape), "col")
+    far = [[c + NEAR * k for k in range(peers // NEAR)] for c in range(NEAR)]
+    steps = (0, 1, -1, 2)
+
+    own = lax.all_gather(jnp.stack([tokens, cotangent]), "col", axis_index_groups=far)
+    rows = [own] + [send_on(own, -step) for step in steps[1:]]
     parts = swap(
         slot_products(rows, first, second, first_coords, second_coords, w1_count, w2_count), "row"
     )
     slots_in = swap(hidden_step(parts), "row")
+    sums = feature_sums(slots_in, first, second, first_coords, second_coords)
+    sums = [sums[0]] + [send_on(part, step) for part, step in zip(sums[1:], steps[1:])]
     grads = block_grads(rows, slots_in, first_coords, second_coords)
-    grads, slots_in = lax.optimization_barrier((grads, slots_in))
     others = lax.ppermute(grads, "tok", [(0, 1), (1, 0)])
-    sums = swap(feature_sums(slots_in, first, second, first_coords, second_coords), "col")
+    sums = near_sums(sums, lax.div(lax.axis_index("col"), NEAR).reshape(1))
+    sums = [sums[0]] + [send_on(sums[k], NEAR * k) for k in range(1, peers // NEAR)]
     return final_sums(sums, grads, others)
 
 

time: 205 us -> 184 us (0.90)
  the two profiles are of different devices: /device:TPU:64 before, /device:TPU:1 now
where the time goes in v4:
time: 184 us; the launch traced here: 183 us
  blocking collectives  92 us (50%)
  starting transfers between devices  39.2 us (21%)
  waiting for transfers between devices  35.8 us (19%)
  Pallas kernels  9.9 us (5%)
  local copies, waits for them, and re-layouts  3.5 us (2%)
  between operations  2.1 us (1%)
    all_to_all x2, blocking collectives, swap(): return lax.all_to_all(parts, axis, split_axis=0, concat_axis=0, tiled=True)  66.7 us
    ppermute x9, waiting for transfers between devices, send_on(): lax.ppermute(value, 'col', [(c, (c + hops) % peers) for c in range(peers)])  35.8 us
    ppermute x9, starting transfers between devices, send_on(): lax.ppermute(value, 'col', [(c, (c + hops) % peers) for c in range(peers)])  32.7 us
    all_gather x1, blocking collectives, on_device(): lax.all_gather(jnp.stack([tokens, cotangent]), 'col', axis_index_groups=far)  25.2 us
    ppermute x1, starting transfers between devices, on_device(): others = lax.ppermute(grads, 'tok', [(0, 1), (1, 0)])  6.54 us
  transfers between devices with their start and end apart: 10, of which 7 were waited for; matrix products, arithmetic and copies ran while one was open for 0% of the time, Pallas kernels for 1%

profile of v4, /device:TPU:1, one launch (start us, length us, event | category | flops | bytes accessed | tf_op | source)
XLA Modules:
  0.0 183.3 jit_solution(611526750403344406)
XLA Ops:
  0.6 0.8 pad_maximum_fusion
  1.4 25.2 %all-gather = bf16[8,16,1024]{2,1,0:T(8,128)(2,1)S(1)} all-gather(bf16[2,16,1024]{2,1,0:T(8,128)(2,1)S(1)} %pad_maximum_fusion), channel_id=2, replica_groups={{0,4,8,12},{1,5,9,13},{2,6,10,14},{3,7,11,15},{16,20,24,28},{17,21,25,2..., dimensions={0}, use_global_device_ids=true | all-gather | bytes 327680 | tf_op jit(solution)/shard_map/all_gather | solution.py:269
  26.7 3.3 %collective-permute-start = (bf16[4,2,16,1024]{3,2,1,0:T(8,128)(2,1)S(1)}, bf16[4,2,16,1024]{3,2,1,0:T(8,128)(2,1)S(1)}, u32[]{:S(2)}, u32[]{:S(2)}) collective-permute-start(bf16[4,2,16,1024]{3,2,1,0:T(8,128)(2,1)S(1)} %bitcast.16), channel_id=1, source_target_pairs={{0,15},{1,0},{2,1},{3,2},{4,3},{5,4},{6,5},{7,6},{8,7},{9,8},{10,9... | collective-permute-start | bytes 786440 | tf_op jit(solution)/shard_map/ppermute | solution.py:259
  30.0 2.0 %collective-permute-start.1 = (bf16[4,2,16,1024]{3,2,1,0:T(8,128)(2,1)S(1)}, bf16[4,2,16,1024]{3,2,1,0:T(8,128)(2,1)S(1)}, u32[]{:S(2)}, u32[]{:S(2)}) collective-permute-start(bf16[4,2,16,1024]{3,2,1,0:T(8,128)(2,1)S(1)} %bitcast.17), channel_id=1, source_target_pairs={{0,1},{1,2},{2,3},{3,4},{4,5},{5,6},{6,7},{7,8},{8,9},{9,10},{10,1... | collective-permute-start | bytes 786440 | tf_op jit(solution)/shard_map/ppermute | solution.py:259
  31.9 3.0 %collective-permute-start.2 = (bf16[4,2,16,1024]{3,2,1,0:T(8,128)(2,1)S(1)}, bf16[4,2,16,1024]{3,2,1,0:T(8,128)(2,1)S(1)}, u32[]{:S(2)}, u32[]{:S(2)}) collective-permute-start(bf16[4,2,16,1024]{3,2,1,0:T(8,128)(2,1)S(1)} %bitcast.18), channel_id=1, source_target_pairs={{0,14},{1,15},{2,0},{3,1},{4,2},{5,3},{6,4},{7,5},{8,6},{9,7},{10,... | collective-permute-start | bytes 786440 | tf_op jit(solution)/shard_map/ppermute | solution.py:259
  36.3 0.0 collective-permute-done.refs_1_
  36.3 2.0 %collective-permute-done.1.refs_2_ = bf16[4,2,16,1024]{3,2,1,0:T(8,128)(2,1)S(1)} collective-permute-done((bf16[4,2,16,1024]{3,2,1,0:T(8,128)(2,1)S(1)}, bf16[4,2,16,1024]{3,2,1,0:T(8,128)(2,1)S(1)}, u32[]{:S(2)}, u32[]{:S(2)}) %collective-permute-start.1) | collective-permute-done | bytes 262176 | tf_op jit(solution)/shard_map/ppermute | solution.py:259
  38.3 9.7 %collective-permute-done.2.refs_3_ = bf16[4,2,16,1024]{3,2,1,0:T(8,128)(2,1)S(1)} collective-permute-done((bf16[4,2,16,1024]{3,2,1,0:T(8,128)(2,1)S(1)}, bf16[4,2,16,1024]{3,2,1,0:T(8,128)(2,1)S(1)}, u32[]{:S(2)}, u32[]{:S(2)}) %collective-permute-start.2) | collective-permute-done | bytes 262176 | tf_op jit(solution)/shard_map/ppermute | solution.py:259
  48.0 0.0 copy-start
  48.0 1.1 copy-done
  49.1 0.0 copy-start.2
  49.1 1.1 copy-done.2
  50.2 0.0 copy-start.4
  50.2 0.7 copy-done.4
  50.8 0.0 copy-start.6
  50.8 0.7 copy-done.6
  51.5 1.4 shard_map.111
  52.9 35.5 %all_to_all.10.parts_ref = bf16[16,37,16,128]{3,2,1,0:T(8,128)(2,1)S(1)} all-to-all(bf16[16,37,16,128]{3,2,1,0:T(8,128)(2,1)S(1)} %shard_map.111), channel_id=1, replica_groups=mesh['tok'=2,'row'=16,'col'=16] {'row'}, dimensions={0} | all-to-all | bytes 4849664 | tf_op jit(solution)/shard_map/all_to_all | solution.py:254
  88.4 3.2 %shard_map.112 = bf16[16,36,16,128]{3,2,1,0:T(8,128)(2,1)S(1)} custom-call(bf16[16,37,16,128]{3,2,1,0:T(8,128)(2,1)S(1)} %all_to_all.10.parts_ref), custom_call_target="tpu_custom_call" | custom-call | flops 4849664 | bytes 7274496 | tf_op jit(solution)/shard_map/pallas_call | solution.py:121
  91.6 0.0 copy-start.5
  91.6 0.0 copy-start.7
  91.6 31.2 %all_to_all.11.in_ref.refs_4_ = bf16[16,36,16,128]{3,2,1,0:T(8,128)(2,1)S(1)} all-to-all(bf16[16,36,16,128]{3,2,1,0:T(8,128)(2,1)S(1)} %shard_map.112), channel_id=1, replica_groups=mesh['tok'=2,'row'=16,'col'=16] {'row'}, dimensions={0} | all-to-all | bytes 4718592 | tf_op jit(solution)/shard_map/all_to_all | solution.py:254
  122.9 0.0 copy-done.5
  122.9 0.0 copy-done.7
  122.9 0.0 copy-start.1
  122.9 0.0 copy-start.3
  122.9 1.5 shard_map.115.refs_4_
  124.4 6.5 %collective-permute-start.9 = (bf16[36,128,128]{2,1,0:T(8,128)(2,1)S(1)}, bf16[36,128,128]{2,1,0:T(8,128)(2,1)S(1)}, u32[]{:S(2)}, u32[]{:S(2)}) collective-permute-start(bf16[36,128,128]{2,1,0:T(8,128)(2,1)S(1)} %shard_map.115.refs_4_), channel_id=1, source_target_pairs={{0,256},{256,0},{1,257},{257,1},{2,258},{258,2},{3,259},{259,3},{4... | collective-permute-start | bytes 3538952 | tf_op jit(solution)/shard_map/ppermute | solution.py:278
  130.9 0.0 copy-done.1
  130.9 0.0 copy-done.3
  130.9 2.4 %shard_map.113 = (bf16[4,16,16,128]{3,2,1,0:T(8,128)(2,1)S(1)}, bf16[4,16,16,128]{3,2,1,0:T(8,128)(2,1)}, bf16[4,16,16,128]{3,2,1,0:T(8,128)(2,1)}, bf16[4,16,16,128]{3,2,1,0:T(8,128)(2,1)}) custom-call(s32[2,18]{1,0:T(2,128)S(1)} %bitcast.23, s32[2,18]{1,0:T(2,128)S(1)} %bitcast.26, bf16[16,36,16,128]{3,2,1,0:T(8,128)(2,1)S(1)} %all_to_all.11.in_ref.refs_4_, ...), custom_call_target="tpu_custom_call" | custom-call | flops 301989888 | bytes 4718592 | tf_op jit(solution)/shard_map/pallas_call | solution.py:161
  133.4 1.9 %collective-permute-start.3 = (bf16[4,16,16,128]{3,2,1,0:T(8,128)(2,1)}, bf16[4,16,16,128]{3,2,1,0:T(8,128)(2,1)S(1)}, u32[]{:S(2)}, u32[]{:S(2)}) collective-permute-start(bf16[4,16,16,128]{3,2,1,0:T(8,128)(2,1)} %get-tuple-element.13), channel_id=1, source_target_pairs={{0,1},{1,2},{2,3},{3,4},{4,5},{5,6},{6,7},{7,8},{8,9},{9,10},{10,1... | collective-permute-start | bytes 786440 | tf_op jit(solution)/shard_map/ppermute | solution.py:259
  135.3 4.6 %collective-permute-start.4 = (bf16[4,16,16,128]{3,2,1,0:T(8,128)(2,1)}, bf16[4,16,16,128]{3,2,1,0:T(8,128)(2,1)S(1)}, u32[]{:S(2)}, u32[]{:S(2)}) collective-permute-start(bf16[4,16,16,128]{3,2,1,0:T(8,128)(2,1)} %get-tuple-element.14), channel_id=1, source_target_pairs={{0,15},{1,0},{2,1},{3,2},{4,3},{5,4},{6,5},{7,6},{8,7},{9,8},{10,9... | collective-permute-start | bytes 786440 | tf_op jit(solution)/shard_map/ppermute | solution.py:259
  139.9 1.9 %collective-permute-start.5 = (bf16[4,16,16,128]{3,2,1,0:T(8,128)(2,1)}, bf16[4,16,16,128]{3,2,1,0:T(8,128)(2,1)S(1)}, u32[]{:S(2)}, u32[]{:S(2)}) collective-permute-start(bf16[4,16,16,128]{3,2,1,0:T(8,128)(2,1)} %get-tuple-element.15), channel_id=1, source_target_pairs={{0,2},{1,3},{2,4},{3,5},{4,6},{5,7},{6,8},{7,9},{8,10},{9,11},{10,... | collective-permute-start | bytes 786440 | tf_op jit(solution)/shard_map/ppermute | solution.py:259
  141.8 2.8 %collective-permute-done.3.refs_1_ = bf16[4,16,16,128]{3,2,1,0:T(8,128)(2,1)S(1)} collective-permute-done((bf16[4,16,16,128]{3,2,1,0:T(8,128)(2,1)}, bf16[4,16,16,128]{3,2,1,0:T(8,128)(2,1)S(1)}, u32[]{:S(2)}, u32[]{:S(2)}) %collective-permute-start.3) | collective-permute-done | bytes 262176 | tf_op jit(solution)/shard_map/ppermute | solution.py:259
  144.6 1.0 collective-permute-done.4.refs_2_
  145.6 11.1 %collective-permute-done.5.refs_3_ = bf16[4,16,16,128]{3,2,1,0:T(8,128)(2,1)S(1)} collective-permute-done((bf16[4,16,16,128]{3,2,1,0:T(8,128)(2,1)}, bf16[4,16,16,128]{3,2,1,0:T(8,128)(2,1)S(1)}, u32[]{:S(2)}, u32[]{:S(2)}) %collective-permute-start.5) | collective-permute-done | bytes 262176 | tf_op jit(solution)/shard_map/ppermute | solution.py:259
  156.6 0.1 shard_map.114
  156.8 3.6 %collective-permute-start.6 = (bf16[16,16,128]{2,1,0:T(8,128)(2,1)S(1)}, bf16[16,16,128]{2,1,0:T(8,128)(2,1)S(1)}, u32[]{:S(2)}, u32[]{:S(2)}) collective-permute-start(bf16[16,16,128]{2,1,0:T(8,128)(2,1)S(1)} %get-tuple-element.17), channel_id=1, source_target_pairs={{0,4},{1,5},{2,6},{3,7},{4,8},{5,9},{6,10},{7,11},{8,12},{9,13},{1... | collective-permute-start | bytes 196616 | tf_op jit(solution)/shard_map/ppermute | solution.py:259
  160.3 7.3 %collective-permute-start.7 = (bf16[16,16,128]{2,1,0:T(8,128)(2,1)S(1)}, bf16[16,16,128]{2,1,0:T(8,128)(2,1)S(1)}, u32[]{:S(2)}, u32[]{:S(2)}) collective-permute-start(bf16[16,16,128]{2,1,0:T(8,128)(2,1)S(1)} %get-tuple-element.18), channel_id=1, source_target_pairs={{0,8},{1,9},{2,10},{3,11},{4,12},{5,13},{6,14},{7,15},{8,0},{9,1},... | collective-permute-start | bytes 196616 | tf_op jit(solution)/shard_map/ppermute | solution.py:259
  167.6 5.1 %collective-permute-start.8 = (bf16[16,16,128]{2,1,0:T(8,128)(2,1)S(1)}, bf16[16,16,128]{2,1,0:T(8,128)(2,1)S(1)}, u32[]{:S(2)}, u32[]{:S(2)}) collective-permute-start(bf16[16,16,128]{2,1,0:T(8,128)(2,1)S(1)} %get-tuple-element.19), channel_id=1, source_target_pairs={{0,12},{1,13},{2,14},{3,15},{4,0},{5,1},{6,2},{7,3},{8,4},{9,5},{1... | collective-permute-start | bytes 196616 | tf_op jit(solution)/shard_map/ppermute | solution.py:259
  172.8 0.0 collective-permute-done.6.refs_1_
  172.8 1.3 collective-permute-done.7.refs_2_
  174.1 7.9 %collective-permute-done.8.refs_3_ = bf16[16,16,128]{2,1,0:T(8,128)(2,1)S(1)} collective-permute-done((bf16[16,16,128]{2,1,0:T(8,128)(2,1)S(1)}, bf16[16,16,128]{2,1,0:T(8,128)(2,1)S(1)}, u32[]{:S(2)}, u32[]{:S(2)}) %collective-permute-start.8) | collective-permute-done | bytes 65568 | tf_op jit(solution)/shard_map/ppermute | solution.py:259
  182.0 0.0 collective-permute-done.9.refs_5_
  182.0 1.3 shard_map.116
Async XLA Ops:
  26.7 9.6 %collective-permute-start = (bf16[4,2,16,1024]{3,2,1,0:T(8,128)(2,1)S(1)}, bf16[4,2,16,1024]{3,2,1,0:T(8,128)(2,1)S(1)}, u32[]{:S(2)}, u32[]{:S(2)}) collective-permute-start(bf16[4,2,16,1024]{3,2,1,0:T(8,128)(2,1)S(1)} %bitcast.16), channel_id=1, source_target_pairs={{0,15},{1,0},{2,1},{3,2},{4,3},{5,4},{6,5},{7,6},{8,7},{9,8},{10,9... | collective-permute-start | bytes 786440 | tf_op jit(solution)/shard_map/ppermute | solution.py:259
  30.0 8.3 %collective-permute-start.1 = (bf16[4,2,16,1024]{3,2,1,0:T(8,128)(2,1)S(1)}, bf16[4,2,16,1024]{3,2,1,0:T(8,128)(2,1)S(1)}, u32[]{:S(2)}, u32[]{:S(2)}) collective-permute-start(bf16[4,2,16,1024]{3,2,1,0:T(8,128)(2,1)S(1)} %bitcast.17), channel_id=1, source_target_pairs={{0,1},{1,2},{2,3},{3,4},{4,5},{5,6},{6,7},{7,8},{8,9},{9,10},{10,1... | collective-permute-start | bytes 786440 | tf_op jit(solution)/shard_map/ppermute | solution.py:259
  31.9 16.1 %collective-permute-start.2 = (bf16[4,2,16,1024]{3,2,1,0:T(8,128)(2,1)S(1)}, bf16[4,2,16,1024]{3,2,1,0:T(8,128)(2,1)S(1)}, u32[]{:S(2)}, u32[]{:S(2)}) collective-permute-start(bf16[4,2,16,1024]{3,2,1,0:T(8,128)(2,1)S(1)} %bitcast.18), channel_id=1, source_target_pairs={{0,14},{1,15},{2,0},{3,1},{4,2},{5,3},{6,4},{7,5},{8,6},{9,7},{10,... | collective-permute-start | bytes 786440 | tf_op jit(solution)/shard_map/ppermute | solution.py:259
  48.0 1.1 copy-start
  49.1 1.1 copy-start.2
  50.2 0.7 copy-start.4
  50.8 0.7 copy-start.6
  91.6 31.2 %copy-start.5 = (s32[1,1,18,2]{2,3,1,0:T(2,128)S(1)}, s32[1,1,18,2]{2,3,1,0:T(2,128)}, u32[]{:S(2)}) copy-start(s32[1,1,18,2]{2,3,1,0:T(2,128)} %param.10) | copy-start | bytes 436
  91.6 31.2 %copy-start.7 = (s32[1,1,18,2]{2,3,1,0:T(2,128)S(1)}, s32[1,1,18,2]{2,3,1,0:T(2,128)}, u32[]{:S(2)}) copy-start(s32[1,1,18,2]{2,3,1,0:T(2,128)} %param.13) | copy-start | bytes 436
  122.9 8.1 %copy-start.1 = (bf16[1,1,18,128,128]{4,3,2,1,0:T(8,128)(2,1)S(1)}, bf16[1,1,18,128,128]{4,3,2,1,0:T(8,128)(2,1)}, u32[]{:S(2)}) copy-start(bf16[1,1,18,128,128]{4,3,2,1,0:T(8,128)(2,1)} %param.9) | copy-start | bytes 1769476
  122.9 8.1 %copy-start.3 = (bf16[1,1,18,128,128]{4,3,2,1,0:T(8,128)(2,1)S(1)}, bf16[1,1,18,128,128]{4,3,2,1,0:T(8,128)(2,1)}, u32[]{:S(2)}) copy-start(bf16[1,1,18,128,128]{4,3,2,1,0:T(8,128)(2,1)} %param.12) | copy-start | bytes 1769476
  124.4 57.7 %collective-permute-start.9 = (bf16[36,128,128]{2,1,0:T(8,128)(2,1)S(1)}, bf16[36,128,128]{2,1,0:T(8,128)(2,1)S(1)}, u32[]{:S(2)}, u32[]{:S(2)}) collective-permute-start(bf16[36,128,128]{2,1,0:T(8,128)(2,1)S(1)} %shard_map.115.refs_4_), channel_id=1, source_target_pairs={{0,256},{256,0},{1,257},{257,1},{2,258},{258,2},{3,259},{259,3},{4... | collective-permute-start | bytes 3538952 | tf_op jit(solution)/shard_map/ppermute | solution.py:278
  133.4 11.2 %collective-permute-start.3 = (bf16[4,16,16,128]{3,2,1,0:T(8,128)(2,1)}, bf16[4,16,16,128]{3,2,1,0:T(8,128)(2,1)S(1)}, u32[]{:S(2)}, u32[]{:S(2)}) collective-permute-start(bf16[4,16,16,128]{3,2,1,0:T(8,128)(2,1)} %get-tuple-element.13), channel_id=1, source_target_pairs={{0,1},{1,2},{2,3},{3,4},{4,5},{5,6},{6,7},{7,8},{8,9},{9,10},{10,1... | collective-permute-start | bytes 786440 | tf_op jit(solution)/shard_map/ppermute | solution.py:259
  135.3 10.3 %collective-permute-start.4 = (bf16[4,16,16,128]{3,2,1,0:T(8,128)(2,1)}, bf16[4,16,16,128]{3,2,1,0:T(8,128)(2,1)S(1)}, u32[]{:S(2)}, u32[]{:S(2)}) collective-permute-start(bf16[4,16,16,128]{3,2,1,0:T(8,128)(2,1)} %get-tuple-element.14), channel_id=1, source_target_pairs={{0,15},{1,0},{2,1},{3,2},{4,3},{5,4},{6,5},{7,6},{8,7},{9,8},{10,9... | collective-permute-start | bytes 786440 | tf_op jit(solution)/shard_map/ppermute | solution.py:259
  139.9 16.8 %collective-permute-start.5 = (bf16[4,16,16,128]{3,2,1,0:T(8,128)(2,1)}, bf16[4,16,16,128]{3,2,1,0:T(8,128)(2,1)S(1)}, u32[]{:S(2)}, u32[]{:S(2)}) collective-permute-start(bf16[4,16,16,128]{3,2,1,0:T(8,128)(2,1)} %get-tuple-element.15), channel_id=1, source_target_pairs={{0,2},{1,3},{2,4},{3,5},{4,6},{5,7},{6,8},{7,9},{8,10},{9,11},{10,... | collective-permute-start | bytes 786440 | tf_op jit(solution)/shard_map/ppermute | solution.py:259
  156.8 16.0 %collective-permute-start.6 = (bf16[16,16,128]{2,1,0:T(8,128)(2,1)S(1)}, bf16[16,16,128]{2,1,0:T(8,128)(2,1)S(1)}, u32[]{:S(2)}, u32[]{:S(2)}) collective-permute-start(bf16[16,16,128]{2,1,0:T(8,128)(2,1)S(1)} %get-tuple-element.17), channel_id=1, source_target_pairs={{0,4},{1,5},{2,6},{3,7},{4,8},{5,9},{6,10},{7,11},{8,12},{9,13},{1... | collective-permute-start | bytes 196616 | tf_op jit(solution)/shard_map/ppermute | solution.py:259
  160.3 13.8 %collective-permute-start.7 = (bf16[16,16,128]{2,1,0:T(8,128)(2,1)S(1)}, bf16[16,16,128]{2,1,0:T(8,128)(2,1)S(1)}, u32[]{:S(2)}, u32[]{:S(2)}) collective-permute-start(bf16[16,16,128]{2,1,0:T(8,128)(2,1)S(1)} %get-tuple-element.18), channel_id=1, source_target_pairs={{0,8},{1,9},{2,10},{3,11},{4,12},{5,13},{6,14},{7,15},{8,0},{9,1},... | collective-permute-start | bytes 196616 | tf_op jit(solution)/shard_map/ppermute | solution.py:259
  167.6 14.4 %collective-permute-start.8 = (bf16[16,16,128]{2,1,0:T(8,128)(2,1)S(1)}, bf16[16,16,128]{2,1,0:T(8,128)(2,1)S(1)}, u32[]{:S(2)}, u32[]{:S(2)}) collective-permute-start(bf16[16,16,128]{2,1,0:T(8,128)(2,1)S(1)} %get-tuple-element.19), channel_id=1, source_target_pairs={{0,12},{1,13},{2,14},{3,15},{4,0},{5,1},{6,2},{7,3},{8,4},{9,5},{1... | collective-permute-start | bytes 196616 | tf_op jit(solution)/shard_map/ppermute | solution.py:259

commit v5 on v4

--- a/solution.py
+++ b/solution.py
@@ -11,10 +11,13 @@
 FEATURE = 8
 HIDDEN = 32
 NEAR = 4
+STEPS = (0, 1, -1, 2, -2)
+PLACES = (4, 4, 4, 2, 2)
 VMEM_BYTES = 12 * 1024 * 1024
 
 VMEM = functools.partial(pl.BlockSpec, memory_space=pltpu.VMEM)
 SMEM = functools.partial(pl.BlockSpec, memory_space=pltpu.SMEM)
+HBM = functools.partial(pl.BlockSpec, memory_space=pltpu.HBM)
 
 
 def call(body, in_specs, out_shapes, scratch=(), flops=0, nbytes=0):
@@ -39,23 +42,56 @@
     return jnp.concatenate(parts, axis=0).reshape(-1, BS)
 
 
-def slot_products(rows, first, second, first_coords, second_coords, first_count, second_count):
-    group, both, share, width = rows[0].shape
-    peers = group * len(rows)
+def stage(first, second, first_coords, second_coords, first_count, second_count):
     slots = first.shape[0]
 
-    def body(c1_ref, c2_ref, n1_ref, n2_ref, *refs):
-        rows_refs, (w1_ref, w2_ref, out_ref) = refs[: len(rows)], refs[len(rows) :]
-        lane = lax.broadcasted_iota(jnp.int32, (share, BS), 1)
-        table = jnp.zeros((share, BS), jnp.int32)
+    def body(c1_ref, c2_ref, n1_ref, n2_ref, w1_hbm, w2_hbm, w1_ref, w2_ref, table_ref, feature_ref, sems):
+        copies = [
+            pltpu.make_async_copy(w1_hbm, w1_ref, sems.at[0]),
+            pltpu.make_async_copy(w2_hbm, w2_ref, sems.at[1]),
+        ]
+        for copy in copies:
+            copy.start()
+        lane = lax.broadcasted_iota(jnp.int32, table_ref.shape, 1)
+        table = jnp.zeros(table_ref.shape, jnp.int32)
+        row = lax.broadcasted_iota(jnp.int32, feature_ref.shape, 0)
+        place = lax.broadcasted_iota(jnp.int32, feature_ref.shape, 1)
+        feature = jnp.zeros(feature_ref.shape, jnp.int32)
         for s in range(slots):
             i = jnp.where(s < n1_ref[0, 0], c1_ref[1, s], HIDDEN)
             j = jnp.where(s < n2_ref[0, 0], c2_ref[0, s], HIDDEN)
             table = jnp.where(lane == s, i, jnp.where(lane == 64 + s, j, table))
-        table = table.astype(jnp.float32).astype(jnp.bfloat16)
+            feature = jnp.where(place == s, jnp.where(row == 0, c1_ref[0, s], c2_ref[1, s]), feature)
+        table_ref[...] = table.astype(jnp.float32).astype(jnp.bfloat16)
+        feature_ref[...] = feature
+        for copy in copies:
+            copy.wait()
+
+    return call(
+        body,
+        [SMEM()] * 4 + [HBM()] * 2,
+        (
+            jax.ShapeDtypeStruct(first.shape, jnp.bfloat16),
+            jax.ShapeDtypeStruct(second.shape, jnp.bfloat16),
+            jax.ShapeDtypeStruct((16, BS), jnp.bfloat16),
+            jax.ShapeDtypeStruct((8, BS), jnp.int32),
+        ),
+        scratch=[pltpu.SemaphoreType.DMA((2,))],
+        flops=first.size,
+        nbytes=8 * first.size,
+    )(first_coords, second_coords, first_count, second_count, first, second)
+
+
+def slot_products(rows, first, second, table, feature):
+    share = rows[0].shape[2]
+    peers = sum(part.shape[0] for part in rows)
+    slots = first.shape[0]
+
+    def body(index_ref, table_ref, w1_ref, w2_ref, *refs):
+        rows_refs, out_ref = refs[: len(rows)], refs[len(rows)]
         for p in range(peers):
-            out_ref[p, 2 * slots] = table
-        for base, line, index_ref, blocks_ref in ((0, 0, c1_ref, w1_ref), (slots, 1, c2_ref, w2_ref)):
+            out_ref[p, 2 * slots] = table_ref[...]
+        for base, line, blocks_ref in ((0, 0, w1_ref), (slots, 1, w2_ref)):
             for s in range(slots):
                 left = block_column(rows_refs, line, index_ref[line, s])
                 product = lax.dot_general(
@@ -65,11 +101,11 @@
 
     return call(
         body,
-        [SMEM()] * 4 + [VMEM()] * (len(rows) + 2),
+        [SMEM()] + [VMEM()] * (len(rows) + 3),
         jax.ShapeDtypeStruct((peers, 2 * slots + 1, share, BS), jnp.bfloat16),
         flops=4 * slots * peers * share * BS * BS,
         nbytes=8 * slots * peers * share * BS,
-    )(first_coords, second_coords, first_count, second_count, *rows, first, second)
+    )(feature, table, first, second, *rows)
 
 
 def hidden_step(parts):
@@ -94,18 +130,21 @@
 
         def add(p, carry):
             for s in range(slots):
-                i, j = index[p, s], index[p, 64 + s]
-                pre[i] = pre[i] + parts_ref[p, s].astype(jnp.float32)
-                grad[j] = grad[j] + parts_ref[p, slots + s].astype(jnp.float32)
+                for half in range(2):
+                    q = p + half * (peers // 2)
+                    i, j = index[q, s], index[q, 64 + s]
+                    pre[half, i] = pre[half, i] + parts_ref[q, s].astype(jnp.float32)
+                    grad[half, j] = grad[half, j] + parts_ref[q, slots + s].astype(jnp.float32)
             return carry
 
-        lax.fori_loop(0, peers, add, 0)
+        lax.fori_loop(0, peers // 2, add, 0)
 
         def point(h, carry):
-            value = pre[h]
+            value = pre[0, h] + pre[1, h]
+            slope = grad[0, h] + grad[1, h]
             gate = 1.0 / (1.0 + jnp.exp(-value))
             act_blocks[h] = (value * gate).astype(jnp.bfloat16)
-            grad_blocks[h] = (grad[h] * gate * (1.0 + value * (1.0 - gate))).astype(jnp.bfloat16)
+            grad_blocks[h] = (slope * gate * (1.0 + value * (1.0 - gate))).astype(jnp.bfloat16)
             return carry
 
         lax.fori_loop(0, hidden_blocks, point, 0, unroll=8)
@@ -123,8 +162,8 @@
         [VMEM()],
         jax.ShapeDtypeStruct((peers, 2 * slots, share, width), jnp.bfloat16),
         scratch=[
-            pltpu.VMEM((hidden_blocks + 1, share, width), jnp.float32),
-            pltpu.VMEM((hidden_blocks + 1, share, width), jnp.float32),
+            pltpu.VMEM((2, hidden_blocks + 1, share, width), jnp.float32),
+            pltpu.VMEM((2, hidden_blocks + 1, share, width), jnp.float32),
             pltpu.VMEM((hidden_blocks + 1, share, width), jnp.bfloat16),
             pltpu.VMEM((hidden_blocks + 1, share, width), jnp.bfloat16),
             pltpu.VMEM((peers, width), jnp.int32),
@@ -136,14 +175,13 @@
     )(parts)
 
 
-def feature_sums(slots_in, first, second, first_coords, second_coords):
+def feature_sums(slots_in, first, second, feature):
     peers, both, share, width = slots_in.shape
     slots = both // 2
-    group = peers // NEAR
-
-    def body(c1_ref, c2_ref, in_ref, w1_ref, w2_ref, *refs):
-        out_refs, total = refs[:NEAR], refs[NEAR]
-        for base, line, index_ref, blocks_ref in ((0, 1, c2_ref, w2_ref), (slots, 0, c1_ref, w1_ref)):
+
+    def body(index_ref, in_ref, w1_ref, w2_ref, *refs):
+        out_refs, total = refs[:-1], refs[-1]
+        for base, line, blocks_ref in ((0, 1, w2_ref), (slots, 0, w1_ref)):
             total[...] = jnp.zeros_like(total)
             for s in range(slots):
                 left = in_ref[:, base + s].reshape(peers * share, width)
@@ -154,67 +192,69 @@
                 total[target] = total[target] + product
             place = FEATURE if base else 0
             for k in range(FEATURE):
-                value = total[k].astype(jnp.bfloat16).reshape(NEAR, group, share, width)
-                for n in range(NEAR):
-                    out_refs[n][:, place + k] = value[n]
-
-    return call(
-        body,
-        [SMEM()] * 2 + [VMEM()] * 3,
-        (jax.ShapeDtypeStruct((group, 2 * FEATURE, share, width), jnp.bfloat16),) * NEAR,
+                value = total[k].astype(jnp.bfloat16).reshape(peers, share, width)
+                at = 0
+                for ref, places in zip(out_refs, PLACES):
+                    ref[:, place + k] = value[at : at + places]
+                    at += places
+
+    return call(
+        body,
+        [SMEM()] + [VMEM()] * 3,
+        tuple(
+            jax.ShapeDtypeStruct((places, 2 * FEATURE, share, width), jnp.bfloat16) for places in PLACES
+        ),
         scratch=[pltpu.VMEM((FEATURE, peers * share, width), jnp.float32)],
         flops=2 * slots_in.size * BS,
         nbytes=4 * slots_in.size,
-    )(first_coords, second_coords, slots_in, first, second)
-
-
-def block_grads(rows, slots_in, first_coords, second_coords):
+    )(feature, slots_in, first, second)
+
+
+def block_grads(rows, slots_in, feature):
     peers, both, share, width = slots_in.shape
     slots = both // 2
     dims = (((0,), (0,)), ((), ()))
 
-    def body(c1_ref, c2_ref, *refs):
+    def body(index_ref, *refs):
         rows_refs, (in_ref, out_ref) = refs[: len(rows)], refs[len(rows) :]
         for s in range(slots):
-            feature = block_column(rows_refs, 0, c1_ref[0, s])
+            left = block_column(rows_refs, 0, index_ref[0, s])
             hidden = in_ref[:, slots + s].reshape(peers * share, width)
-            grad = lax.dot_general(feature, hidden, dims, preferred_element_type=jnp.float32)
+            grad = lax.dot_general(left, hidden, dims, preferred_element_type=jnp.float32)
             out_ref[s] = grad.astype(jnp.bfloat16)
         for s in range(slots):
-            feature = block_column(rows_refs, 1, c2_ref[1, s])
+            right = block_column(rows_refs, 1, index_ref[1, s])
             hidden = in_ref[:, s].reshape(peers * share, width)
-            grad = lax.dot_general(hidden, feature, dims, preferred_element_type=jnp.float32)
+            grad = lax.dot_general(hidden, right, dims, preferred_element_type=jnp.float32)
             out_ref[slots + s] = grad.astype(jnp.bfloat16)
 
     return call(
         body,
-        [SMEM()] * 2 + [VMEM()] * (len(rows) + 1),
+        [SMEM()] + [VMEM()] * (len(rows) + 1),
         jax.ShapeDtypeStruct((both, BS, BS), jnp.bfloat16),
         flops=2 * slots_in.size * BS,
         nbytes=4 * slots_in.size,
-    )(first_coords, second_coords, *rows, slots_in)
+    )(feature, *rows, slots_in)
 
 
 def near_sums(parts, far_place):
     group, blocks, share, width = parts[0].shape
+    half = group // 2
 
     def body(place_ref, *refs):
-        part_refs, out_refs = refs[:NEAR], refs[NEAR:]
+        part_refs, (low_ref, high_ref), out_refs = refs[:3], refs[3:5], refs[5:]
         for step in range(group):
             k = lax.rem(place_ref[0] + step, group)
-
-            def add(b, carry):
-                total = part_refs[0][k, b].astype(jnp.float32)
-                for ref in part_refs[1:]:
+            for b in range(blocks):
+                pair = lax.rem(k, half)
+                total = jnp.where(k < half, low_ref[pair, b], high_ref[pair, b]).astype(jnp.float32)
+                for ref in part_refs:
                     total = total + ref[k, b].astype(jnp.float32)
                 out_refs[step][b] = total.astype(jnp.bfloat16)
-                return carry
-
-            lax.fori_loop(0, blocks, add, 0, unroll=True)
-
-    return call(
-        body,
-        [SMEM()] + [VMEM()] * NEAR,
+
+    return call(
+        body,
+        [SMEM()] + [VMEM()] * len(parts),
         (jax.ShapeDtypeStruct((blocks, share, width), jnp.bfloat16),) * group,
         flops=4 * parts[0].size,
         nbytes=8 * parts[0].size,
@@ -260,21 +300,24 @@
 
 
 def on_device(tokens, w1_blocks, w1_coords, w1_count, w2_blocks, w2_coords, w2_count, cotangent):
-    first, second = w1_blocks[0, 0], w2_blocks[0, 0]
-    first_coords, second_coords = w1_coords[0, 0].T, w2_coords[0, 0].T
     peers = lax.axis_size("col")
     far = [[c + NEAR * k for k in range(peers // NEAR)] for c in range(NEAR)]
-    steps = (0, 1, -1, 2)
 
     own = lax.all_gather(jnp.stack([tokens, cotangent]), "col", axis_index_groups=far)
-    rows = [own] + [send_on(own, -step) for step in steps[1:]]
-    parts = swap(
-        slot_products(rows, first, second, first_coords, second_coords, w1_count, w2_count), "row"
+    own, first, second = lax.optimization_barrier((own, w1_blocks, w2_blocks))
+    half = len(far[0]) // 2
+    rows = [own] + [
+        send_on(part, -step)
+        for part, step in zip((own, own, own[:half], own[half:]), STEPS[1:])
+    ]
+    first, second, table, feature = stage(
+        first[0, 0], second[0, 0], w1_coords[0, 0].T, w2_coords[0, 0].T, w1_count, w2_count
     )
+    parts = swap(slot_products(rows, first, second, table, feature), "row")
     slots_in = swap(hidden_step(parts), "row")
-    sums = feature_sums(slots_in, first, second, first_coords, second_coords)
-    sums = [sums[0]] + [send_on(part, step) for part, step in zip(sums[1:], steps[1:])]
-    grads = block_grads(rows, slots_in, first_coords, second_coords)
+    sums = feature_sums(slots_in, first, second, feature)
+    sums = [sums[0]] + [send_on(part, step) for part, step in zip(sums[1:], STEPS[1:])]
+    grads = block_grads(rows, slots_in, feature)
     others = lax.ppermute(grads, "tok", [(0, 1), (1, 0)])
     sums = near_sums(sums, lax.div(lax.axis_index("col"), NEAR).reshape(1))
     sums = [sums[0]] + [send_on(sums[k], NEAR * k) for k in range(1, peers // NEAR)]

time: 184 us -> 173 us (0.940)
  the two profiles are of different devices: /device:TPU:1 before, /device:TPU:64 now
where the time goes in v5:
time: 173 us; the launch traced here: 172 us
  blocking collectives  91.4 us (53%)
  starting transfers between devices  45.8 us (26%)
  waiting for transfers between devices  18.1 us (10%)
  Pallas kernels  10.7 us (6%)
  local copies, waits for them, and re-layouts  3.5 us (2%)
  between operations  2.13 us (1%)
    all_to_all x2, blocking collectives, swap(): return lax.all_to_all(parts, axis, split_axis=0, concat_axis=0, tiled=True)  66.4 us
    ppermute x11, starting transfers between devices, send_on(): lax.ppermute(value, 'col', [(c, (c + hops) % peers) for c in range(peers)])  43.9 us
    all_gather x1, blocking collectives, on_device(): lax.all_gather(jnp.stack([tokens, cotangent]), 'col', axis_index_groups=far)  25 us
    ppermute x11, waiting for transfers between devices, send_on(): lax.ppermute(value, 'col', [(c, (c + hops) % peers) for c in range(peers)])  18.1 us
    unnamed x8, local copies, waits for them, and re-layouts  3.48 us
  transfers between devices with their start and end apart: 12, of which 3 were waited for; matrix products, arithmetic and copies ran while one was open for 0% of the time, Pallas kernels for 2%

profile of v5, /device:TPU:64, one launch (start us, length us, event | category | flops | bytes accessed | tf_op | source)
XLA Modules:
  0.0 172.5 jit_solution(5742430438622102291)
XLA Ops:
  0.6 0.8 pad_maximum_fusion
  1.4 25.0 %all-gather = bf16[8,16,1024]{2,1,0:T(8,128)(2,1)S(1)} all-gather(bf16[2,16,1024]{2,1,0:T(8,128)(2,1)S(1)} %pad_maximum_fusion), channel_id=2, replica_groups={{0,4,8,12},{1,5,9,13},{2,6,10,14},{3,7,11,15},{16,20,24,28},{17,21,25,2..., dimensions={0}, use_global_device_ids=true | all-gather | bytes 327680 | tf_op jit(solution)/shard_map/all_gather | solution.py:306
  26.4 3.0 %collective-permute-start = (bf16[4,2,16,1024]{3,2,1,0:T(8,128)(2,1)S(1)}, bf16[4,2,16,1024]{3,2,1,0:T(8,128)(2,1)S(1)}, u32[]{:S(2)}, u32[]{:S(2)}) collective-permute-start(bf16[4,2,16,1024]{3,2,1,0:T(8,128)(2,1)S(1)} %bitcast.12), channel_id=1, source_target_pairs={{0,15},{1,0},{2,1},{3,2},{4,3},{5,4},{6,5},{7,6},{8,7},{9,8},{10,9... | collective-permute-start | bytes 786440 | tf_op jit(solution)/shard_map/ppermute | solution.py:299
  29.4 2.8 %collective-permute-start.1 = (bf16[4,2,16,1024]{3,2,1,0:T(8,128)(2,1)S(1)}, bf16[4,2,16,1024]{3,2,1,0:T(8,128)(2,1)S(1)}, u32[]{:S(2)}, u32[]{:S(2)}) collective-permute-start(bf16[4,2,16,1024]{3,2,1,0:T(8,128)(2,1)S(1)} %bitcast.13), channel_id=1, source_target_pairs={{0,1},{1,2},{2,3},{3,4},{4,5},{5,6},{6,7},{7,8},{8,9},{9,10},{10,1... | collective-permute-start | bytes 786440 | tf_op jit(solution)/shard_map/ppermute | solution.py:299
  32.3 3.5 %collective-permute-start.2 = (bf16[2,2,16,1024]{3,2,1,0:T(8,128)(2,1)S(1)}, bf16[2,2,16,1024]{3,2,1,0:T(8,128)(2,1)S(1)}, u32[]{:S(2)}, u32[]{:S(2)}) collective-permute-start(bf16[2,2,16,1024]{3,2,1,0:T(8,128)(2,1)S(1)} %get-tuple-element.37), channel_id=1, source_target_pairs={{0,14},{1,15},{2,0},{3,1},{4,2},{5,3},{6,4},{7,5},{8,6},{9,7},{10,... | collective-permute-start | bytes 393224 | tf_op jit(solution)/shard_map/ppermute | solution.py:299
  35.8 4.4 %collective-permute-start.3 = (bf16[2,2,16,1024]{3,2,1,0:T(8,128)(2,1)S(1)}, bf16[2,2,16,1024]{3,2,1,0:T(8,128)(2,1)S(1)}, u32[]{:S(2)}, u32[]{:S(2)}) collective-permute-start(bf16[2,2,16,1024]{3,2,1,0:T(8,128)(2,1)S(1)} %get-tuple-element.36), channel_id=1, source_target_pairs={{0,2},{1,3},{2,4},{3,5},{4,6},{5,7},{6,8},{7,9},{8,10},{9,11},{10,... | collective-permute-start | bytes 393224 | tf_op jit(solution)/shard_map/ppermute | solution.py:299
  41.5 0.0 copy-start
  41.5 1.1 copy-done
  42.6 0.0 copy-start.1
  42.6 1.1 copy-done.1
  43.7 0.0 copy-start.2
  43.7 0.7 copy-done.2
  44.4 0.0 copy-start.3
  44.4 0.7 copy-done.3
  45.0 0.9 shard_map.111
  45.9 0.0 collective-permute-done.2.refs_3_
  45.9 0.0 collective-permute-done.3.refs_4_
  45.9 0.0 collective-permute-done.refs_1_
  45.9 0.0 collective-permute-done.1.refs_2_
  45.9 1.4 shard_map.112
  47.4 34.9 %all_to_all.10.parts_ref = bf16[16,37,16,128]{3,2,1,0:T(8,128)(2,1)S(1)} all-to-all(bf16[16,37,16,128]{3,2,1,0:T(8,128)(2,1)S(1)} %shard_map.112), channel_id=1, replica_groups=mesh['tok'=2,'row'=16,'col'=16] {'row'}, dimensions={0} | all-to-all | bytes 4849664 | tf_op jit(solution)/shard_map/all_to_all | solution.py:294
  82.3 3.1 %shard_map.113 = bf16[16,36,16,128]{3,2,1,0:T(8,128)(2,1)S(1)} custom-call(bf16[16,37,16,128]{3,2,1,0:T(8,128)(2,1)S(1)} %all_to_all.10.parts_ref), custom_call_target="tpu_custom_call" | custom-call | flops 4849664 | bytes 7274496 | tf_op jit(solution)/shard_map/pallas_call | solution.py:160
  85.4 31.4 %all_to_all.11.in_ref.refs_5_ = bf16[16,36,16,128]{3,2,1,0:T(8,128)(2,1)S(1)} all-to-all(bf16[16,36,16,128]{3,2,1,0:T(8,128)(2,1)S(1)} %shard_map.113), channel_id=1, replica_groups=mesh['tok'=2,'row'=16,'col'=16] {'row'}, dimensions={0} | all-to-all | bytes 4718592 | tf_op jit(solution)/shard_map/all_to_all | solution.py:294
  116.8 1.5 shard_map.116.refs_4_
  118.4 1.9 %collective-permute-start.11 = (bf16[36,128,128]{2,1,0:T(8,128)(2,1)S(1)}, bf16[36,128,128]{2,1,0:T(8,128)(2,1)S(1)}, u32[]{:S(2)}, u32[]{:S(2)}) collective-permute-start(bf16[36,128,128]{2,1,0:T(8,128)(2,1)S(1)} %shard_map.116.refs_4_), channel_id=1, source_target_pairs={{0,256},{256,0},{1,257},{257,1},{2,258},{258,2},{3,259},{259,3},{4... | collective-permute-start | bytes 3538952 | tf_op jit(solution)/shard_map/ppermute | solution.py:321
  120.3 2.4 %shard_map.114 = (bf16[4,16,16,128]{3,2,1,0:T(8,128)(2,1)S(1)}, bf16[4,16,16,128]{3,2,1,0:T(8,128)(2,1)}, bf16[4,16,16,128]{3,2,1,0:T(8,128)(2,1)}, bf16[2,16,16...) custom-call(s32[8,128]{1,0:T(8,128)S(1)} %get-tuple-element.22.index_ref, ...), custom_call_target="tpu_custom_call" | custom-call | flops 301989888 | bytes 4718592 | tf_op jit(solution)/shard_map/pallas_call | solution.py:201
  122.8 2.1 %collective-permute-start.4 = (bf16[4,16,16,128]{3,2,1,0:T(8,128)(2,1)}, bf16[4,16,16,128]{3,2,1,0:T(8,128)(2,1)S(1)}, u32[]{:S(2)}, u32[]{:S(2)}) collective-permute-start(bf16[4,16,16,128]{3,2,1,0:T(8,128)(2,1)} %get-tuple-element.28), channel_id=1, source_target_pairs={{0,1},{1,2},{2,3},{3,4},{4,5},{5,6},{6,7},{7,8},{8,9},{9,10},{10,1... | collective-permute-start | bytes 786440 | tf_op jit(solution)/shard_map/ppermute | solution.py:299
  124.9 3.7 %collective-permute-start.5 = (bf16[4,16,16,128]{3,2,1,0:T(8,128)(2,1)}, bf16[4,16,16,128]{3,2,1,0:T(8,128)(2,1)S(1)}, u32[]{:S(2)}, u32[]{:S(2)}) collective-permute-start(bf16[4,16,16,128]{3,2,1,0:T(8,128)(2,1)} %get-tuple-element.29), channel_id=1, source_target_pairs={{0,15},{1,0},{2,1},{3,2},{4,3},{5,4},{6,5},{7,6},{8,7},{9,8},{10,9... | collective-permute-start | bytes 786440 | tf_op jit(solution)/shard_map/ppermute | solution.py:299
  128.6 2.9 %collective-permute-start.6 = (bf16[2,16,16,128]{3,2,1,0:T(8,128)(2,1)}, bf16[2,16,16,128]{3,2,1,0:T(8,128)(2,1)S(1)}, u32[]{:S(2)}, u32[]{:S(2)}) collective-permute-start(bf16[2,16,16,128]{3,2,1,0:T(8,128)(2,1)} %get-tuple-element.30), channel_id=1, source_target_pairs={{0,2},{1,3},{2,4},{3,5},{4,6},{5,7},{6,8},{7,9},{8,10},{9,11},{10,... | collective-permute-start | bytes 393224 | tf_op jit(solution)/shard_map/ppermute | solution.py:299
  131.5 3.8 %collective-permute-start.7 = (bf16[2,16,16,128]{3,2,1,0:T(8,128)(2,1)S(1)}, bf16[2,16,16,128]{3,2,1,0:T(8,128)(2,1)S(1)}, u32[]{:S(2)}, u32[]{:S(2)}) collective-permute-start(bf16[2,16,16,128]{3,2,1,0:T(8,128)(2,1)S(1)} %get-tuple-element.31), channel_id=1, source_target_pairs={{0,14},{1,15},{2,0},{3,1},{4,2},{5,3},{6,4},{7,5},{8,6},{9,7},{10,... | collective-permute-start | bytes 393224 | tf_op jit(solution)/shard_map/ppermute | solution.py:299
  135.4 4.4 %collective-permute-done.6.refs_3_ = bf16[2,16,16,128]{3,2,1,0:T(8,128)(2,1)S(1)} collective-permute-done((bf16[2,16,16,128]{3,2,1,0:T(8,128)(2,1)}, bf16[2,16,16,128]{3,2,1,0:T(8,128)(2,1)S(1)}, u32[]{:S(2)}, u32[]{:S(2)}) %collective-permute-start.6) | collective-permute-done | bytes 131104 | tf_op jit(solution)/shard_map/ppermute | solution.py:299
  139.8 3.8 %collective-permute-done.7.refs_4_ = bf16[2,16,16,128]{3,2,1,0:T(8,128)(2,1)S(1)} collective-permute-done((bf16[2,16,16,128]{3,2,1,0:T(8,128)(2,1)S(1)}, bf16[2,16,16,128]{3,2,1,0:T(8,128)(2,1)S(1)}, u32[]{:S(2)}, u32[]{:S(2)}) %collective-permute-start.7) | collective-permute-done | bytes 131104 | tf_op jit(solution)/shard_map/ppermute | solution.py:299
  143.5 0.0 collective-permute-done.4.refs_1_
  143.5 0.0 collective-permute-done.5.refs_2_
  143.5 0.1 shard_map.115
  143.7 4.7 %collective-permute-start.10 = (bf16[16,16,128]{2,1,0:T(8,128)(2,1)S(1)}, bf16[16,16,128]{2,1,0:T(8,128)(2,1)S(1)}, u32[]{:S(2)}, u32[]{:S(2)}) collective-permute-start(bf16[16,16,128]{2,1,0:T(8,128)(2,1)S(1)} %get-tuple-element.35), channel_id=1, source_target_pairs={{0,12},{1,13},{2,14},{3,15},{4,0},{5,1},{6,2},{7,3},{8,4},{9,5},{1... | collective-permute-start | bytes 196616 | tf_op jit(solution)/shard_map/ppermute | solution.py:299
  148.4 5.1 %collective-permute-start.8 = (bf16[16,16,128]{2,1,0:T(8,128)(2,1)S(1)}, bf16[16,16,128]{2,1,0:T(8,128)(2,1)S(1)}, u32[]{:S(2)}, u32[]{:S(2)}) collective-permute-start(bf16[16,16,128]{2,1,0:T(8,128)(2,1)S(1)} %get-tuple-element.33), channel_id=1, source_target_pairs={{0,4},{1,5},{2,6},{3,7},{4,8},{5,9},{6,10},{7,11},{8,12},{9,13},{1... | collective-permute-start | bytes 196616 | tf_op jit(solution)/shard_map/ppermute | solution.py:299
  153.5 7.8 %collective-permute-start.9 = (bf16[16,16,128]{2,1,0:T(8,128)(2,1)S(1)}, bf16[16,16,128]{2,1,0:T(8,128)(2,1)S(1)}, u32[]{:S(2)}, u32[]{:S(2)}) collective-permute-start(bf16[16,16,128]{2,1,0:T(8,128)(2,1)S(1)} %get-tuple-element.34), channel_id=1, source_target_pairs={{0,8},{1,9},{2,10},{3,11},{4,12},{5,13},{6,14},{7,15},{8,0},{9,1},... | collective-permute-start | bytes 196616 | tf_op jit(solution)/shard_map/ppermute | solution.py:299
  161.2 0.0 collective-permute-done.10.refs_3_
  161.2 0.0 collective-permute-done.8.refs_1_
  161.3 10.0 %collective-permute-done.9.refs_2_ = bf16[16,16,128]{2,1,0:T(8,128)(2,1)S(1)} collective-permute-done((bf16[16,16,128]{2,1,0:T(8,128)(2,1)S(1)}, bf16[16,16,128]{2,1,0:T(8,128)(2,1)S(1)}, u32[]{:S(2)}, u32[]{:S(2)}) %collective-permute-start.9) | collective-permute-done | bytes 65568 | tf_op jit(solution)/shard_map/ppermute | solution.py:299
  171.2 0.0 collective-permute-done.11.refs_5_
  171.2 1.3 shard_map.117
  (1 shorter events, 0.0 us)
Async XLA Ops:
  26.4 19.5 %collective-permute-start = (bf16[4,2,16,1024]{3,2,1,0:T(8,128)(2,1)S(1)}, bf16[4,2,16,1024]{3,2,1,0:T(8,128)(2,1)S(1)}, u32[]{:S(2)}, u32[]{:S(2)}) collective-permute-start(bf16[4,2,16,1024]{3,2,1,0:T(8,128)(2,1)S(1)} %bitcast.12), channel_id=1, source_target_pairs={{0,15},{1,0},{2,1},{3,2},{4,3},{5,4},{6,5},{7,6},{8,7},{9,8},{10,9... | collective-permute-start | bytes 786440 | tf_op jit(solution)/shard_map/ppermute | solution.py:299
  29.4 16.5 %collective-permute-start.1 = (bf16[4,2,16,1024]{3,2,1,0:T(8,128)(2,1)S(1)}, bf16[4,2,16,1024]{3,2,1,0:T(8,128)(2,1)S(1)}, u32[]{:S(2)}, u32[]{:S(2)}) collective-permute-start(bf16[4,2,16,1024]{3,2,1,0:T(8,128)(2,1)S(1)} %bitcast.13), channel_id=1, source_target_pairs={{0,1},{1,2},{2,3},{3,4},{4,5},{5,6},{6,7},{7,8},{8,9},{9,10},{10,1... | collective-permute-start | bytes 786440 | tf_op jit(solution)/shard_map/ppermute | solution.py:299
  32.3 13.6 %collective-permute-start.2 = (bf16[2,2,16,1024]{3,2,1,0:T(8,128)(2,1)S(1)}, bf16[2,2,16,1024]{3,2,1,0:T(8,128)(2,1)S(1)}, u32[]{:S(2)}, u32[]{:S(2)}) collective-permute-start(bf16[2,2,16,1024]{3,2,1,0:T(8,128)(2,1)S(1)} %get-tuple-element.37), channel_id=1, source_target_pairs={{0,14},{1,15},{2,0},{3,1},{4,2},{5,3},{6,4},{7,5},{8,6},{9,7},{10,... | collective-permute-start | bytes 393224 | tf_op jit(solution)/shard_map/ppermute | solution.py:299
  35.8 10.1 %collective-permute-start.3 = (bf16[2,2,16,1024]{3,2,1,0:T(8,128)(2,1)S(1)}, bf16[2,2,16,1024]{3,2,1,0:T(8,128)(2,1)S(1)}, u32[]{:S(2)}, u32[]{:S(2)}) collective-permute-start(bf16[2,2,16,1024]{3,2,1,0:T(8,128)(2,1)S(1)} %get-tuple-element.36), channel_id=1, source_target_pairs={{0,2},{1,3},{2,4},{3,5},{4,6},{5,7},{6,8},{7,9},{8,10},{9,11},{10,... | collective-permute-start | bytes 393224 | tf_op jit(solution)/shard_map/ppermute | solution.py:299
  41.5 1.1 copy-start
  42.6 1.1 copy-start.1
  43.7 0.7 copy-start.2
  44.4 0.7 copy-start.3
  118.4 52.8 %collective-permute-start.11 = (bf16[36,128,128]{2,1,0:T(8,128)(2,1)S(1)}, bf16[36,128,128]{2,1,0:T(8,128)(2,1)S(1)}, u32[]{:S(2)}, u32[]{:S(2)}) collective-permute-start(bf16[36,128,128]{2,1,0:T(8,128)(2,1)S(1)} %shard_map.116.refs_4_), channel_id=1, source_target_pairs={{0,256},{256,0},{1,257},{257,1},{2,258},{258,2},{3,259},{259,3},{4... | collective-permute-start | bytes 3538952 | tf_op jit(solution)/shard_map/ppermute | solution.py:321
  122.8 20.8 %collective-permute-start.4 = (bf16[4,16,16,128]{3,2,1,0:T(8,128)(2,1)}, bf16[4,16,16,128]{3,2,1,0:T(8,128)(2,1)S(1)}, u32[]{:S(2)}, u32[]{:S(2)}) collective-permute-start(bf16[4,16,16,128]{3,2,1,0:T(8,128)(2,1)} %get-tuple-element.28), channel_id=1, source_target_pairs={{0,1},{1,2},{2,3},{3,4},{4,5},{5,6},{6,7},{7,8},{8,9},{9,10},{10,1... | collective-permute-start | bytes 786440 | tf_op jit(solution)/shard_map/ppermute | solution.py:299
  124.9 18.6 %collective-permute-start.5 = (bf16[4,16,16,128]{3,2,1,0:T(8,128)(2,1)}, bf16[4,16,16,128]{3,2,1,0:T(8,128)(2,1)S(1)}, u32[]{:S(2)}, u32[]{:S(2)}) collective-permute-start(bf16[4,16,16,128]{3,2,1,0:T(8,128)(2,1)} %get-tuple-element.29), channel_id=1, source_target_pairs={{0,15},{1,0},{2,1},{3,2},{4,3},{5,4},{6,5},{7,6},{8,7},{9,8},{10,9... | collective-permute-start | bytes 786440 | tf_op jit(solution)/shard_map/ppermute | solution.py:299
  128.6 11.2 %collective-permute-start.6 = (bf16[2,16,16,128]{3,2,1,0:T(8,128)(2,1)}, bf16[2,16,16,128]{3,2,1,0:T(8,128)(2,1)S(1)}, u32[]{:S(2)}, u32[]{:S(2)}) collective-permute-start(bf16[2,16,16,128]{3,2,1,0:T(8,128)(2,1)} %get-tuple-element.30), channel_id=1, source_target_pairs={{0,2},{1,3},{2,4},{3,5},{4,6},{5,7},{6,8},{7,9},{8,10},{9,11},{10,... | collective-permute-start | bytes 393224 | tf_op jit(solution)/shard_map/ppermute | solution.py:299
  131.5 12.0 %collective-permute-start.7 = (bf16[2,16,16,128]{3,2,1,0:T(8,128)(2,1)S(1)}, bf16[2,16,16,128]{3,2,1,0:T(8,128)(2,1)S(1)}, u32[]{:S(2)}, u32[]{:S(2)}) collective-permute-start(bf16[2,16,16,128]{3,2,1,0:T(8,128)(2,1)S(1)} %get-tuple-element.31), channel_id=1, source_target_pairs={{0,14},{1,15},{2,0},{3,1},{4,2},{5,3},{6,4},{7,5},{8,6},{9,7},{10,... | collective-permute-start | bytes 393224 | tf_op jit(solution)/shard_map/ppermute | solution.py:299
  143.7 17.5 %collective-permute-start.10 = (bf16[16,16,128]{2,1,0:T(8,128)(2,1)S(1)}, bf16[16,16,128]{2,1,0:T(8,128)(2,1)S(1)}, u32[]{:S(2)}, u32[]{:S(2)}) collective-permute-start(bf16[16,16,128]{2,1,0:T(8,128)(2,1)S(1)} %get-tuple-element.35), channel_id=1, source_target_pairs={{0,12},{1,13},{2,14},{3,15},{4,0},{5,1},{6,2},{7,3},{8,4},{9,5},{1... | collective-permute-start | bytes 196616 | tf_op jit(solution)/shard_map/ppermute | solution.py:299
  148.4 12.9 %collective-permute-start.8 = (bf16[16,16,128]{2,1,0:T(8,128)(2,1)S(1)}, bf16[16,16,128]{2,1,0:T(8,128)(2,1)S(1)}, u32[]{:S(2)}, u32[]{:S(2)}) collective-permute-start(bf16[16,16,128]{2,1,0:T(8,128)(2,1)S(1)} %get-tuple-element.33), channel_id=1, source_target_pairs={{0,4},{1,5},{2,6},{3,7},{4,8},{5,9},{6,10},{7,11},{8,12},{9,13},{1... | collective-permute-start | bytes 196616 | tf_op jit(solution)/shard_map/ppermute | solution.py:299
  153.5 17.8 %collective-permute-start.9 = (bf16[16,16,128]{2,1,0:T(8,128)(2,1)S(1)}, bf16[16,16,128]{2,1,0:T(8,128)(2,1)S(1)}, u32[]{:S(2)}, u32[]{:S(2)}) collective-permute-start(bf16[16,16,128]{2,1,0:T(8,128)(2,1)S(1)} %get-tuple-element.34), channel_id=1, source_target_pairs={{0,8},{1,9},{2,10},{3,11},{4,12},{5,13},{6,14},{7,15},{8,0},{9,1},... | collective-permute-start | bytes 196616 | tf_op jit(solution)/shard_map/ppermute | solution.py:299

commit v6 on v5

--- a/solution.py
+++ b/solution.py
@@ -237,61 +237,55 @@
     )(feature, *rows, slots_in)
 
 
-def near_sums(parts, far_place):
+def near_sums(parts):
     group, blocks, share, width = parts[0].shape
     half = group // 2
 
-    def body(place_ref, *refs):
-        part_refs, (low_ref, high_ref), out_refs = refs[:3], refs[3:5], refs[5:]
-        for step in range(group):
-            k = lax.rem(place_ref[0] + step, group)
+    def body(*refs):
+        part_refs, halves, out_ref = refs[:3], refs[3:5], refs[5]
+        for k in range(group):
             for b in range(blocks):
-                pair = lax.rem(k, half)
-                total = jnp.where(k < half, low_ref[pair, b], high_ref[pair, b]).astype(jnp.float32)
+                total = halves[k // half][k % half, b].astype(jnp.float32)
                 for ref in part_refs:
                     total = total + ref[k, b].astype(jnp.float32)
-                out_refs[step][b] = total.astype(jnp.bfloat16)
-
-    return call(
-        body,
-        [SMEM()] + [VMEM()] * len(parts),
-        (jax.ShapeDtypeStruct((blocks, share, width), jnp.bfloat16),) * group,
+                out_ref[k, b] = total.astype(jnp.bfloat16)
+
+    return call(
+        body,
+        [VMEM()] * len(parts),
+        jax.ShapeDtypeStruct((group, blocks, share, width), jnp.bfloat16),
         flops=4 * parts[0].size,
         nbytes=8 * parts[0].size,
-    )(far_place, *parts)
+    )(*parts)
 
 
 def final_sums(parts, grads, others):
-    both, share, width = parts[0].shape
+    group, both, share, width = parts.shape
     slots = grads.shape[0] // 2
 
-    def body(*refs):
-        part_refs, refs = refs[: len(parts)], refs[len(parts) :]
-        grads_ref, others_ref, out_ref, in_ref, w1_ref, w2_ref = refs
+    def body(parts_ref, grads_ref, others_ref, out_ref, in_ref, w1_ref, w2_ref):
         for s in range(2 * slots):
             total = grads_ref[s].astype(jnp.float32) + others_ref[s].astype(jnp.float32)
             target = w1_ref if s < slots else w2_ref
             target[0, 0, s % slots] = total.astype(jnp.bfloat16)
         for k in range(both):
-            total = part_refs[0][k].astype(jnp.float32)
-            for ref in part_refs[1:]:
-                total = total + ref[k].astype(jnp.float32)
+            total = parts_ref[0, k].astype(jnp.float32)
+            for c in range(1, group):
+                total = total + parts_ref[c, k].astype(jnp.float32)
             target, place = (out_ref, k) if k < FEATURE else (in_ref, k - FEATURE)
             target[:, place * width : (place + 1) * width] = total.astype(jnp.bfloat16)
 
     row = jax.ShapeDtypeStruct((share, FEATURE * width), jnp.bfloat16)
     grad = jax.ShapeDtypeStruct((1, 1, slots, BS, BS), jnp.bfloat16)
     return call(
-        body,
-        [VMEM()] * (len(parts) + 2),
-        (row, row, grad, grad),
-        flops=grads.size,
-        nbytes=6 * grads.size,
-    )(*parts, grads, others)
-
-
-def swap(parts, axis):
-    return lax.all_to_all(parts, axis, split_axis=0, concat_axis=0, tiled=True)
+        body, [VMEM()] * 3, (row, row, grad, grad), flops=grads.size, nbytes=6 * grads.size
+    )(parts, grads, others)
+
+
+def swap(parts, axis, groups=None):
+    return lax.all_to_all(
+        parts, axis, split_axis=0, concat_axis=0, tiled=True, axis_index_groups=groups
+    )
 
 
 def send_on(value, hops):
@@ -319,8 +313,7 @@
     sums = [sums[0]] + [send_on(part, step) for part, step in zip(sums[1:], STEPS[1:])]
     grads = block_grads(rows, slots_in, feature)
     others = lax.ppermute(grads, "tok", [(0, 1), (1, 0)])
-    sums = near_sums(sums, lax.div(lax.axis_index("col"), NEAR).reshape(1))
-    sums = [sums[0]] + [send_on(sums[k], NEAR * k) for k in range(1, peers // NEAR)]
+    sums = swap(near_sums(sums), "col", far)
     return final_sums(sums, grads, others)
 
 

time: 173 us -> 170 us (0.983)
  blocking collectives: 91.4 us -> 112 us
  starting transfers between devices: 45.8 us -> 29.9 us
  waiting for transfers between devices: 18.1 us -> 11.2 us
    all_to_all x2 -> x3, blocking collectives: 66.4 us -> 87.3 us  [swap(): lax.all_to_all(parts, axis, split_axis=0, concat_axis=0, tiled=True, axis...]
    ppermute x11 -> x8, starting transfers between devices: 43.9 us -> 27.9 us  [send_on(): lax.ppermute(value, 'col', [(c, (c + hops) % peers) for c in range(peers)])]
    ppermute x11 -> x8, waiting for transfers between devices: 18.1 us -> 11.2 us  [send_on(): lax.ppermute(value, 'col', [(c, (c + hops) % peers) for c in range(peers)])]
  transfers between devices with their start and end apart: 12 -> 9, of which waited for: 3 -> 3; matrix products, arithmetic and copies ran while one was open for 0% -> 0% of each run, Pallas kernels for 2% -> 2%
where the time goes in v6:
time: 170 us
  blocking collectives  112 us (66%)
  starting transfers between devices  29.9 us (18%)
  waiting for transfers between devices  11.2 us (7%)
  Pallas kernels  9.93 us (6%)
  local copies, waits for them, and re-layouts  3.5 us (2%)
  between operations  2.07 us (1%)
    all_to_all x3, blocking collectives, swap(): lax.all_to_all(parts, axis, split_axis=0, concat_axis=0, tiled=True, axis...  87.3 us
    ppermute x8, starting transfers between devices, send_on(): lax.ppermute(value, 'col', [(c, (c + hops) % peers) for c in range(peers)])  27.9 us
    all_gather x1, blocking collectives, on_device(): lax.all_gather(jnp.stack([tokens, cotangent]), 'col', axis_index_groups=far)  25 us
    ppermute x8, waiting for transfers between devices, send_on(): lax.ppermute(value, 'col', [(c, (c + hops) % peers) for c in range(peers)])  11.2 us
    unnamed x8, local copies, waits for them, and re-layouts  3.48 us
  transfers between devices with their start and end apart: 9, of which 3 were waited for; matrix products, arithmetic and copies ran while one was open for 0% of the time, Pallas kernels for 2%

profile of v6, /device:TPU:64, one launch (start us, length us, event | category | flops | bytes accessed | tf_op | source)
XLA Modules:
  0.0 169.6 jit_solution(16530394896383502721)
XLA Ops:
  0.6 0.8 pad_maximum_fusion
  1.4 25.0 %all-gather = bf16[8,16,1024]{2,1,0:T(8,128)(2,1)S(1)} all-gather(bf16[2,16,1024]{2,1,0:T(8,128)(2,1)S(1)} %pad_maximum_fusion), channel_id=2, replica_groups={{0,4,8,12},{1,5,9,13},{2,6,10,14},{3,7,11,15},{16,20,24,28},{17,21,25,2..., dimensions={0}, use_global_device_ids=true | all-gather | bytes 327680 | tf_op jit(solution)/shard_map/all_gather | solution.py:300
  26.4 3.4 %collective-permute-start.1 = (bf16[4,2,16,1024]{3,2,1,0:T(8,128)(2,1)S(1)}, bf16[4,2,16,1024]{3,2,1,0:T(8,128)(2,1)S(1)}, u32[]{:S(2)}, u32[]{:S(2)}) collective-permute-start(bf16[4,2,16,1024]{3,2,1,0:T(8,128)(2,1)S(1)} %bitcast.11), channel_id=1, source_target_pairs={{0,1},{1,2},{2,3},{3,4},{4,5},{5,6},{6,7},{7,8},{8,9},{9,10},{10,1... | collective-permute-start | bytes 786440 | tf_op jit(solution)/shard_map/ppermute | solution.py:293
  29.8 2.5 %collective-permute-start = (bf16[4,2,16,1024]{3,2,1,0:T(8,128)(2,1)S(1)}, bf16[4,2,16,1024]{3,2,1,0:T(8,128)(2,1)S(1)}, u32[]{:S(2)}, u32[]{:S(2)}) collective-permute-start(bf16[4,2,16,1024]{3,2,1,0:T(8,128)(2,1)S(1)} %bitcast.12), channel_id=1, source_target_pairs={{0,15},{1,0},{2,1},{3,2},{4,3},{5,4},{6,5},{7,6},{8,7},{9,8},{10,9... | collective-permute-start | bytes 786440 | tf_op jit(solution)/shard_map/ppermute | solution.py:293
  32.3 5.7 %collective-permute-start.3 = (bf16[2,2,16,1024]{3,2,1,0:T(8,128)(2,1)S(1)}, bf16[2,2,16,1024]{3,2,1,0:T(8,128)(2,1)S(1)}, u32[]{:S(2)}, u32[]{:S(2)}) collective-permute-start(bf16[2,2,16,1024]{3,2,1,0:T(8,128)(2,1)S(1)} %get-tuple-element.28), channel_id=1, source_target_pairs={{0,2},{1,3},{2,4},{3,5},{4,6},{5,7},{6,8},{7,9},{8,10},{9,11},{10,... | collective-permute-start | bytes 393224 | tf_op jit(solution)/shard_map/ppermute | solution.py:293
  38.0 1.9 %collective-permute-start.2 = (bf16[2,2,16,1024]{3,2,1,0:T(8,128)(2,1)S(1)}, bf16[2,2,16,1024]{3,2,1,0:T(8,128)(2,1)S(1)}, u32[]{:S(2)}, u32[]{:S(2)}) collective-permute-start(bf16[2,2,16,1024]{3,2,1,0:T(8,128)(2,1)S(1)} %get-tuple-element.29), channel_id=1, source_target_pairs={{0,14},{1,15},{2,0},{3,1},{4,2},{5,3},{6,4},{7,5},{8,6},{9,7},{10,... | collective-permute-start | bytes 393224 | tf_op jit(solution)/shard_map/ppermute | solution.py:293
  41.3 0.0 copy-start
  41.3 1.1 copy-done
  42.3 0.0 copy-start.1
  42.3 1.1 copy-done.1
  43.4 0.0 copy-start.2
  43.4 0.7 copy-done.2
  44.1 0.0 copy-start.3
  44.1 0.7 copy-done.3
  44.7 0.9 shard_map.111
  45.6 0.0 collective-permute-done.3.refs_4_
  45.6 2.6 %collective-permute-done.2.refs_3_ = bf16[2,2,16,1024]{3,2,1,0:T(8,128)(2,1)S(1)} collective-permute-done((bf16[2,2,16,1024]{3,2,1,0:T(8,128)(2,1)S(1)}, bf16[2,2,16,1024]{3,2,1,0:T(8,128)(2,1)S(1)}, u32[]{:S(2)}, u32[]{:S(2)}) %collective-permute-start.2) | collective-permute-done | bytes 131104 | tf_op jit(solution)/shard_map/ppermute | solution.py:293
  48.3 0.0 collective-permute-done.1.refs_2_
  48.3 0.0 collective-permute-done.refs_1_
  48.3 1.4 shard_map.112
  49.7 33.5 %all_to_all.15.parts_ref = bf16[16,37,16,128]{3,2,1,0:T(8,128)(2,1)S(1)} all-to-all(bf16[16,37,16,128]{3,2,1,0:T(8,128)(2,1)S(1)} %shard_map.112), channel_id=1, replica_groups=mesh['tok'=2,'row'=16,'col'=16] {'row'}, dimensions={0} | all-to-all | bytes 4849664 | tf_op jit(solution)/shard_map/all_to_all | solution.py:286
  83.2 3.1 %shard_map.113 = bf16[16,36,16,128]{3,2,1,0:T(8,128)(2,1)S(1)} custom-call(bf16[16,37,16,128]{3,2,1,0:T(8,128)(2,1)S(1)} %all_to_all.15.parts_ref), custom_call_target="tpu_custom_call" | custom-call | flops 4849664 | bytes 7274496 | tf_op jit(solution)/shard_map/pallas_call | solution.py:160
  86.3 28.3 %all_to_all.16.in_ref.refs_5_ = bf16[16,36,16,128]{3,2,1,0:T(8,128)(2,1)S(1)} all-to-all(bf16[16,36,16,128]{3,2,1,0:T(8,128)(2,1)S(1)} %shard_map.113), channel_id=1, replica_groups=mesh['tok'=2,'row'=16,'col'=16] {'row'}, dimensions={0} | all-to-all | bytes 4718592 | tf_op jit(solution)/shard_map/all_to_all | solution.py:286
  114.6 1.5 shard_map.116.grads_ref
  116.1 1.9 %collective-permute-start.8 = (bf16[36,128,128]{2,1,0:T(8,128)(2,1)S(1)}, bf16[36,128,128]{2,1,0:T(8,128)(2,1)S(1)}, u32[]{:S(2)}, u32[]{:S(2)}) collective-permute-start(bf16[36,128,128]{2,1,0:T(8,128)(2,1)S(1)} %shard_map.116.grads_ref), channel_id=1, source_target_pairs={{0,256},{256,0},{1,257},{257,1},{2,258},{258,2},{3,259},{259,3},{4... | collective-permute-start | bytes 3538952 | tf_op jit(solution)/shard_map/ppermute | solution.py:315
  118.1 1.7 shard_map.114
  119.7 1.9 %collective-permute-start.4 = (bf16[4,16,16,128]{3,2,1,0:T(8,128)(2,1)S(1)}, bf16[4,16,16,128]{3,2,1,0:T(8,128)(2,1)S(1)}, u32[]{:S(2)}, u32[]{:S(2)}) collective-permute-start(bf16[4,16,16,128]{3,2,1,0:T(8,128)(2,1)S(1)} %get-tuple-element.24), channel_id=1, source_target_pairs={{0,1},{1,2},{2,3},{3,4},{4,5},{5,6},{6,7},{7,8},{8,9},{9,10},{10,1... | collective-permute-start | bytes 786440 | tf_op jit(solution)/shard_map/ppermute | solution.py:293
  121.6 4.1 %collective-permute-start.5 = (bf16[4,16,16,128]{3,2,1,0:T(8,128)(2,1)S(1)}, bf16[4,16,16,128]{3,2,1,0:T(8,128)(2,1)S(1)}, u32[]{:S(2)}, u32[]{:S(2)}) collective-permute-start(bf16[4,16,16,128]{3,2,1,0:T(8,128)(2,1)S(1)} %get-tuple-element.25), channel_id=1, source_target_pairs={{0,15},{1,0},{2,1},{3,2},{4,3},{5,4},{6,5},{7,6},{8,7},{9,8},{10,9... | collective-permute-start | bytes 786440 | tf_op jit(solution)/shard_map/ppermute | solution.py:293
  125.7 6.5 %collective-permute-start.6 = (bf16[2,16,16,128]{3,2,1,0:T(8,128)(2,1)S(1)}, bf16[2,16,16,128]{3,2,1,0:T(8,128)(2,1)S(1)}, u32[]{:S(2)}, u32[]{:S(2)}) collective-permute-start(bf16[2,16,16,128]{3,2,1,0:T(8,128)(2,1)S(1)} %get-tuple-element.26), channel_id=1, source_target_pairs={{0,2},{1,3},{2,4},{3,5},{4,6},{5,7},{6,8},{7,9},{8,10},{9,11},{10,... | collective-permute-start | bytes 393224 | tf_op jit(solution)/shard_map/ppermute | solution.py:293
  132.3 1.9 %collective-permute-start.7 = (bf16[2,16,16,128]{3,2,1,0:T(8,128)(2,1)S(1)}, bf16[2,16,16,128]{3,2,1,0:T(8,128)(2,1)S(1)}, u32[]{:S(2)}, u32[]{:S(2)}) collective-permute-start(bf16[2,16,16,128]{3,2,1,0:T(8,128)(2,1)S(1)} %get-tuple-element.27), channel_id=1, source_target_pairs={{0,14},{1,15},{2,0},{3,1},{4,2},{5,3},{6,4},{7,5},{8,6},{9,7},{10,... | collective-permute-start | bytes 393224 | tf_op jit(solution)/shard_map/ppermute | solution.py:293
  134.2 4.1 %collective-permute-done.6.refs_3_ = bf16[2,16,16,128]{3,2,1,0:T(8,128)(2,1)S(1)} collective-permute-done((bf16[2,16,16,128]{3,2,1,0:T(8,128)(2,1)S(1)}, bf16[2,16,16,128]{3,2,1,0:T(8,128)(2,1)S(1)}, u32[]{:S(2)}, u32[]{:S(2)}) %collective-permute-start.6) | collective-permute-done | bytes 131104 | tf_op jit(solution)/shard_map/ppermute | solution.py:293
  138.3 4.4 %collective-permute-done.7.refs_4_ = bf16[2,16,16,128]{3,2,1,0:T(8,128)(2,1)S(1)} collective-permute-done((bf16[2,16,16,128]{3,2,1,0:T(8,128)(2,1)S(1)}, bf16[2,16,16,128]{3,2,1,0:T(8,128)(2,1)S(1)}, u32[]{:S(2)}, u32[]{:S(2)}) %collective-permute-start.7) | collective-permute-done | bytes 131104 | tf_op jit(solution)/shard_map/ppermute | solution.py:293
  142.7 0.0 collective-permute-done.4.refs_1_
  142.7 0.0 collective-permute-done.5.refs_2_
  142.7 0.1 shard_map.115
  142.9 25.5 %all_to_all.17.parts_ref = bf16[4,16,16,128]{3,2,1,0:T(8,128)(2,1)S(1)} all-to-all(bf16[4,16,16,128]{3,2,1,0:T(8,128)(2,1)S(1)} %shard_map.115), channel_id=1, replica_groups={{0,4,8,12},{1,5,9,13},{2,6,10,14},{3,7,11,15},{16,20,24,28},{17,21,25,2..., dimensions={0} | all-to-all | bytes 524288 | tf_op jit(solution)/shard_map/all_to_all | solution.py:286
  168.3 0.0 collective-permute-done.8.others_ref
  168.3 1.3 shard_map.117
  (1 shorter events, 0.0 us)
Async XLA Ops:
  26.4 21.9 %collective-permute-start.1 = (bf16[4,2,16,1024]{3,2,1,0:T(8,128)(2,1)S(1)}, bf16[4,2,16,1024]{3,2,1,0:T(8,128)(2,1)S(1)}, u32[]{:S(2)}, u32[]{:S(2)}) collective-permute-start(bf16[4,2,16,1024]{3,2,1,0:T(8,128)(2,1)S(1)} %bitcast.11), channel_id=1, source_target_pairs={{0,1},{1,2},{2,3},{3,4},{4,5},{5,6},{6,7},{7,8},{8,9},{9,10},{10,1... | collective-permute-start | bytes 786440 | tf_op jit(solution)/shard_map/ppermute | solution.py:293
  29.8 18.5 %collective-permute-start = (bf16[4,2,16,1024]{3,2,1,0:T(8,128)(2,1)S(1)}, bf16[4,2,16,1024]{3,2,1,0:T(8,128)(2,1)S(1)}, u32[]{:S(2)}, u32[]{:S(2)}) collective-permute-start(bf16[4,2,16,1024]{3,2,1,0:T(8,128)(2,1)S(1)} %bitcast.12), channel_id=1, source_target_pairs={{0,15},{1,0},{2,1},{3,2},{4,3},{5,4},{6,5},{7,6},{8,7},{9,8},{10,9... | collective-permute-start | bytes 786440 | tf_op jit(solution)/shard_map/ppermute | solution.py:293
  32.3 13.3 %collective-permute-start.3 = (bf16[2,2,16,1024]{3,2,1,0:T(8,128)(2,1)S(1)}, bf16[2,2,16,1024]{3,2,1,0:T(8,128)(2,1)S(1)}, u32[]{:S(2)}, u32[]{:S(2)}) collective-permute-start(bf16[2,2,16,1024]{3,2,1,0:T(8,128)(2,1)S(1)} %get-tuple-element.28), channel_id=1, source_target_pairs={{0,2},{1,3},{2,4},{3,5},{4,6},{5,7},{6,8},{7,9},{8,10},{9,11},{10,... | collective-permute-start | bytes 393224 | tf_op jit(solution)/shard_map/ppermute | solution.py:293
  38.0 10.2 %collective-permute-start.2 = (bf16[2,2,16,1024]{3,2,1,0:T(8,128)(2,1)S(1)}, bf16[2,2,16,1024]{3,2,1,0:T(8,128)(2,1)S(1)}, u32[]{:S(2)}, u32[]{:S(2)}) collective-permute-start(bf16[2,2,16,1024]{3,2,1,0:T(8,128)(2,1)S(1)} %get-tuple-element.29), channel_id=1, source_target_pairs={{0,14},{1,15},{2,0},{3,1},{4,2},{5,3},{6,4},{7,5},{8,6},{9,7},{10,... | collective-permute-start | bytes 393224 | tf_op jit(solution)/shard_map/ppermute | solution.py:293
  41.3 1.1 copy-start
  42.3 1.1 copy-start.1
  43.4 0.7 copy-start.2
  44.1 0.7 copy-start.3
  116.1 52.2 %collective-permute-start.8 = (bf16[36,128,128]{2,1,0:T(8,128)(2,1)S(1)}, bf16[36,128,128]{2,1,0:T(8,128)(2,1)S(1)}, u32[]{:S(2)}, u32[]{:S(2)}) collective-permute-start(bf16[36,128,128]{2,1,0:T(8,128)(2,1)S(1)} %shard_map.116.grads_ref), channel_id=1, source_target_pairs={{0,256},{256,0},{1,257},{257,1},{2,258},{258,2},{3,259},{259,3},{4... | collective-permute-start | bytes 3538952 | tf_op jit(solution)/shard_map/ppermute | solution.py:315
  119.7 23.0 %collective-permute-start.4 = (bf16[4,16,16,128]{3,2,1,0:T(8,128)(2,1)S(1)}, bf16[4,16,16,128]{3,2,1,0:T(8,128)(2,1)S(1)}, u32[]{:S(2)}, u32[]{:S(2)}) collective-permute-start(bf16[4,16,16,128]{3,2,1,0:T(8,128)(2,1)S(1)} %get-tuple-element.24), channel_id=1, source_target_pairs={{0,1},{1,2},{2,3},{3,4},{4,5},{5,6},{6,7},{7,8},{8,9},{9,10},{10,1... | collective-permute-start | bytes 786440 | tf_op jit(solution)/shard_map/ppermute | solution.py:293
  121.6 21.1 %collective-permute-start.5 = (bf16[4,16,16,128]{3,2,1,0:T(8,128)(2,1)S(1)}, bf16[4,16,16,128]{3,2,1,0:T(8,128)(2,1)S(1)}, u32[]{:S(2)}, u32[]{:S(2)}) collective-permute-start(bf16[4,16,16,128]{3,2,1,0:T(8,128)(2,1)S(1)} %get-tuple-element.25), channel_id=1, source_target_pairs={{0,15},{1,0},{2,1},{3,2},{4,3},{5,4},{6,5},{7,6},{8,7},{9,8},{10,9... | collective-permute-start | bytes 786440 | tf_op jit(solution)/shard_map/ppermute | solution.py:293
  125.7 12.6 %collective-permute-start.6 = (bf16[2,16,16,128]{3,2,1,0:T(8,128)(2,1)S(1)}, bf16[2,16,16,128]{3,2,1,0:T(8,128)(2,1)S(1)}, u32[]{:S(2)}, u32[]{:S(2)}) collective-permute-start(bf16[2,16,16,128]{3,2,1,0:T(8,128)(2,1)S(1)} %get-tuple-element.26), channel_id=1, source_target_pairs={{0,2},{1,3},{2,4},{3,5},{4,6},{5,7},{6,8},{7,9},{8,10},{9,11},{10,... | collective-permute-start | bytes 393224 | tf_op jit(solution)/shard_map/ppermute | solution.py:293
  132.3 10.5 %collective-permute-start.7 = (bf16[2,16,16,128]{3,2,1,0:T(8,128)(2,1)S(1)}, bf16[2,16,16,128]{3,2,1,0:T(8,128)(2,1)S(1)}, u32[]{:S(2)}, u32[]{:S(2)}) collective-permute-start(bf16[2,16,16,128]{3,2,1,0:T(8,128)(2,1)S(1)} %get-tuple-element.27), channel_id=1, source_target_pairs={{0,14},{1,15},{2,0},{3,1},{4,2},{5,3},{6,4},{7,5},{8,6},{9,7},{10,... | collective-permute-start | bytes 393224 | tf_op jit(solution)/shard_map/ppermute | solution.py:293

commit v7 on v6

--- a/solution.py
+++ b/solution.py
@@ -45,13 +45,17 @@
 def stage(first, second, first_coords, second_coords, first_count, second_count):
     slots = first.shape[0]
 
-    def body(c1_ref, c2_ref, n1_ref, n2_ref, w1_hbm, w2_hbm, w1_ref, w2_ref, table_ref, feature_ref, sems):
+    def body(n1_ref, n2_ref, *refs):
+        sources, (w1_ref, w2_ref, table_ref, feature_ref) = refs[:4], refs[4:8]
+        c1_ref, c2_ref, sems = refs[8:]
+        targets = (c1_ref, c2_ref, w1_ref, w2_ref)
         copies = [
-            pltpu.make_async_copy(w1_hbm, w1_ref, sems.at[0]),
-            pltpu.make_async_copy(w2_hbm, w2_ref, sems.at[1]),
+            pltpu.make_async_copy(x, y, sems.at[i]) for i, (x, y) in enumerate(zip(sources, targets))
         ]
         for copy in copies:
             copy.start()
+        for copy in copies[:2]:
+            copy.wait()
         lane = lax.broadcasted_iota(jnp.int32, table_ref.shape, 1)
         table = jnp.zeros(table_ref.shape, jnp.int32)
         row = lax.broadcasted_iota(jnp.int32, feature_ref.shape, 0)
@@ -64,22 +68,33 @@
             feature = jnp.where(place == s, jnp.where(row == 0, c1_ref[0, s], c2_ref[1, s]), feature)
         table_ref[...] = table.astype(jnp.float32).astype(jnp.bfloat16)
         feature_ref[...] = feature
-        for copy in copies:
+        for copy in copies[2:]:
             copy.wait()
 
     return call(
         body,
-        [SMEM()] * 4 + [HBM()] * 2,
+        [SMEM()] * 2 + [HBM()] * 4,
         (
             jax.ShapeDtypeStruct(first.shape, jnp.bfloat16),
             jax.ShapeDtypeStruct(second.shape, jnp.bfloat16),
             jax.ShapeDtypeStruct((16, BS), jnp.bfloat16),
             jax.ShapeDtypeStruct((8, BS), jnp.int32),
         ),
-        scratch=[pltpu.SemaphoreType.DMA((2,))],
+        scratch=[
+            pltpu.SMEM(first_coords.shape, jnp.int32),
+            pltpu.SMEM(second_coords.shape, jnp.int32),
+            pltpu.SemaphoreType.DMA((4,)),
+        ],
         flops=first.size,
         nbytes=8 * first.size,
-    )(first_coords, second_coords, first_count, second_count, first, second)
+    )(
+        first_count,
+        second_count,
+        *(
+            pltpu.with_memory_space_constraint(value, pltpu.HBM)
+            for value in (first_coords, second_coords, first, second)
+        ),
+    )
 
 
 def slot_products(rows, first, second, table, feature):

time: 170 us -> 168 us (0.988)
  local copies, waits for them, and re-layouts: 3.5 us -> 0.02 us
  waiting for transfers between devices: 11.2 us -> 13.7 us
  starting transfers between devices: 29.9 us -> 28 us
    unnamed x8 -> x0, local copies, waits for them, and re-layouts: 3.48 us -> none
    ppermute x8, waiting for transfers between devices: 11.2 us -> 13.7 us  [send_on(): lax.ppermute(value, 'col', [(c, (c + hops) % peers) for c in range(peers)])]
    ppermute x8, starting transfers between devices: 27.9 us -> 26.1 us  [send_on(): lax.ppermute(value, 'col', [(c, (c + hops) % peers) for c in range(peers)])]
where the time goes in v7:
time: 168 us
  blocking collectives  113 us (67%)
  starting transfers between devices  28 us (17%)
  waiting for transfers between devices  13.7 us (8%)
  Pallas kernels  10.3 us (6%)
  between operations  2.06 us (1%)
    all_to_all x3, blocking collectives, swap(): lax.all_to_all(parts, axis, split_axis=0, concat_axis=0, tiled=True, axis...  87.7 us
    ppermute x8, starting transfers between devices, send_on(): lax.ppermute(value, 'col', [(c, (c + hops) % peers) for c in range(peers)])  26.1 us
    all_gather x1, blocking collectives, on_device(): lax.all_gather(jnp.stack([tokens, cotangent]), 'col', axis_index_groups=far)  25 us
    ppermute x8, waiting for transfers between devices, send_on(): lax.ppermute(value, 'col', [(c, (c + hops) % peers) for c in range(peers)])  13.7 us
  transfers between devices with their start and end apart: 9, of which 3 were waited for; matrix products, arithmetic and copies ran while one was open for 0% of the time, Pallas kernels for 2%

profile of v7, /device:TPU:64, one launch (start us, length us, event | category | flops | bytes accessed | tf_op | source)
XLA Modules:
  0.0 167.7 jit_solution(14703935039155928125)
XLA Ops:
  0.6 0.8 pad_maximum_fusion
  1.4 25.0 %all-gather = bf16[8,16,1024]{2,1,0:T(8,128)(2,1)S(1)} all-gather(bf16[2,16,1024]{2,1,0:T(8,128)(2,1)S(1)} %pad_maximum_fusion), channel_id=2, replica_groups={{0,4,8,12},{1,5,9,13},{2,6,10,14},{3,7,11,15},{16,20,24,28},{17,21,25,2..., dimensions={0}, use_global_device_ids=true | all-gather | bytes 327680 | tf_op jit(solution)/shard_map/all_gather | solution.py:315
  26.4 3.4 %collective-permute-start.1 = (bf16[4,2,16,1024]{3,2,1,0:T(8,128)(2,1)S(1)}, bf16[4,2,16,1024]{3,2,1,0:T(8,128)(2,1)S(1)}, u32[]{:S(2)}, u32[]{:S(2)}) collective-permute-start(bf16[4,2,16,1024]{3,2,1,0:T(8,128)(2,1)S(1)} %bitcast.11), channel_id=1, source_target_pairs={{0,1},{1,2},{2,3},{3,4},{4,5},{5,6},{6,7},{7,8},{8,9},{9,10},{10,1... | collective-permute-start | bytes 786440 | tf_op jit(solution)/shard_map/ppermute | solution.py:308
  29.8 2.5 %collective-permute-start = (bf16[4,2,16,1024]{3,2,1,0:T(8,128)(2,1)S(1)}, bf16[4,2,16,1024]{3,2,1,0:T(8,128)(2,1)S(1)}, u32[]{:S(2)}, u32[]{:S(2)}) collective-permute-start(bf16[4,2,16,1024]{3,2,1,0:T(8,128)(2,1)S(1)} %bitcast.12), channel_id=1, source_target_pairs={{0,15},{1,0},{2,1},{3,2},{4,3},{5,4},{6,5},{7,6},{8,7},{9,8},{10,9... | collective-permute-start | bytes 786440 | tf_op jit(solution)/shard_map/ppermute | solution.py:308
  32.3 5.7 %collective-permute-start.3 = (bf16[2,2,16,1024]{3,2,1,0:T(8,128)(2,1)S(1)}, bf16[2,2,16,1024]{3,2,1,0:T(8,128)(2,1)S(1)}, u32[]{:S(2)}, u32[]{:S(2)}) collective-permute-start(bf16[2,2,16,1024]{3,2,1,0:T(8,128)(2,1)S(1)} %get-tuple-element.28), channel_id=1, source_target_pairs={{0,2},{1,3},{2,4},{3,5},{4,6},{5,7},{6,8},{7,9},{8,10},{9,11},{10,... | collective-permute-start | bytes 393224 | tf_op jit(solution)/shard_map/ppermute | solution.py:308
  38.0 1.9 %collective-permute-start.2 = (bf16[2,2,16,1024]{3,2,1,0:T(8,128)(2,1)S(1)}, bf16[2,2,16,1024]{3,2,1,0:T(8,128)(2,1)S(1)}, u32[]{:S(2)}, u32[]{:S(2)}) collective-permute-start(bf16[2,2,16,1024]{3,2,1,0:T(8,128)(2,1)S(1)} %get-tuple-element.29), channel_id=1, source_target_pairs={{0,14},{1,15},{2,0},{3,1},{4,2},{5,3},{6,4},{7,5},{8,6},{9,7},{10,... | collective-permute-start | bytes 393224 | tf_op jit(solution)/shard_map/ppermute | solution.py:308
  41.3 1.3 shard_map.111
  42.5 0.0 collective-permute-done.3.refs_4_
  42.6 5.7 %collective-permute-done.2.refs_3_ = bf16[2,2,16,1024]{3,2,1,0:T(8,128)(2,1)S(1)} collective-permute-done((bf16[2,2,16,1024]{3,2,1,0:T(8,128)(2,1)S(1)}, bf16[2,2,16,1024]{3,2,1,0:T(8,128)(2,1)S(1)}, u32[]{:S(2)}, u32[]{:S(2)}) %collective-permute-start.2) | collective-permute-done | bytes 131104 | tf_op jit(solution)/shard_map/ppermute | solution.py:308
  48.3 0.0 collective-permute-done.1.refs_2_
  48.3 0.0 collective-permute-done.refs_1_
  48.3 1.4 shard_map.112
  49.7 33.5 %all_to_all.15.parts_ref = bf16[16,37,16,128]{3,2,1,0:T(8,128)(2,1)S(1)} all-to-all(bf16[16,37,16,128]{3,2,1,0:T(8,128)(2,1)S(1)} %shard_map.112), channel_id=1, replica_groups=mesh['tok'=2,'row'=16,'col'=16] {'row'}, dimensions={0} | all-to-all | bytes 4849664 | tf_op jit(solution)/shard_map/all_to_all | solution.py:301
  83.2 3.1 %shard_map.113 = bf16[16,36,16,128]{3,2,1,0:T(8,128)(2,1)S(1)} custom-call(bf16[16,37,16,128]{3,2,1,0:T(8,128)(2,1)S(1)} %all_to_all.15.parts_ref), custom_call_target="tpu_custom_call" | custom-call | flops 4849664 | bytes 7274496 | tf_op jit(solution)/shard_map/pallas_call | solution.py:175
  86.3 28.3 %all_to_all.16.in_ref.refs_5_ = bf16[16,36,16,128]{3,2,1,0:T(8,128)(2,1)S(1)} all-to-all(bf16[16,36,16,128]{3,2,1,0:T(8,128)(2,1)S(1)} %shard_map.113), channel_id=1, replica_groups=mesh['tok'=2,'row'=16,'col'=16] {'row'}, dimensions={0} | all-to-all | bytes 4718592 | tf_op jit(solution)/shard_map/all_to_all | solution.py:301
  114.6 1.5 shard_map.116.grads_ref
  116.1 1.9 %collective-permute-start.8 = (bf16[36,128,128]{2,1,0:T(8,128)(2,1)S(1)}, bf16[36,128,128]{2,1,0:T(8,128)(2,1)S(1)}, u32[]{:S(2)}, u32[]{:S(2)}) collective-permute-start(bf16[36,128,128]{2,1,0:T(8,128)(2,1)S(1)} %shard_map.116.grads_ref), channel_id=1, source_target_pairs={{0,256},{256,0},{1,257},{257,1},{2,258},{258,2},{3,259},{259,3},{4... | collective-permute-start | bytes 3538952 | tf_op jit(solution)/shard_map/ppermute | solution.py:330
  118.1 1.7 shard_map.114
  119.7 1.9 %collective-permute-start.4 = (bf16[4,16,16,128]{3,2,1,0:T(8,128)(2,1)S(1)}, bf16[4,16,16,128]{3,2,1,0:T(8,128)(2,1)S(1)}, u32[]{:S(2)}, u32[]{:S(2)}) collective-permute-start(bf16[4,16,16,128]{3,2,1,0:T(8,128)(2,1)S(1)} %get-tuple-element.24), channel_id=1, source_target_pairs={{0,1},{1,2},{2,3},{3,4},{4,5},{5,6},{6,7},{7,8},{8,9},{9,10},{10,1... | collective-permute-start | bytes 786440 | tf_op jit(solution)/shard_map/ppermute | solution.py:308
  121.6 3.9 %collective-permute-start.5 = (bf16[4,16,16,128]{3,2,1,0:T(8,128)(2,1)S(1)}, bf16[4,16,16,128]{3,2,1,0:T(8,128)(2,1)S(1)}, u32[]{:S(2)}, u32[]{:S(2)}) collective-permute-start(bf16[4,16,16,128]{3,2,1,0:T(8,128)(2,1)S(1)} %get-tuple-element.25), channel_id=1, source_target_pairs={{0,15},{1,0},{2,1},{3,2},{4,3},{5,4},{6,5},{7,6},{8,7},{9,8},{10,9... | collective-permute-start | bytes 786440 | tf_op jit(solution)/shard_map/ppermute | solution.py:308
  125.6 3.2 %collective-permute-start.6 = (bf16[2,16,16,128]{3,2,1,0:T(8,128)(2,1)S(1)}, bf16[2,16,16,128]{3,2,1,0:T(8,128)(2,1)S(1)}, u32[]{:S(2)}, u32[]{:S(2)}) collective-permute-start(bf16[2,16,16,128]{3,2,1,0:T(8,128)(2,1)S(1)} %get-tuple-element.26), channel_id=1, source_target_pairs={{0,2},{1,3},{2,4},{3,5},{4,6},{5,7},{6,8},{7,9},{8,10},{9,11},{10,... | collective-permute-start | bytes 393224 | tf_op jit(solution)/shard_map/ppermute | solution.py:308
  128.8 3.5 %collective-permute-start.7 = (bf16[2,16,16,128]{3,2,1,0:T(8,128)(2,1)S(1)}, bf16[2,16,16,128]{3,2,1,0:T(8,128)(2,1)S(1)}, u32[]{:S(2)}, u32[]{:S(2)}) collective-permute-start(bf16[2,16,16,128]{3,2,1,0:T(8,128)(2,1)S(1)} %get-tuple-element.27), channel_id=1, source_target_pairs={{0,14},{1,15},{2,0},{3,1},{4,2},{5,3},{6,4},{7,5},{8,6},{9,7},{10,... | collective-permute-start | bytes 393224 | tf_op jit(solution)/shard_map/ppermute | solution.py:308
  132.3 3.4 %collective-permute-done.6.refs_3_ = bf16[2,16,16,128]{3,2,1,0:T(8,128)(2,1)S(1)} collective-permute-done((bf16[2,16,16,128]{3,2,1,0:T(8,128)(2,1)S(1)}, bf16[2,16,16,128]{3,2,1,0:T(8,128)(2,1)S(1)}, u32[]{:S(2)}, u32[]{:S(2)}) %collective-permute-start.6) | collective-permute-done | bytes 131104 | tf_op jit(solution)/shard_map/ppermute | solution.py:308
  135.8 4.6 %collective-permute-done.7.refs_4_ = bf16[2,16,16,128]{3,2,1,0:T(8,128)(2,1)S(1)} collective-permute-done((bf16[2,16,16,128]{3,2,1,0:T(8,128)(2,1)S(1)}, bf16[2,16,16,128]{3,2,1,0:T(8,128)(2,1)S(1)}, u32[]{:S(2)}, u32[]{:S(2)}) %collective-permute-start.7) | collective-permute-done | bytes 131104 | tf_op jit(solution)/shard_map/ppermute | solution.py:308
  140.3 0.0 collective-permute-done.4.refs_1_
  140.4 0.0 collective-permute-done.5.refs_2_
  140.4 0.1 shard_map.115
  140.5 25.9 %all_to_all.17.parts_ref = bf16[4,16,16,128]{3,2,1,0:T(8,128)(2,1)S(1)} all-to-all(bf16[4,16,16,128]{3,2,1,0:T(8,128)(2,1)S(1)} %shard_map.115), channel_id=1, replica_groups={{0,4,8,12},{1,5,9,13},{2,6,10,14},{3,7,11,15},{16,20,24,28},{17,21,25,2..., dimensions={0} | all-to-all | bytes 524288 | tf_op jit(solution)/shard_map/all_to_all | solution.py:301
  166.4 0.0 collective-permute-done.8.others_ref
  166.4 1.3 shard_map.117
  (1 shorter events, 0.0 us)
Async XLA Ops:
  26.4 21.9 %collective-permute-start.1 = (bf16[4,2,16,1024]{3,2,1,0:T(8,128)(2,1)S(1)}, bf16[4,2,16,1024]{3,2,1,0:T(8,128)(2,1)S(1)}, u32[]{:S(2)}, u32[]{:S(2)}) collective-permute-start(bf16[4,2,16,1024]{3,2,1,0:T(8,128)(2,1)S(1)} %bitcast.11), channel_id=1, source_target_pairs={{0,1},{1,2},{2,3},{3,4},{4,5},{5,6},{6,7},{7,8},{8,9},{9,10},{10,1... | collective-permute-start | bytes 786440 | tf_op jit(solution)/shard_map/ppermute | solution.py:308
  29.8 18.5 %collective-permute-start = (bf16[4,2,16,1024]{3,2,1,0:T(8,128)(2,1)S(1)}, bf16[4,2,16,1024]{3,2,1,0:T(8,128)(2,1)S(1)}, u32[]{:S(2)}, u32[]{:S(2)}) collective-permute-start(bf16[4,2,16,1024]{3,2,1,0:T(8,128)(2,1)S(1)} %bitcast.12), channel_id=1, source_target_pairs={{0,15},{1,0},{2,1},{3,2},{4,3},{5,4},{6,5},{7,6},{8,7},{9,8},{10,9... | collective-permute-start | bytes 786440 | tf_op jit(solution)/shard_map/ppermute | solution.py:308
  32.3 10.3 %collective-permute-start.3 = (bf16[2,2,16,1024]{3,2,1,0:T(8,128)(2,1)S(1)}, bf16[2,2,16,1024]{3,2,1,0:T(8,128)(2,1)S(1)}, u32[]{:S(2)}, u32[]{:S(2)}) collective-permute-start(bf16[2,2,16,1024]{3,2,1,0:T(8,128)(2,1)S(1)} %get-tuple-element.28), channel_id=1, source_target_pairs={{0,2},{1,3},{2,4},{3,5},{4,6},{5,7},{6,8},{7,9},{8,10},{9,11},{10,... | collective-permute-start | bytes 393224 | tf_op jit(solution)/shard_map/ppermute | solution.py:308
  38.0 10.2 %collective-permute-start.2 = (bf16[2,2,16,1024]{3,2,1,0:T(8,128)(2,1)S(1)}, bf16[2,2,16,1024]{3,2,1,0:T(8,128)(2,1)S(1)}, u32[]{:S(2)}, u32[]{:S(2)}) collective-permute-start(bf16[2,2,16,1024]{3,2,1,0:T(8,128)(2,1)S(1)} %get-tuple-element.29), channel_id=1, source_target_pairs={{0,14},{1,15},{2,0},{3,1},{4,2},{5,3},{6,4},{7,5},{8,6},{9,7},{10,... | collective-permute-start | bytes 393224 | tf_op jit(solution)/shard_map/ppermute | solution.py:308
  116.1 50.3 %collective-permute-start.8 = (bf16[36,128,128]{2,1,0:T(8,128)(2,1)S(1)}, bf16[36,128,128]{2,1,0:T(8,128)(2,1)S(1)}, u32[]{:S(2)}, u32[]{:S(2)}) collective-permute-start(bf16[36,128,128]{2,1,0:T(8,128)(2,1)S(1)} %shard_map.116.grads_ref), channel_id=1, source_target_pairs={{0,256},{256,0},{1,257},{257,1},{2,258},{258,2},{3,259},{259,3},{4... | collective-permute-start | bytes 3538952 | tf_op jit(solution)/shard_map/ppermute | solution.py:330
  119.7 20.6 %collective-permute-start.4 = (bf16[4,16,16,128]{3,2,1,0:T(8,128)(2,1)S(1)}, bf16[4,16,16,128]{3,2,1,0:T(8,128)(2,1)S(1)}, u32[]{:S(2)}, u32[]{:S(2)}) collective-permute-start(bf16[4,16,16,128]{3,2,1,0:T(8,128)(2,1)S(1)} %get-tuple-element.24), channel_id=1, source_target_pairs={{0,1},{1,2},{2,3},{3,4},{4,5},{5,6},{6,7},{7,8},{8,9},{9,10},{10,1... | collective-permute-start | bytes 786440 | tf_op jit(solution)/shard_map/ppermute | solution.py:308
  121.6 18.7 %collective-permute-start.5 = (bf16[4,16,16,128]{3,2,1,0:T(8,128)(2,1)S(1)}, bf16[4,16,16,128]{3,2,1,0:T(8,128)(2,1)S(1)}, u32[]{:S(2)}, u32[]{:S(2)}) collective-permute-start(bf16[4,16,16,128]{3,2,1,0:T(8,128)(2,1)S(1)} %get-tuple-element.25), channel_id=1, source_target_pairs={{0,15},{1,0},{2,1},{3,2},{4,3},{5,4},{6,5},{7,6},{8,7},{9,8},{10,9... | collective-permute-start | bytes 786440 | tf_op jit(solution)/shard_map/ppermute | solution.py:308
  125.6 10.2 %collective-permute-start.6 = (bf16[2,16,16,128]{3,2,1,0:T(8,128)(2,1)S(1)}, bf16[2,16,16,128]{3,2,1,0:T(8,128)(2,1)S(1)}, u32[]{:S(2)}, u32[]{:S(2)}) collective-permute-start(bf16[2,16,16,128]{3,2,1,0:T(8,128)(2,1)S(1)} %get-tuple-element.26), channel_id=1, source_target_pairs={{0,2},{1,3},{2,4},{3,5},{4,6},{5,7},{6,8},{7,9},{8,10},{9,11},{10,... | collective-permute-start | bytes 393224 | tf_op jit(solution)/shard_map/ppermute | solution.py:308
  128.8 11.6 %collective-permute-start.7 = (bf16[2,16,16,128]{3,2,1,0:T(8,128)(2,1)S(1)}, bf16[2,16,16,128]{3,2,1,0:T(8,128)(2,1)S(1)}, u32[]{:S(2)}, u32[]{:S(2)}) collective-permute-start(bf16[2,16,16,128]{3,2,1,0:T(8,128)(2,1)S(1)} %get-tuple-element.27), channel_id=1, source_target_pairs={{0,14},{1,15},{2,0},{3,1},{4,2},{5,3},{6,4},{7,5},{8,6},{9,7},{10,... | collective-permute-start | bytes 393224 | tf_op jit(solution)/shard_map/ppermute | solution.py:308

commit v8 on v7

--- a/solution.py
+++ b/solution.py
@@ -11,6 +11,7 @@
 FEATURE = 8
 HIDDEN = 32
 NEAR = 4
+TOTALS = 4
 STEPS = (0, 1, -1, 2, -2)
 PLACES = (4, 4, 4, 2, 2)
 VMEM_BYTES = 12 * 1024 * 1024
@@ -129,7 +130,9 @@
     share = parts.shape[2]
     hidden_blocks = HIDDEN
 
-    def body(parts_ref, out_ref, pre, grad, act_blocks, grad_blocks, table, index, sem):
+    def body(parts_ref, out_ref, *refs):
+        pre, grad = refs[:TOTALS], refs[TOTALS : 2 * TOTALS]
+        act_blocks, grad_blocks, table, index, sem = refs[2 * TOTALS :]
         row = lax.broadcasted_iota(jnp.int32, (peers, width), 0)
         lines = jnp.zeros((peers, width), jnp.float32)
         for p in range(peers):
@@ -137,26 +140,26 @@
         table[...] = lines.astype(jnp.int32)
         copy = pltpu.make_async_copy(table, index, sem)
         copy.start()
-        pre[...] = jnp.zeros_like(pre)
-        grad[...] = jnp.zeros_like(grad)
+        for total in pre + grad:
+            total[...] = jnp.zeros_like(total)
         act_blocks[hidden_blocks:] = jnp.zeros((1, share, width), jnp.bfloat16)
         grad_blocks[hidden_blocks:] = jnp.zeros((1, share, width), jnp.bfloat16)
         copy.wait()
 
         def add(p, carry):
             for s in range(slots):
-                for half in range(2):
-                    q = p + half * (peers // 2)
+                for t in range(TOTALS):
+                    q = p + t * (peers // TOTALS)
                     i, j = index[q, s], index[q, 64 + s]
-                    pre[half, i] = pre[half, i] + parts_ref[q, s].astype(jnp.float32)
-                    grad[half, j] = grad[half, j] + parts_ref[q, slots + s].astype(jnp.float32)
+                    pre[t][i] = pre[t][i] + parts_ref[q, s].astype(jnp.float32)
+                    grad[t][j] = grad[t][j] + parts_ref[q, slots + s].astype(jnp.float32)
             return carry
 
-        lax.fori_loop(0, peers // 2, add, 0)
+        lax.fori_loop(0, peers // TOTALS, add, 0)
 
         def point(h, carry):
-            value = pre[0, h] + pre[1, h]
-            slope = grad[0, h] + grad[1, h]
+            value = sum(total[h] for total in pre[1:]) + pre[0][h]
+            slope = sum(total[h] for total in grad[1:]) + grad[0][h]
             gate = 1.0 / (1.0 + jnp.exp(-value))
             act_blocks[h] = (value * gate).astype(jnp.bfloat16)
             grad_blocks[h] = (slope * gate * (1.0 + value * (1.0 - gate))).astype(jnp.bfloat16)
@@ -177,8 +180,7 @@
         [VMEM()],
         jax.ShapeDtypeStruct((peers, 2 * slots, share, width), jnp.bfloat16),
         scratch=[
-            pltpu.VMEM((2, hidden_blocks + 1, share, width), jnp.float32),
-            pltpu.VMEM((2, hidden_blocks + 1, share, width), jnp.float32),
+            *[pltpu.VMEM((hidden_blocks + 1, share, width), jnp.float32)] * (2 * TOTALS),
             pltpu.VMEM((hidden_blocks + 1, share, width), jnp.bfloat16),
             pltpu.VMEM((hidden_blocks + 1, share, width), jnp.bfloat16),
             pltpu.VMEM((peers, width), jnp.int32),

time: 168 us -> 168 us (level)
  no operation moved by 1% of the time
where the time goes in v8:
time: 168 us; the launch traced here: 167 us
  blocking collectives  113 us (67%)
  starting transfers between devices  28 us (17%)
  waiting for transfers between devices  13.7 us (8%)
  Pallas kernels  9.65 us (6%)
  between operations  2.06 us (1%)
    all_to_all x3, blocking collectives, swap(): lax.all_to_all(parts, axis, split_axis=0, concat_axis=0, tiled=True, axis...  87.8 us
    ppermute x8, starting transfers between devices, send_on(): lax.ppermute(value, 'col', [(c, (c + hops) % peers) for c in range(peers)])  26.1 us
    all_gather x1, blocking collectives, on_device(): lax.all_gather(jnp.stack([tokens, cotangent]), 'col', axis_index_groups=far)  25 us
    ppermute x8, waiting for transfers between devices, send_on(): lax.ppermute(value, 'col', [(c, (c + hops) % peers) for c in range(peers)])  13.7 us
  transfers between devices with their start and end apart: 9, of which 3 were waited for; matrix products, arithmetic and copies ran while one was open for 0% of the time, Pallas kernels for 2%

profile of v8, /device:TPU:64, one launch (start us, length us, event | category | flops | bytes accessed | tf_op | source)
XLA Modules:
  0.0 167.0 jit_solution(15117732094250708696)
XLA Ops:
  0.6 0.8 pad_maximum_fusion
  1.4 25.0 %all-gather = bf16[8,16,1024]{2,1,0:T(8,128)(2,1)S(1)} all-gather(bf16[2,16,1024]{2,1,0:T(8,128)(2,1)S(1)} %pad_maximum_fusion), channel_id=2, replica_groups={{0,4,8,12},{1,5,9,13},{2,6,10,14},{3,7,11,15},{16,20,24,28},{17,21,25,2..., dimensions={0}, use_global_device_ids=true | all-gather | bytes 327680 | tf_op jit(solution)/shard_map/all_gather | solution.py:317
  26.4 3.4 %collective-permute-start.1 = (bf16[4,2,16,1024]{3,2,1,0:T(8,128)(2,1)S(1)}, bf16[4,2,16,1024]{3,2,1,0:T(8,128)(2,1)S(1)}, u32[]{:S(2)}, u32[]{:S(2)}) collective-permute-start(bf16[4,2,16,1024]{3,2,1,0:T(8,128)(2,1)S(1)} %bitcast.11), channel_id=1, source_target_pairs={{0,1},{1,2},{2,3},{3,4},{4,5},{5,6},{6,7},{7,8},{8,9},{9,10},{10,1... | collective-permute-start | bytes 786440 | tf_op jit(solution)/shard_map/ppermute | solution.py:310
  29.8 2.5 %collective-permute-start = (bf16[4,2,16,1024]{3,2,1,0:T(8,128)(2,1)S(1)}, bf16[4,2,16,1024]{3,2,1,0:T(8,128)(2,1)S(1)}, u32[]{:S(2)}, u32[]{:S(2)}) collective-permute-start(bf16[4,2,16,1024]{3,2,1,0:T(8,128)(2,1)S(1)} %bitcast.12), channel_id=1, source_target_pairs={{0,15},{1,0},{2,1},{3,2},{4,3},{5,4},{6,5},{7,6},{8,7},{9,8},{10,9... | collective-permute-start | bytes 786440 | tf_op jit(solution)/shard_map/ppermute | solution.py:310
  32.3 5.7 %collective-permute-start.3 = (bf16[2,2,16,1024]{3,2,1,0:T(8,128)(2,1)S(1)}, bf16[2,2,16,1024]{3,2,1,0:T(8,128)(2,1)S(1)}, u32[]{:S(2)}, u32[]{:S(2)}) collective-permute-start(bf16[2,2,16,1024]{3,2,1,0:T(8,128)(2,1)S(1)} %get-tuple-element.28), channel_id=1, source_target_pairs={{0,2},{1,3},{2,4},{3,5},{4,6},{5,7},{6,8},{7,9},{8,10},{9,11},{10,... | collective-permute-start | bytes 393224 | tf_op jit(solution)/shard_map/ppermute | solution.py:310
  38.0 1.9 %collective-permute-start.2 = (bf16[2,2,16,1024]{3,2,1,0:T(8,128)(2,1)S(1)}, bf16[2,2,16,1024]{3,2,1,0:T(8,128)(2,1)S(1)}, u32[]{:S(2)}, u32[]{:S(2)}) collective-permute-start(bf16[2,2,16,1024]{3,2,1,0:T(8,128)(2,1)S(1)} %get-tuple-element.29), channel_id=1, source_target_pairs={{0,14},{1,15},{2,0},{3,1},{4,2},{5,3},{6,4},{7,5},{8,6},{9,7},{10,... | collective-permute-start | bytes 393224 | tf_op jit(solution)/shard_map/ppermute | solution.py:310
  41.3 1.3 shard_map.111
  42.5 0.0 collective-permute-done.3.refs_4_
  42.6 5.7 %collective-permute-done.2.refs_3_ = bf16[2,2,16,1024]{3,2,1,0:T(8,128)(2,1)S(1)} collective-permute-done((bf16[2,2,16,1024]{3,2,1,0:T(8,128)(2,1)S(1)}, bf16[2,2,16,1024]{3,2,1,0:T(8,128)(2,1)S(1)}, u32[]{:S(2)}, u32[]{:S(2)}) %collective-permute-start.2) | collective-permute-done | bytes 131104 | tf_op jit(solution)/shard_map/ppermute | solution.py:310
  48.3 0.0 collective-permute-done.1.refs_2_
  48.3 0.0 collective-permute-done.refs_1_
  48.3 1.4 shard_map.112
  49.7 33.5 %all_to_all.15.parts_ref = bf16[16,37,16,128]{3,2,1,0:T(8,128)(2,1)S(1)} all-to-all(bf16[16,37,16,128]{3,2,1,0:T(8,128)(2,1)S(1)} %shard_map.112), channel_id=1, replica_groups=mesh['tok'=2,'row'=16,'col'=16] {'row'}, dimensions={0} | all-to-all | bytes 4849664 | tf_op jit(solution)/shard_map/all_to_all | solution.py:303
  83.2 2.4 %shard_map.113 = bf16[16,36,16,128]{3,2,1,0:T(8,128)(2,1)S(1)} custom-call(bf16[16,37,16,128]{3,2,1,0:T(8,128)(2,1)S(1)} %all_to_all.15.parts_ref), custom_call_target="tpu_custom_call" | custom-call | flops 4849664 | bytes 7274496 | tf_op jit(solution)/shard_map/pallas_call | solution.py:178
  85.6 28.3 %all_to_all.16.in_ref.refs_5_ = bf16[16,36,16,128]{3,2,1,0:T(8,128)(2,1)S(1)} all-to-all(bf16[16,36,16,128]{3,2,1,0:T(8,128)(2,1)S(1)} %shard_map.113), channel_id=1, replica_groups=mesh['tok'=2,'row'=16,'col'=16] {'row'}, dimensions={0} | all-to-all | bytes 4718592 | tf_op jit(solution)/shard_map/all_to_all | solution.py:303
  113.9 1.5 shard_map.116.grads_ref
  115.4 1.9 %collective-permute-start.8 = (bf16[36,128,128]{2,1,0:T(8,128)(2,1)S(1)}, bf16[36,128,128]{2,1,0:T(8,128)(2,1)S(1)}, u32[]{:S(2)}, u32[]{:S(2)}) collective-permute-start(bf16[36,128,128]{2,1,0:T(8,128)(2,1)S(1)} %shard_map.116.grads_ref), channel_id=1, source_target_pairs={{0,256},{256,0},{1,257},{257,1},{2,258},{258,2},{3,259},{259,3},{4... | collective-permute-start | bytes 3538952 | tf_op jit(solution)/shard_map/ppermute | solution.py:332
  117.4 1.7 shard_map.114
  119.0 1.9 %collective-permute-start.4 = (bf16[4,16,16,128]{3,2,1,0:T(8,128)(2,1)S(1)}, bf16[4,16,16,128]{3,2,1,0:T(8,128)(2,1)S(1)}, u32[]{:S(2)}, u32[]{:S(2)}) collective-permute-start(bf16[4,16,16,128]{3,2,1,0:T(8,128)(2,1)S(1)} %get-tuple-element.24), channel_id=1, source_target_pairs={{0,1},{1,2},{2,3},{3,4},{4,5},{5,6},{6,7},{7,8},{8,9},{9,10},{10,1... | collective-permute-start | bytes 786440 | tf_op jit(solution)/shard_map/ppermute | solution.py:310
  121.0 3.9 %collective-permute-start.5 = (bf16[4,16,16,128]{3,2,1,0:T(8,128)(2,1)S(1)}, bf16[4,16,16,128]{3,2,1,0:T(8,128)(2,1)S(1)}, u32[]{:S(2)}, u32[]{:S(2)}) collective-permute-start(bf16[4,16,16,128]{3,2,1,0:T(8,128)(2,1)S(1)} %get-tuple-element.25), channel_id=1, source_target_pairs={{0,15},{1,0},{2,1},{3,2},{4,3},{5,4},{6,5},{7,6},{8,7},{9,8},{10,9... | collective-permute-start | bytes 786440 | tf_op jit(solution)/shard_map/ppermute | solution.py:310
  124.9 3.2 %collective-permute-start.6 = (bf16[2,16,16,128]{3,2,1,0:T(8,128)(2,1)S(1)}, bf16[2,16,16,128]{3,2,1,0:T(8,128)(2,1)S(1)}, u32[]{:S(2)}, u32[]{:S(2)}) collective-permute-start(bf16[2,16,16,128]{3,2,1,0:T(8,128)(2,1)S(1)} %get-tuple-element.26), channel_id=1, source_target_pairs={{0,2},{1,3},{2,4},{3,5},{4,6},{5,7},{6,8},{7,9},{8,10},{9,11},{10,... | collective-permute-start | bytes 393224 | tf_op jit(solution)/shard_map/ppermute | solution.py:310
  128.1 3.6 %collective-permute-start.7 = (bf16[2,16,16,128]{3,2,1,0:T(8,128)(2,1)S(1)}, bf16[2,16,16,128]{3,2,1,0:T(8,128)(2,1)S(1)}, u32[]{:S(2)}, u32[]{:S(2)}) collective-permute-start(bf16[2,16,16,128]{3,2,1,0:T(8,128)(2,1)S(1)} %get-tuple-element.27), channel_id=1, source_target_pairs={{0,14},{1,15},{2,0},{3,1},{4,2},{5,3},{6,4},{7,5},{8,6},{9,7},{10,... | collective-permute-start | bytes 393224 | tf_op jit(solution)/shard_map/ppermute | solution.py:310
  131.7 3.3 %collective-permute-done.6.refs_3_ = bf16[2,16,16,128]{3,2,1,0:T(8,128)(2,1)S(1)} collective-permute-done((bf16[2,16,16,128]{3,2,1,0:T(8,128)(2,1)S(1)}, bf16[2,16,16,128]{3,2,1,0:T(8,128)(2,1)S(1)}, u32[]{:S(2)}, u32[]{:S(2)}) %collective-permute-start.6) | collective-permute-done | bytes 131104 | tf_op jit(solution)/shard_map/ppermute | solution.py:310
  135.0 4.7 %collective-permute-done.7.refs_4_ = bf16[2,16,16,128]{3,2,1,0:T(8,128)(2,1)S(1)} collective-permute-done((bf16[2,16,16,128]{3,2,1,0:T(8,128)(2,1)S(1)}, bf16[2,16,16,128]{3,2,1,0:T(8,128)(2,1)S(1)}, u32[]{:S(2)}, u32[]{:S(2)}) %collective-permute-start.7) | collective-permute-done | bytes 131104 | tf_op jit(solution)/shard_map/ppermute | solution.py:310
  139.7 0.0 collective-permute-done.4.refs_1_
  139.7 0.0 collective-permute-done.5.refs_2_
  139.7 0.1 shard_map.115
  139.8 26.0 %all_to_all.17.parts_ref = bf16[4,16,16,128]{3,2,1,0:T(8,128)(2,1)S(1)} all-to-all(bf16[4,16,16,128]{3,2,1,0:T(8,128)(2,1)S(1)} %shard_map.115), channel_id=1, replica_groups={{0,4,8,12},{1,5,9,13},{2,6,10,14},{3,7,11,15},{16,20,24,28},{17,21,25,2..., dimensions={0} | all-to-all | bytes 524288 | tf_op jit(solution)/shard_map/all_to_all | solution.py:303
  165.8 0.0 collective-permute-done.8.others_ref
  165.8 1.3 shard_map.117
  (1 shorter events, 0.0 us)
Async XLA Ops:
  26.4 21.9 %collective-permute-start.1 = (bf16[4,2,16,1024]{3,2,1,0:T(8,128)(2,1)S(1)}, bf16[4,2,16,1024]{3,2,1,0:T(8,128)(2,1)S(1)}, u32[]{:S(2)}, u32[]{:S(2)}) collective-permute-start(bf16[4,2,16,1024]{3,2,1,0:T(8,128)(2,1)S(1)} %bitcast.11), channel_id=1, source_target_pairs={{0,1},{1,2},{2,3},{3,4},{4,5},{5,6},{6,7},{7,8},{8,9},{9,10},{10,1... | collective-permute-start | bytes 786440 | tf_op jit(solution)/shard_map/ppermute | solution.py:310
  29.8 18.5 %collective-permute-start = (bf16[4,2,16,1024]{3,2,1,0:T(8,128)(2,1)S(1)}, bf16[4,2,16,1024]{3,2,1,0:T(8,128)(2,1)S(1)}, u32[]{:S(2)}, u32[]{:S(2)}) collective-permute-start(bf16[4,2,16,1024]{3,2,1,0:T(8,128)(2,1)S(1)} %bitcast.12), channel_id=1, source_target_pairs={{0,15},{1,0},{2,1},{3,2},{4,3},{5,4},{6,5},{7,6},{8,7},{9,8},{10,9... | collective-permute-start | bytes 786440 | tf_op jit(solution)/shard_map/ppermute | solution.py:310
  32.3 10.3 %collective-permute-start.3 = (bf16[2,2,16,1024]{3,2,1,0:T(8,128)(2,1)S(1)}, bf16[2,2,16,1024]{3,2,1,0:T(8,128)(2,1)S(1)}, u32[]{:S(2)}, u32[]{:S(2)}) collective-permute-start(bf16[2,2,16,1024]{3,2,1,0:T(8,128)(2,1)S(1)} %get-tuple-element.28), channel_id=1, source_target_pairs={{0,2},{1,3},{2,4},{3,5},{4,6},{5,7},{6,8},{7,9},{8,10},{9,11},{10,... | collective-permute-start | bytes 393224 | tf_op jit(solution)/shard_map/ppermute | solution.py:310
  38.0 10.2 %collective-permute-start.2 = (bf16[2,2,16,1024]{3,2,1,0:T(8,128)(2,1)S(1)}, bf16[2,2,16,1024]{3,2,1,0:T(8,128)(2,1)S(1)}, u32[]{:S(2)}, u32[]{:S(2)}) collective-permute-start(bf16[2,2,16,1024]{3,2,1,0:T(8,128)(2,1)S(1)} %get-tuple-element.29), channel_id=1, source_target_pairs={{0,14},{1,15},{2,0},{3,1},{4,2},{5,3},{6,4},{7,5},{8,6},{9,7},{10,... | collective-permute-start | bytes 393224 | tf_op jit(solution)/shard_map/ppermute | solution.py:310
  115.4 50.3 %collective-permute-start.8 = (bf16[36,128,128]{2,1,0:T(8,128)(2,1)S(1)}, bf16[36,128,128]{2,1,0:T(8,128)(2,1)S(1)}, u32[]{:S(2)}, u32[]{:S(2)}) collective-permute-start(bf16[36,128,128]{2,1,0:T(8,128)(2,1)S(1)} %shard_map.116.grads_ref), channel_id=1, source_target_pairs={{0,256},{256,0},{1,257},{257,1},{2,258},{258,2},{3,259},{259,3},{4... | collective-permute-start | bytes 3538952 | tf_op jit(solution)/shard_map/ppermute | solution.py:332
  119.0 20.6 %collective-permute-start.4 = (bf16[4,16,16,128]{3,2,1,0:T(8,128)(2,1)S(1)}, bf16[4,16,16,128]{3,2,1,0:T(8,128)(2,1)S(1)}, u32[]{:S(2)}, u32[]{:S(2)}) collective-permute-start(bf16[4,16,16,128]{3,2,1,0:T(8,128)(2,1)S(1)} %get-tuple-element.24), channel_id=1, source_target_pairs={{0,1},{1,2},{2,3},{3,4},{4,5},{5,6},{6,7},{7,8},{8,9},{9,10},{10,1... | collective-permute-start | bytes 786440 | tf_op jit(solution)/shard_map/ppermute | solution.py:310
  121.0 18.7 %collective-permute-start.5 = (bf16[4,16,16,128]{3,2,1,0:T(8,128)(2,1)S(1)}, bf16[4,16,16,128]{3,2,1,0:T(8,128)(2,1)S(1)}, u32[]{:S(2)}, u32[]{:S(2)}) collective-permute-start(bf16[4,16,16,128]{3,2,1,0:T(8,128)(2,1)S(1)} %get-tuple-element.25), channel_id=1, source_target_pairs={{0,15},{1,0},{2,1},{3,2},{4,3},{5,4},{6,5},{7,6},{8,7},{9,8},{10,9... | collective-permute-start | bytes 786440 | tf_op jit(solution)/shard_map/ppermute | solution.py:310
  124.9 10.1 %collective-permute-start.6 = (bf16[2,16,16,128]{3,2,1,0:T(8,128)(2,1)S(1)}, bf16[2,16,16,128]{3,2,1,0:T(8,128)(2,1)S(1)}, u32[]{:S(2)}, u32[]{:S(2)}) collective-permute-start(bf16[2,16,16,128]{3,2,1,0:T(8,128)(2,1)S(1)} %get-tuple-element.26), channel_id=1, source_target_pairs={{0,2},{1,3},{2,4},{3,5},{4,6},{5,7},{6,8},{7,9},{8,10},{9,11},{10,... | collective-permute-start | bytes 393224 | tf_op jit(solution)/shard_map/ppermute | solution.py:310
  128.1 11.6 %collective-permute-start.7 = (bf16[2,16,16,128]{3,2,1,0:T(8,128)(2,1)S(1)}, bf16[2,16,16,128]{3,2,1,0:T(8,128)(2,1)S(1)}, u32[]{:S(2)}, u32[]{:S(2)}) collective-permute-start(bf16[2,16,16,128]{3,2,1,0:T(8,128)(2,1)S(1)} %get-tuple-element.27), channel_id=1, source_target_pairs={{0,14},{1,15},{2,0},{3,1},{4,2},{5,3},{6,4},{7,5},{8,6},{9,7},{10,... | collective-permute-start | bytes 393224 | tf_op jit(solution)/shard_map/ppermute | solution.py:310

commit v9 on v8

--- a/solution.py
+++ b/solution.py
@@ -155,7 +155,7 @@
                     grad[t][j] = grad[t][j] + parts_ref[q, slots + s].astype(jnp.float32)
             return carry
 
-        lax.fori_loop(0, peers // TOTALS, add, 0)
+        lax.fori_loop(0, peers // TOTALS, add, 0, unroll=True)
 
         def point(h, carry):
             value = sum(total[h] for total in pre[1:]) + pre[0][h]
@@ -173,7 +173,7 @@
                 out_ref[p, slots + s] = grad_blocks[index[p, s]]
             return carry
 
-        lax.fori_loop(0, peers, pick, 0)
+        lax.fori_loop(0, peers, pick, 0, unroll=True)
 
     return call(
         body,

time: 168 us -> 167 us (level)
  no operation moved by 1% of the time
where the time goes in v9:
time: 167 us
  blocking collectives  113 us (68%)
  starting transfers between devices  28 us (17%)
  waiting for transfers between devices  13.7 us (8%)
  Pallas kernels  9.33 us (6%)
  between operations  2.06 us (1%)
    all_to_all x3, blocking collectives, swap(): lax.all_to_all(parts, axis, split_axis=0, concat_axis=0, tiled=True, axis...  87.7 us
    ppermute x8, starting transfers between devices, send_on(): lax.ppermute(value, 'col', [(c, (c + hops) % peers) for c in range(peers)])  26.1 us
    all_gather x1, blocking collectives, on_device(): lax.all_gather(jnp.stack([tokens, cotangent]), 'col', axis_index_groups=far)  25 us
    ppermute x8, waiting for transfers between devices, send_on(): lax.ppermute(value, 'col', [(c, (c + hops) % peers) for c in range(peers)])  13.7 us
  transfers between devices with their start and end apart: 9, of which 3 were waited for; matrix products, arithmetic and copies ran while one was open for 0% of the time, Pallas kernels for 2%

profile of v9, /device:TPU:64, one launch (start us, length us, event | category | flops | bytes accessed | tf_op | source)
XLA Modules:
  0.0 166.6 jit_solution(8711979474930763119)
XLA Ops:
  0.6 0.8 pad_maximum_fusion
  1.4 25.0 %all-gather = bf16[8,16,1024]{2,1,0:T(8,128)(2,1)S(1)} all-gather(bf16[2,16,1024]{2,1,0:T(8,128)(2,1)S(1)} %pad_maximum_fusion), channel_id=2, replica_groups={{0,4,8,12},{1,5,9,13},{2,6,10,14},{3,7,11,15},{16,20,24,28},{17,21,25,2..., dimensions={0}, use_global_device_ids=true | all-gather | bytes 327680 | tf_op jit(solution)/shard_map/all_gather | solution.py:317
  26.4 3.4 %collective-permute-start.1 = (bf16[4,2,16,1024]{3,2,1,0:T(8,128)(2,1)S(1)}, bf16[4,2,16,1024]{3,2,1,0:T(8,128)(2,1)S(1)}, u32[]{:S(2)}, u32[]{:S(2)}) collective-permute-start(bf16[4,2,16,1024]{3,2,1,0:T(8,128)(2,1)S(1)} %bitcast.11), channel_id=1, source_target_pairs={{0,1},{1,2},{2,3},{3,4},{4,5},{5,6},{6,7},{7,8},{8,9},{9,10},{10,1... | collective-permute-start | bytes 786440 | tf_op jit(solution)/shard_map/ppermute | solution.py:310
  29.8 2.5 %collective-permute-start = (bf16[4,2,16,1024]{3,2,1,0:T(8,128)(2,1)S(1)}, bf16[4,2,16,1024]{3,2,1,0:T(8,128)(2,1)S(1)}, u32[]{:S(2)}, u32[]{:S(2)}) collective-permute-start(bf16[4,2,16,1024]{3,2,1,0:T(8,128)(2,1)S(1)} %bitcast.12), channel_id=1, source_target_pairs={{0,15},{1,0},{2,1},{3,2},{4,3},{5,4},{6,5},{7,6},{8,7},{9,8},{10,9... | collective-permute-start | bytes 786440 | tf_op jit(solution)/shard_map/ppermute | solution.py:310
  32.3 5.7 %collective-permute-start.3 = (bf16[2,2,16,1024]{3,2,1,0:T(8,128)(2,1)S(1)}, bf16[2,2,16,1024]{3,2,1,0:T(8,128)(2,1)S(1)}, u32[]{:S(2)}, u32[]{:S(2)}) collective-permute-start(bf16[2,2,16,1024]{3,2,1,0:T(8,128)(2,1)S(1)} %get-tuple-element.28), channel_id=1, source_target_pairs={{0,2},{1,3},{2,4},{3,5},{4,6},{5,7},{6,8},{7,9},{8,10},{9,11},{10,... | collective-permute-start | bytes 393224 | tf_op jit(solution)/shard_map/ppermute | solution.py:310
  38.0 1.9 %collective-permute-start.2 = (bf16[2,2,16,1024]{3,2,1,0:T(8,128)(2,1)S(1)}, bf16[2,2,16,1024]{3,2,1,0:T(8,128)(2,1)S(1)}, u32[]{:S(2)}, u32[]{:S(2)}) collective-permute-start(bf16[2,2,16,1024]{3,2,1,0:T(8,128)(2,1)S(1)} %get-tuple-element.29), channel_id=1, source_target_pairs={{0,14},{1,15},{2,0},{3,1},{4,2},{5,3},{6,4},{7,5},{8,6},{9,7},{10,... | collective-permute-start | bytes 393224 | tf_op jit(solution)/shard_map/ppermute | solution.py:310
  41.3 1.3 shard_map.111
  42.5 0.0 collective-permute-done.3.refs_4_
  42.6 5.7 %collective-permute-done.2.refs_3_ = bf16[2,2,16,1024]{3,2,1,0:T(8,128)(2,1)S(1)} collective-permute-done((bf16[2,2,16,1024]{3,2,1,0:T(8,128)(2,1)S(1)}, bf16[2,2,16,1024]{3,2,1,0:T(8,128)(2,1)S(1)}, u32[]{:S(2)}, u32[]{:S(2)}) %collective-permute-start.2) | collective-permute-done | bytes 131104 | tf_op jit(solution)/shard_map/ppermute | solution.py:310
  48.3 0.0 collective-permute-done.1.refs_2_
  48.3 0.0 collective-permute-done.refs_1_
  48.3 1.4 shard_map.112
  49.7 33.5 %all_to_all.15.parts_ref = bf16[16,37,16,128]{3,2,1,0:T(8,128)(2,1)S(1)} all-to-all(bf16[16,37,16,128]{3,2,1,0:T(8,128)(2,1)S(1)} %shard_map.112), channel_id=1, replica_groups=mesh['tok'=2,'row'=16,'col'=16] {'row'}, dimensions={0} | all-to-all | bytes 4849664 | tf_op jit(solution)/shard_map/all_to_all | solution.py:303
  83.2 2.1 %shard_map.113 = bf16[16,36,16,128]{3,2,1,0:T(8,128)(2,1)S(1)} custom-call(bf16[16,37,16,128]{3,2,1,0:T(8,128)(2,1)S(1)} %all_to_all.15.parts_ref), custom_call_target="tpu_custom_call" | custom-call | flops 4849664 | bytes 7274496 | tf_op jit(solution)/shard_map/pallas_call | solution.py:178
  85.3 28.3 %all_to_all.16.in_ref.refs_5_ = bf16[16,36,16,128]{3,2,1,0:T(8,128)(2,1)S(1)} all-to-all(bf16[16,36,16,128]{3,2,1,0:T(8,128)(2,1)S(1)} %shard_map.113), channel_id=1, replica_groups=mesh['tok'=2,'row'=16,'col'=16] {'row'}, dimensions={0} | all-to-all | bytes 4718592 | tf_op jit(solution)/shard_map/all_to_all | solution.py:303
  113.6 1.5 shard_map.116.grads_ref
  115.1 1.9 %collective-permute-start.8 = (bf16[36,128,128]{2,1,0:T(8,128)(2,1)S(1)}, bf16[36,128,128]{2,1,0:T(8,128)(2,1)S(1)}, u32[]{:S(2)}, u32[]{:S(2)}) collective-permute-start(bf16[36,128,128]{2,1,0:T(8,128)(2,1)S(1)} %shard_map.116.grads_ref), channel_id=1, source_target_pairs={{0,256},{256,0},{1,257},{257,1},{2,258},{258,2},{3,259},{259,3},{4... | collective-permute-start | bytes 3538952 | tf_op jit(solution)/shard_map/ppermute | solution.py:332
  117.0 1.7 shard_map.114
  118.7 1.9 %collective-permute-start.4 = (bf16[4,16,16,128]{3,2,1,0:T(8,128)(2,1)S(1)}, bf16[4,16,16,128]{3,2,1,0:T(8,128)(2,1)S(1)}, u32[]{:S(2)}, u32[]{:S(2)}) collective-permute-start(bf16[4,16,16,128]{3,2,1,0:T(8,128)(2,1)S(1)} %get-tuple-element.24), channel_id=1, source_target_pairs={{0,1},{1,2},{2,3},{3,4},{4,5},{5,6},{6,7},{7,8},{8,9},{9,10},{10,1... | collective-permute-start | bytes 786440 | tf_op jit(solution)/shard_map/ppermute | solution.py:310
  120.6 3.9 %collective-permute-start.5 = (bf16[4,16,16,128]{3,2,1,0:T(8,128)(2,1)S(1)}, bf16[4,16,16,128]{3,2,1,0:T(8,128)(2,1)S(1)}, u32[]{:S(2)}, u32[]{:S(2)}) collective-permute-start(bf16[4,16,16,128]{3,2,1,0:T(8,128)(2,1)S(1)} %get-tuple-element.25), channel_id=1, source_target_pairs={{0,15},{1,0},{2,1},{3,2},{4,3},{5,4},{6,5},{7,6},{8,7},{9,8},{10,9... | collective-permute-start | bytes 786440 | tf_op jit(solution)/shard_map/ppermute | solution.py:310
  124.6 3.2 %collective-permute-start.6 = (bf16[2,16,16,128]{3,2,1,0:T(8,128)(2,1)S(1)}, bf16[2,16,16,128]{3,2,1,0:T(8,128)(2,1)S(1)}, u32[]{:S(2)}, u32[]{:S(2)}) collective-permute-start(bf16[2,16,16,128]{3,2,1,0:T(8,128)(2,1)S(1)} %get-tuple-element.26), channel_id=1, source_target_pairs={{0,2},{1,3},{2,4},{3,5},{4,6},{5,7},{6,8},{7,9},{8,10},{9,11},{10,... | collective-permute-start | bytes 393224 | tf_op jit(solution)/shard_map/ppermute | solution.py:310
  127.8 3.6 %collective-permute-start.7 = (bf16[2,16,16,128]{3,2,1,0:T(8,128)(2,1)S(1)}, bf16[2,16,16,128]{3,2,1,0:T(8,128)(2,1)S(1)}, u32[]{:S(2)}, u32[]{:S(2)}) collective-permute-start(bf16[2,16,16,128]{3,2,1,0:T(8,128)(2,1)S(1)} %get-tuple-element.27), channel_id=1, source_target_pairs={{0,14},{1,15},{2,0},{3,1},{4,2},{5,3},{6,4},{7,5},{8,6},{9,7},{10,... | collective-permute-start | bytes 393224 | tf_op jit(solution)/shard_map/ppermute | solution.py:310
  131.3 3.4 %collective-permute-done.6.refs_3_ = bf16[2,16,16,128]{3,2,1,0:T(8,128)(2,1)S(1)} collective-permute-done((bf16[2,16,16,128]{3,2,1,0:T(8,128)(2,1)S(1)}, bf16[2,16,16,128]{3,2,1,0:T(8,128)(2,1)S(1)}, u32[]{:S(2)}, u32[]{:S(2)}) %collective-permute-start.6) | collective-permute-done | bytes 131104 | tf_op jit(solution)/shard_map/ppermute | solution.py:310
  134.8 4.6 %collective-permute-done.7.refs_4_ = bf16[2,16,16,128]{3,2,1,0:T(8,128)(2,1)S(1)} collective-permute-done((bf16[2,16,16,128]{3,2,1,0:T(8,128)(2,1)S(1)}, bf16[2,16,16,128]{3,2,1,0:T(8,128)(2,1)S(1)}, u32[]{:S(2)}, u32[]{:S(2)}) %collective-permute-start.7) | collective-permute-done | bytes 131104 | tf_op jit(solution)/shard_map/ppermute | solution.py:310
  139.3 0.0 collective-permute-done.4.refs_1_
  139.3 0.0 collective-permute-done.5.refs_2_
  139.3 0.1 shard_map.115
  139.5 25.9 %all_to_all.17.parts_ref = bf16[4,16,16,128]{3,2,1,0:T(8,128)(2,1)S(1)} all-to-all(bf16[4,16,16,128]{3,2,1,0:T(8,128)(2,1)S(1)} %shard_map.115), channel_id=1, replica_groups={{0,4,8,12},{1,5,9,13},{2,6,10,14},{3,7,11,15},{16,20,24,28},{17,21,25,2..., dimensions={0} | all-to-all | bytes 524288 | tf_op jit(solution)/shard_map/all_to_all | solution.py:303
  165.4 0.0 collective-permute-done.8.others_ref
  165.4 1.3 shard_map.117
  (1 shorter events, 0.0 us)
Async XLA Ops:
  26.4 21.9 %collective-permute-start.1 = (bf16[4,2,16,1024]{3,2,1,0:T(8,128)(2,1)S(1)}, bf16[4,2,16,1024]{3,2,1,0:T(8,128)(2,1)S(1)}, u32[]{:S(2)}, u32[]{:S(2)}) collective-permute-start(bf16[4,2,16,1024]{3,2,1,0:T(8,128)(2,1)S(1)} %bitcast.11), channel_id=1, source_target_pairs={{0,1},{1,2},{2,3},{3,4},{4,5},{5,6},{6,7},{7,8},{8,9},{9,10},{10,1... | collective-permute-start | bytes 786440 | tf_op jit(solution)/shard_map/ppermute | solution.py:310
  29.8 18.5 %collective-permute-start = (bf16[4,2,16,1024]{3,2,1,0:T(8,128)(2,1)S(1)}, bf16[4,2,16,1024]{3,2,1,0:T(8,128)(2,1)S(1)}, u32[]{:S(2)}, u32[]{:S(2)}) collective-permute-start(bf16[4,2,16,1024]{3,2,1,0:T(8,128)(2,1)S(1)} %bitcast.12), channel_id=1, source_target_pairs={{0,15},{1,0},{2,1},{3,2},{4,3},{5,4},{6,5},{7,6},{8,7},{9,8},{10,9... | collective-permute-start | bytes 786440 | tf_op jit(solution)/shard_map/ppermute | solution.py:310
  32.3 10.3 %collective-permute-start.3 = (bf16[2,2,16,1024]{3,2,1,0:T(8,128)(2,1)S(1)}, bf16[2,2,16,1024]{3,2,1,0:T(8,128)(2,1)S(1)}, u32[]{:S(2)}, u32[]{:S(2)}) collective-permute-start(bf16[2,2,16,1024]{3,2,1,0:T(8,128)(2,1)S(1)} %get-tuple-element.28), channel_id=1, source_target_pairs={{0,2},{1,3},{2,4},{3,5},{4,6},{5,7},{6,8},{7,9},{8,10},{9,11},{10,... | collective-permute-start | bytes 393224 | tf_op jit(solution)/shard_map/ppermute | solution.py:310
  38.0 10.2 %collective-permute-start.2 = (bf16[2,2,16,1024]{3,2,1,0:T(8,128)(2,1)S(1)}, bf16[2,2,16,1024]{3,2,1,0:T(8,128)(2,1)S(1)}, u32[]{:S(2)}, u32[]{:S(2)}) collective-permute-start(bf16[2,2,16,1024]{3,2,1,0:T(8,128)(2,1)S(1)} %get-tuple-element.29), channel_id=1, source_target_pairs={{0,14},{1,15},{2,0},{3,1},{4,2},{5,3},{6,4},{7,5},{8,6},{9,7},{10,... | collective-permute-start | bytes 393224 | tf_op jit(solution)/shard_map/ppermute | solution.py:310
  115.1 50.3 %collective-permute-start.8 = (bf16[36,128,128]{2,1,0:T(8,128)(2,1)S(1)}, bf16[36,128,128]{2,1,0:T(8,128)(2,1)S(1)}, u32[]{:S(2)}, u32[]{:S(2)}) collective-permute-start(bf16[36,128,128]{2,1,0:T(8,128)(2,1)S(1)} %shard_map.116.grads_ref), channel_id=1, source_target_pairs={{0,256},{256,0},{1,257},{257,1},{2,258},{258,2},{3,259},{259,3},{4... | collective-permute-start | bytes 3538952 | tf_op jit(solution)/shard_map/ppermute | solution.py:332
  118.7 20.6 %collective-permute-start.4 = (bf16[4,16,16,128]{3,2,1,0:T(8,128)(2,1)S(1)}, bf16[4,16,16,128]{3,2,1,0:T(8,128)(2,1)S(1)}, u32[]{:S(2)}, u32[]{:S(2)}) collective-permute-start(bf16[4,16,16,128]{3,2,1,0:T(8,128)(2,1)S(1)} %get-tuple-element.24), channel_id=1, source_target_pairs={{0,1},{1,2},{2,3},{3,4},{4,5},{5,6},{6,7},{7,8},{8,9},{9,10},{10,1... | collective-permute-start | bytes 786440 | tf_op jit(solution)/shard_map/ppermute | solution.py:310
  120.6 18.7 %collective-permute-start.5 = (bf16[4,16,16,128]{3,2,1,0:T(8,128)(2,1)S(1)}, bf16[4,16,16,128]{3,2,1,0:T(8,128)(2,1)S(1)}, u32[]{:S(2)}, u32[]{:S(2)}) collective-permute-start(bf16[4,16,16,128]{3,2,1,0:T(8,128)(2,1)S(1)} %get-tuple-element.25), channel_id=1, source_target_pairs={{0,15},{1,0},{2,1},{3,2},{4,3},{5,4},{6,5},{7,6},{8,7},{9,8},{10,9... | collective-permute-start | bytes 786440 | tf_op jit(solution)/shard_map/ppermute | solution.py:310
  124.6 10.2 %collective-permute-start.6 = (bf16[2,16,16,128]{3,2,1,0:T(8,128)(2,1)S(1)}, bf16[2,16,16,128]{3,2,1,0:T(8,128)(2,1)S(1)}, u32[]{:S(2)}, u32[]{:S(2)}) collective-permute-start(bf16[2,16,16,128]{3,2,1,0:T(8,128)(2,1)S(1)} %get-tuple-element.26), channel_id=1, source_target_pairs={{0,2},{1,3},{2,4},{3,5},{4,6},{5,7},{6,8},{7,9},{8,10},{9,11},{10,... | collective-permute-start | bytes 393224 | tf_op jit(solution)/shard_map/ppermute | solution.py:310
  127.8 11.6 %collective-permute-start.7 = (bf16[2,16,16,128]{3,2,1,0:T(8,128)(2,1)S(1)}, bf16[2,16,16,128]{3,2,1,0:T(8,128)(2,1)S(1)}, u32[]{:S(2)}, u32[]{:S(2)}) collective-permute-start(bf16[2,16,16,128]{3,2,1,0:T(8,128)(2,1)S(1)} %get-tuple-element.27), channel_id=1, source_target_pairs={{0,14},{1,15},{2,0},{3,1},{4,2},{5,3},{6,4},{7,5},{8,6},{9,7},{10,... | collective-permute-start | bytes 393224 | tf_op jit(solution)/shard_map/ppermute | solution.py:310

commit v10 on v9

--- a/solution.py
+++ b/solution.py
@@ -328,9 +328,11 @@
     slots_in = swap(hidden_step(parts), "row")
     sums = feature_sums(slots_in, first, second, feature)
     sums = [sums[0]] + [send_on(part, step) for part, step in zip(sums[1:], STEPS[1:])]
+    sums = near_sums(sums)
+    sums, slots_in = lax.optimization_barrier((sums, slots_in))
     grads = block_grads(rows, slots_in, feature)
     others = lax.ppermute(grads, "tok", [(0, 1), (1, 0)])
-    sums = swap(near_sums(sums), "col", far)
+    sums = swap(sums, "col", far)
     return final_sums(sums, grads, others)
 
 

time: 167 us -> 167 us (level)
  transfers between devices with their start and end apart: 9 -> 9, of which waited for: 3 -> 3; matrix products, arithmetic and copies ran while one was open for 0% -> 0% of each run, Pallas kernels for 2% -> 1%
where the time goes in v10:
time: 167 us; the launch traced here: 166 us
  blocking collectives  114 us (68%)
  starting transfers between devices  28 us (17%)
  waiting for transfers between devices  12.3 us (7%)
  Pallas kernels  9.37 us (6%)
  between operations  2.06 us (1%)
    all_to_all x3, blocking collectives, swap(): lax.all_to_all(parts, axis, split_axis=0, concat_axis=0, tiled=True, axis...  88.7 us
    ppermute x8, starting transfers between devices, send_on(): lax.ppermute(value, 'col', [(c, (c + hops) % peers) for c in range(peers)])  26.1 us
    all_gather x1, blocking collectives, on_device(): lax.all_gather(jnp.stack([tokens, cotangent]), 'col', axis_index_groups=far)  25 us
    ppermute x8, waiting for transfers between devices, send_on(): lax.ppermute(value, 'col', [(c, (c + hops) % peers) for c in range(peers)])  12.3 us
  transfers between devices with their start and end apart: 9, of which 3 were waited for; matrix products, arithmetic and copies ran while one was open for 0% of the time, Pallas kernels for 1%

profile of v10, /device:TPU:64, one launch (start us, length us, event | category | flops | bytes accessed | tf_op | source)
XLA Modules:
  0.0 166.2 jit_solution(12123155484000906591)
XLA Ops:
  0.6 0.8 pad_maximum_fusion
  1.4 25.0 %all-gather = bf16[8,16,1024]{2,1,0:T(8,128)(2,1)S(1)} all-gather(bf16[2,16,1024]{2,1,0:T(8,128)(2,1)S(1)} %pad_maximum_fusion), channel_id=2, replica_groups={{0,4,8,12},{1,5,9,13},{2,6,10,14},{3,7,11,15},{16,20,24,28},{17,21,25,2..., dimensions={0}, use_global_device_ids=true | all-gather | bytes 327680 | tf_op jit(solution)/shard_map/all_gather | solution.py:317
  26.4 3.4 %collective-permute-start.1 = (bf16[4,2,16,1024]{3,2,1,0:T(8,128)(2,1)S(1)}, bf16[4,2,16,1024]{3,2,1,0:T(8,128)(2,1)S(1)}, u32[]{:S(2)}, u32[]{:S(2)}) collective-permute-start(bf16[4,2,16,1024]{3,2,1,0:T(8,128)(2,1)S(1)} %bitcast.11), channel_id=1, source_target_pairs={{0,1},{1,2},{2,3},{3,4},{4,5},{5,6},{6,7},{7,8},{8,9},{9,10},{10,1... | collective-permute-start | bytes 786440 | tf_op jit(solution)/shard_map/ppermute | solution.py:310
  29.8 2.5 %collective-permute-start = (bf16[4,2,16,1024]{3,2,1,0:T(8,128)(2,1)S(1)}, bf16[4,2,16,1024]{3,2,1,0:T(8,128)(2,1)S(1)}, u32[]{:S(2)}, u32[]{:S(2)}) collective-permute-start(bf16[4,2,16,1024]{3,2,1,0:T(8,128)(2,1)S(1)} %bitcast.12), channel_id=1, source_target_pairs={{0,15},{1,0},{2,1},{3,2},{4,3},{5,4},{6,5},{7,6},{8,7},{9,8},{10,9... | collective-permute-start | bytes 786440 | tf_op jit(solution)/shard_map/ppermute | solution.py:310
  32.3 5.7 %collective-permute-start.3 = (bf16[2,2,16,1024]{3,2,1,0:T(8,128)(2,1)S(1)}, bf16[2,2,16,1024]{3,2,1,0:T(8,128)(2,1)S(1)}, u32[]{:S(2)}, u32[]{:S(2)}) collective-permute-start(bf16[2,2,16,1024]{3,2,1,0:T(8,128)(2,1)S(1)} %get-tuple-element.32), channel_id=1, source_target_pairs={{0,2},{1,3},{2,4},{3,5},{4,6},{5,7},{6,8},{7,9},{8,10},{9,11},{10,... | collective-permute-start | bytes 393224 | tf_op jit(solution)/shard_map/ppermute | solution.py:310
  38.0 1.9 %collective-permute-start.2 = (bf16[2,2,16,1024]{3,2,1,0:T(8,128)(2,1)S(1)}, bf16[2,2,16,1024]{3,2,1,0:T(8,128)(2,1)S(1)}, u32[]{:S(2)}, u32[]{:S(2)}) collective-permute-start(bf16[2,2,16,1024]{3,2,1,0:T(8,128)(2,1)S(1)} %get-tuple-element.33), channel_id=1, source_target_pairs={{0,14},{1,15},{2,0},{3,1},{4,2},{5,3},{6,4},{7,5},{8,6},{9,7},{10,... | collective-permute-start | bytes 393224 | tf_op jit(solution)/shard_map/ppermute | solution.py:310
  41.3 1.3 shard_map.111
  42.5 0.0 collective-permute-done.3.refs_4_
  42.6 5.7 %collective-permute-done.2.refs_3_ = bf16[2,2,16,1024]{3,2,1,0:T(8,128)(2,1)S(1)} collective-permute-done((bf16[2,2,16,1024]{3,2,1,0:T(8,128)(2,1)S(1)}, bf16[2,2,16,1024]{3,2,1,0:T(8,128)(2,1)S(1)}, u32[]{:S(2)}, u32[]{:S(2)}) %collective-permute-start.2) | collective-permute-done | bytes 131104 | tf_op jit(solution)/shard_map/ppermute | solution.py:310
  48.3 0.0 collective-permute-done.1.refs_2_
  48.3 0.0 collective-permute-done.refs_1_
  48.3 1.4 shard_map.112
  49.7 33.5 %all_to_all.15.parts_ref = bf16[16,37,16,128]{3,2,1,0:T(8,128)(2,1)S(1)} all-to-all(bf16[16,37,16,128]{3,2,1,0:T(8,128)(2,1)S(1)} %shard_map.112), channel_id=1, replica_groups=mesh['tok'=2,'row'=16,'col'=16] {'row'}, dimensions={0} | all-to-all | bytes 4849664 | tf_op jit(solution)/shard_map/all_to_all | solution.py:303
  83.2 2.1 %shard_map.113 = bf16[16,36,16,128]{3,2,1,0:T(8,128)(2,1)S(1)} custom-call(bf16[16,37,16,128]{3,2,1,0:T(8,128)(2,1)S(1)} %all_to_all.15.parts_ref), custom_call_target="tpu_custom_call" | custom-call | flops 4849664 | bytes 7274496 | tf_op jit(solution)/shard_map/pallas_call | solution.py:178
  85.3 28.3 %all_to_all.16.in_ref.refs_5_ = bf16[16,36,16,128]{3,2,1,0:T(8,128)(2,1)S(1)} all-to-all(bf16[16,36,16,128]{3,2,1,0:T(8,128)(2,1)S(1)} %shard_map.113), channel_id=1, replica_groups=mesh['tok'=2,'row'=16,'col'=16] {'row'}, dimensions={0} | all-to-all | bytes 4718592 | tf_op jit(solution)/shard_map/all_to_all | solution.py:303
  113.6 1.7 %shard_map.114 = (bf16[4,16,16,128]{3,2,1,0:T(8,128)(2,1)S(1)}, bf16[4,16,16,128]{3,2,1,0:T(8,128)(2,1)S(1)}, bf16[4,16,16,128]{3,2,1,0:T(8,128)(2,1)S(1)}, bf16...) custom-call(s32[8,128]{1,0:T(8,128)S(1)} %get-tuple-element.20.index_ref, ...), custom_call_target="tpu_custom_call" | custom-call | flops 301989888 | bytes 4718592 | tf_op jit(solution)/shard_map/pallas_call | solution.py:218
  115.3 1.9 %collective-permute-start.4 = (bf16[4,16,16,128]{3,2,1,0:T(8,128)(2,1)S(1)}, bf16[4,16,16,128]{3,2,1,0:T(8,128)(2,1)S(1)}, u32[]{:S(2)}, u32[]{:S(2)}) collective-permute-start(bf16[4,16,16,128]{3,2,1,0:T(8,128)(2,1)S(1)} %get-tuple-element.26), channel_id=1, source_target_pairs={{0,1},{1,2},{2,3},{3,4},{4,5},{5,6},{6,7},{7,8},{8,9},{9,10},{10,1... | collective-permute-start | bytes 786440 | tf_op jit(solution)/shard_map/ppermute | solution.py:310
  117.2 3.9 %collective-permute-start.5 = (bf16[4,16,16,128]{3,2,1,0:T(8,128)(2,1)S(1)}, bf16[4,16,16,128]{3,2,1,0:T(8,128)(2,1)S(1)}, u32[]{:S(2)}, u32[]{:S(2)}) collective-permute-start(bf16[4,16,16,128]{3,2,1,0:T(8,128)(2,1)S(1)} %get-tuple-element.27), channel_id=1, source_target_pairs={{0,15},{1,0},{2,1},{3,2},{4,3},{5,4},{6,5},{7,6},{8,7},{9,8},{10,9... | collective-permute-start | bytes 786440 | tf_op jit(solution)/shard_map/ppermute | solution.py:310
  121.1 3.2 %collective-permute-start.6 = (bf16[2,16,16,128]{3,2,1,0:T(8,128)(2,1)S(1)}, bf16[2,16,16,128]{3,2,1,0:T(8,128)(2,1)S(1)}, u32[]{:S(2)}, u32[]{:S(2)}) collective-permute-start(bf16[2,16,16,128]{3,2,1,0:T(8,128)(2,1)S(1)} %get-tuple-element.28), channel_id=1, source_target_pairs={{0,2},{1,3},{2,4},{3,5},{4,6},{5,7},{6,8},{7,9},{8,10},{9,11},{10,... | collective-permute-start | bytes 393224 | tf_op jit(solution)/shard_map/ppermute | solution.py:310
  124.3 3.6 %collective-permute-start.7 = (bf16[2,16,16,128]{3,2,1,0:T(8,128)(2,1)S(1)}, bf16[2,16,16,128]{3,2,1,0:T(8,128)(2,1)S(1)}, u32[]{:S(2)}, u32[]{:S(2)}) collective-permute-start(bf16[2,16,16,128]{3,2,1,0:T(8,128)(2,1)S(1)} %get-tuple-element.29), channel_id=1, source_target_pairs={{0,14},{1,15},{2,0},{3,1},{4,2},{5,3},{6,4},{7,5},{8,6},{9,7},{10,... | collective-permute-start | bytes 393224 | tf_op jit(solution)/shard_map/ppermute | solution.py:310
  127.9 2.4 %collective-permute-done.6.refs_3_ = bf16[2,16,16,128]{3,2,1,0:T(8,128)(2,1)S(1)} collective-permute-done((bf16[2,16,16,128]{3,2,1,0:T(8,128)(2,1)S(1)}, bf16[2,16,16,128]{3,2,1,0:T(8,128)(2,1)S(1)}, u32[]{:S(2)}, u32[]{:S(2)}) %collective-permute-start.6) | collective-permute-done | bytes 131104 | tf_op jit(solution)/shard_map/ppermute | solution.py:310
  130.3 4.2 %collective-permute-done.7.refs_4_ = bf16[2,16,16,128]{3,2,1,0:T(8,128)(2,1)S(1)} collective-permute-done((bf16[2,16,16,128]{3,2,1,0:T(8,128)(2,1)S(1)}, bf16[2,16,16,128]{3,2,1,0:T(8,128)(2,1)S(1)}, u32[]{:S(2)}, u32[]{:S(2)}) %collective-permute-start.7) | collective-permute-done | bytes 131104 | tf_op jit(solution)/shard_map/ppermute | solution.py:310
  134.5 0.0 collective-permute-done.4.refs_1_
  134.5 0.0 collective-permute-done.5.refs_2_
  134.5 0.1 shard_map.115
  134.6 1.5 shard_map.116.grads_ref
  136.2 1.9 %collective-permute-start.8 = (bf16[36,128,128]{2,1,0:T(8,128)(2,1)S(1)}, bf16[36,128,128]{2,1,0:T(8,128)(2,1)S(1)}, u32[]{:S(2)}, u32[]{:S(2)}) collective-permute-start(bf16[36,128,128]{2,1,0:T(8,128)(2,1)S(1)} %shard_map.116.grads_ref), channel_id=1, source_target_pairs={{0,256},{256,0},{1,257},{257,1},{2,258},{258,2},{3,259},{259,3},{4... | collective-permute-start | bytes 3538952 | tf_op jit(solution)/shard_map/ppermute | solution.py:334
  138.1 26.8 %all_to_all.17.parts_ref = bf16[4,16,16,128]{3,2,1,0:T(8,128)(2,1)S(1)} all-to-all(bf16[4,16,16,128]{3,2,1,0:T(8,128)(2,1)S(1)} %shard_map.115), channel_id=1, replica_groups={{0,4,8,12},{1,5,9,13},{2,6,10,14},{3,7,11,15},{16,20,24,28},{17,21,25,2..., dimensions={0} | all-to-all | bytes 524288 | tf_op jit(solution)/shard_map/all_to_all | solution.py:303
  164.9 0.0 collective-permute-done.8.others_ref
  165.0 1.3 shard_map.117
  (1 shorter events, 0.0 us)
Async XLA Ops:
  26.4 21.9 %collective-permute-start.1 = (bf16[4,2,16,1024]{3,2,1,0:T(8,128)(2,1)S(1)}, bf16[4,2,16,1024]{3,2,1,0:T(8,128)(2,1)S(1)}, u32[]{:S(2)}, u32[]{:S(2)}) collective-permute-start(bf16[4,2,16,1024]{3,2,1,0:T(8,128)(2,1)S(1)} %bitcast.11), channel_id=1, source_target_pairs={{0,1},{1,2},{2,3},{3,4},{4,5},{5,6},{6,7},{7,8},{8,9},{9,10},{10,1... | collective-permute-start | bytes 786440 | tf_op jit(solution)/shard_map/ppermute | solution.py:310
  29.8 18.5 %collective-permute-start = (bf16[4,2,16,1024]{3,2,1,0:T(8,128)(2,1)S(1)}, bf16[4,2,16,1024]{3,2,1,0:T(8,128)(2,1)S(1)}, u32[]{:S(2)}, u32[]{:S(2)}) collective-permute-start(bf16[4,2,16,1024]{3,2,1,0:T(8,128)(2,1)S(1)} %bitcast.12), channel_id=1, source_target_pairs={{0,15},{1,0},{2,1},{3,2},{4,3},{5,4},{6,5},{7,6},{8,7},{9,8},{10,9... | collective-permute-start | bytes 786440 | tf_op jit(solution)/shard_map/ppermute | solution.py:310
  32.3 10.3 %collective-permute-start.3 = (bf16[2,2,16,1024]{3,2,1,0:T(8,128)(2,1)S(1)}, bf16[2,2,16,1024]{3,2,1,0:T(8,128)(2,1)S(1)}, u32[]{:S(2)}, u32[]{:S(2)}) collective-permute-start(bf16[2,2,16,1024]{3,2,1,0:T(8,128)(2,1)S(1)} %get-tuple-element.32), channel_id=1, source_target_pairs={{0,2},{1,3},{2,4},{3,5},{4,6},{5,7},{6,8},{7,9},{8,10},{9,11},{10,... | collective-permute-start | bytes 393224 | tf_op jit(solution)/shard_map/ppermute | solution.py:310
  38.0 10.2 %collective-permute-start.2 = (bf16[2,2,16,1024]{3,2,1,0:T(8,128)(2,1)S(1)}, bf16[2,2,16,1024]{3,2,1,0:T(8,128)(2,1)S(1)}, u32[]{:S(2)}, u32[]{:S(2)}) collective-permute-start(bf16[2,2,16,1024]{3,2,1,0:T(8,128)(2,1)S(1)} %get-tuple-element.33), channel_id=1, source_target_pairs={{0,14},{1,15},{2,0},{3,1},{4,2},{5,3},{6,4},{7,5},{8,6},{9,7},{10,... | collective-permute-start | bytes 393224 | tf_op jit(solution)/shard_map/ppermute | solution.py:310
  115.3 19.2 %collective-permute-start.4 = (bf16[4,16,16,128]{3,2,1,0:T(8,128)(2,1)S(1)}, bf16[4,16,16,128]{3,2,1,0:T(8,128)(2,1)S(1)}, u32[]{:S(2)}, u32[]{:S(2)}) collective-permute-start(bf16[4,16,16,128]{3,2,1,0:T(8,128)(2,1)S(1)} %get-tuple-element.26), channel_id=1, source_target_pairs={{0,1},{1,2},{2,3},{3,4},{4,5},{5,6},{6,7},{7,8},{8,9},{9,10},{10,1... | collective-permute-start | bytes 786440 | tf_op jit(solution)/shard_map/ppermute | solution.py:310
  117.2 17.3 %collective-permute-start.5 = (bf16[4,16,16,128]{3,2,1,0:T(8,128)(2,1)S(1)}, bf16[4,16,16,128]{3,2,1,0:T(8,128)(2,1)S(1)}, u32[]{:S(2)}, u32[]{:S(2)}) collective-permute-start(bf16[4,16,16,128]{3,2,1,0:T(8,128)(2,1)S(1)} %get-tuple-element.27), channel_id=1, source_target_pairs={{0,15},{1,0},{2,1},{3,2},{4,3},{5,4},{6,5},{7,6},{8,7},{9,8},{10,9... | collective-permute-start | bytes 786440 | tf_op jit(solution)/shard_map/ppermute | solution.py:310
  121.1 9.2 %collective-permute-start.6 = (bf16[2,16,16,128]{3,2,1,0:T(8,128)(2,1)S(1)}, bf16[2,16,16,128]{3,2,1,0:T(8,128)(2,1)S(1)}, u32[]{:S(2)}, u32[]{:S(2)}) collective-permute-start(bf16[2,16,16,128]{3,2,1,0:T(8,128)(2,1)S(1)} %get-tuple-element.28), channel_id=1, source_target_pairs={{0,2},{1,3},{2,4},{3,5},{4,6},{5,7},{6,8},{7,9},{8,10},{9,11},{10,... | collective-permute-start | bytes 393224 | tf_op jit(solution)/shard_map/ppermute | solution.py:310
  124.3 10.2 %collective-permute-start.7 = (bf16[2,16,16,128]{3,2,1,0:T(8,128)(2,1)S(1)}, bf16[2,16,16,128]{3,2,1,0:T(8,128)(2,1)S(1)}, u32[]{:S(2)}, u32[]{:S(2)}) collective-permute-start(bf16[2,16,16,128]{3,2,1,0:T(8,128)(2,1)S(1)} %get-tuple-element.29), channel_id=1, source_target_pairs={{0,14},{1,15},{2,0},{3,1},{4,2},{5,3},{6,4},{7,5},{8,6},{9,7},{10,... | collective-permute-start | bytes 393224 | tf_op jit(solution)/shard_map/ppermute | solution.py:310
  136.2 28.8 %collective-permute-start.8 = (bf16[36,128,128]{2,1,0:T(8,128)(2,1)S(1)}, bf16[36,128,128]{2,1,0:T(8,128)(2,1)S(1)}, u32[]{:S(2)}, u32[]{:S(2)}) collective-permute-start(bf16[36,128,128]{2,1,0:T(8,128)(2,1)S(1)} %shard_map.116.grads_ref), channel_id=1, source_target_pairs={{0,256},{256,0},{1,257},{257,1},{2,258},{258,2},{3,259},{259,3},{4... | collective-permute-start | bytes 3538952 | tf_op jit(solution)/shard_map/ppermute | solution.py:334
